TPU v7x, 512 devices: a whole 4x8x8 slice. The times are simulated.
512 devices in a mesh: gx: 32 (over y, x), gy: 16 (over z, core).
Axes of the slice: x: 4, y: 8, z: 8, core: 2. Of those that a mesh axis runs over, the one named last changes fastest.
Arguments:
- right_sides: bfloat16 [32, 16, 512, 144], P('gx', 'gy'), may hold values from -6 to 6
- near_self: bfloat16 [32, 16, 512, 512], P('gx', 'gy'), may hold values from -0.09375 to 0.09375
- near_blocks: bfloat16 [32, 16, 4, 512, 512], P('gx', 'gy'), may hold values from -0.09375 to 0.09375
- near_list: int32 [32, 16, 4], P('gx', 'gy'), may hold values from -1 to 511, as said below
- basis: bfloat16 [32, 16, 512, 160], P('gx', 'gy'), may hold values from -0.25 to 0.25
- transfer_one: bfloat16 [32, 16, 160, 160], P('gx', 'gy'), may hold values from -0.25 to 0.25
- transfer_two: bfloat16 [32, 16, 40, 160], P('gx', 'gy'), may hold values from -0.3125 to 0.3125
- couple_one: bfloat16 [32, 16, 7, 160, 160], P('gx', 'gy'), may hold values from -0.09375 to 0.09375
- couple_two: bfloat16 [32, 16, 4, 160, 160], P('gx', 'gy'), may hold values from -0.09375 to 0.09375
- far_list_one: int32 [32, 16, 7], P('gx', 'gy'), may hold values from -1 to 127, as said below
- far_list_two: int32 [32, 16, 4], P('gx', 'gy'), may hold values from -1 to 63, as said below
Outputs:
- applied: bfloat16 [32, 16, 512, 144], P('gx', 'gy')
Inputs may be any that keep to these rules, and one draw needn't show every extreme that they name: `near_list`: the four entries of leaf (i, j) name, in some order, the leaves (i, j + 1), (i + 1, j - 1), (i + 1, j), (i + 1, j + 1), each once, or -1 where that leaf lies outside the grid of 32 x 16 leaves. `far_list_one`: each entry is -1 or the index of a first-level cluster (c, d) with c - a in -2 - a % 2 to 3 - a % 2 and d - b in -2 - b % 2 to 3 - b % 2 that is not adjacent to the leaf's own first-level cluster (a, b); over the four leaves of a first-level cluster every such cluster inside the grid is named exactly once. `far_list_two`: each entry is -1 or the index of a second-level cluster (c, d) with c - a in -2 - a % 2 to 3 - a % 2 and d - b in -2 - b % 2 to 3 - b % 2 that is not adjacent to the leaf's own second-level cluster (a, b); over the eight leaves of a second-level cluster every such cluster inside the grid is named exactly once.
All inputs are finite; a program needn't handle non-finite values.
Results may differ from a plain program's by a relative error of at most 0.012.
Values may be sent and summed in bfloat16 or wider, within the bound.
No kernel may reach another device: no remote copies, remote signals or barrier semaphores. Data moves between devices by JAX's collectives and lax.ppermute only.
A program may use at most 64 MiB of HBM per device.

v0:
```python
import jax
import jax.numpy as jnp
from jax import lax
from jax.sharding import PartitionSpec as P


def swapped(array, axis, apart):
    return lax.ppermute(array, axis, [(i, i ^ 1 << apart) for i in range(lax.axis_size(axis))])


def from_behind(value, axis, steps):
    count = lax.axis_size(axis)
    first, last = (max(0, -steps), min(count, count - steps))
    return lax.ppermute(value, axis, [(source, source + steps) for source in range(first, last)])


def inner(left, right):
    return lax.dot_general(
        left, right, (((0,), (0,)), ((), ())), preferred_element_type=jnp.float32
    )


def climb_sum(values, col_bits):
    bit_index = 0
    values = values + swapped(values.astype(jnp.bfloat16), "gx", bit_index).astype(values.dtype)
    for bit_index in range(col_bits):
        values = values + swapped(values.astype(jnp.bfloat16), "gy", bit_index).astype(values.dtype)
    return values


def descend_sum(values, col_bits):
    bit_index = 0
    values = values + swapped(values.astype(jnp.bfloat16), "gx", bit_index).astype(values.dtype)
    for bit_index in range(col_bits):
        values = values + swapped(values.astype(jnp.bfloat16), "gy", bit_index).astype(values.dtype)
    return values


def cluster_window(coefficients, row_stride, col_stride):
    blank = jnp.zeros_like(coefficients)
    tiles = []
    for down_off in range(-3, 4):
        if down_off == 0:
            strip = coefficients
        else:
            strip = from_behind(coefficients, "gx", -down_off * row_stride)
        for side_off in range(-3, 4):
            if abs(down_off) <= 1 and abs(side_off) <= 1:
                tiles.append(blank)
            else:
                tiles.append(from_behind(strip, "gy", -side_off * col_stride))
    return jnp.stack(tiles)


def coupled_sum(windowed, couplings, offset_code):
    is_valid = offset_code >= 0
    selected = jnp.take(windowed, jnp.maximum(offset_code, 0), axis=0)
    selected = jnp.where(is_valid[:, None, None], selected, jnp.zeros((), selected.dtype))
    return jnp.einsum("krs,ksn->rn", couplings, selected, preferred_element_type=jnp.float32)


def far_level(coefficients, couplings, sources, row_bits, col_bits, grid_row, grid_col, grid_width):
    row_stride = 2**row_bits
    col_stride = 2**col_bits
    cluster_cols = grid_width // col_stride
    is_valid = sources >= 0
    safe_source = jnp.maximum(sources, 0)
    offset_code = (safe_source // cluster_cols - grid_row // row_stride + 3) * 7 + (
        safe_source % cluster_cols - grid_col // col_stride + 3
    )
    offset_code = jnp.where(is_valid, offset_code, -1)
    windowed = cluster_window(coefficients, row_stride, col_stride)
    return coupled_sum(windowed, couplings, offset_code)


def shards(
    right_sides,
    near_self,
    near_blocks,
    near_list,
    basis,
    transfer_one,
    transfer_two,
    couple_one,
    couple_two,
    far_list_one,
    far_list_two,
):
    grid_row = lax.axis_index("gx")
    grid_col = lax.axis_index("gy")
    grid_height = lax.axis_size("gx")
    grid_width = lax.axis_size("gy")
    own_rhs = right_sides[0, 0]
    below = from_behind(own_rhs, "gx", -1)
    right_pair = from_behind(jnp.stack([own_rhs, below]), "gy", -1)
    below_left = from_behind(below, "gy", 1)
    neighbours = {(0, 1): right_pair[0], (1, -1): below_left, (1, 0): below, (1, 1): right_pair[1]}
    near_sum = jnp.dot(near_self[0, 0], own_rhs, preferred_element_type=jnp.float32)
    neighbor_ids = near_list[0, 0]
    stored_blocks = near_blocks[0, 0]
    slot_order = jnp.arange(4, dtype=jnp.int32)
    mirrored = []
    for down_off, side_off in ((0, 1), (1, -1), (1, 0), (1, 1)):
        target = (grid_row + down_off) * grid_width + grid_col + side_off
        inside = (
            (grid_row + down_off < grid_height)
            & (grid_col + side_off >= 0)
            & (grid_col + side_off < grid_width)
        )
        matches = (neighbor_ids == target) & inside
        chosen = jnp.sum(jnp.where(matches, slot_order, 0))
        coupling = lax.dynamic_index_in_dim(stored_blocks, chosen, 0, keepdims=False)
        near_sum = near_sum + jnp.dot(
            coupling, neighbours[down_off, side_off], preferred_element_type=jnp.float32
        )
        mirrored.append(inner(coupling, own_rhs).astype(jnp.bfloat16))
    downward = from_behind(jnp.stack(mirrored[1:]), "gx", 1)
    arrivals = (mirrored[0], downward[0], downward[1], downward[2])
    for arrival, side_off in zip(arrivals, (1, -1, 0, 1)):
        if side_off != 0:
            arrival = from_behind(arrival, "gy", side_off)
        near_sum = near_sum + arrival.astype(jnp.float32)
    leaf_coeff = inner(basis[0, 0], own_rhs).astype(jnp.bfloat16)
    coeff_one = climb_sum(inner(transfer_one[0, 0], leaf_coeff), 1).astype(jnp.bfloat16)
    quarter = transfer_two.shape[2]
    position_one = grid_row % 2 * 2 + grid_col % 2
    rows_one = lax.dynamic_slice_in_dim(coeff_one, position_one * quarter, quarter, 0)
    coeff_two = climb_sum(inner(transfer_two[0, 0], rows_one), 2).astype(jnp.bfloat16)
    far_two_terms = far_level(
        coeff_two, couple_two[0, 0], far_list_two[0, 0], 1, 2, grid_row, grid_col, grid_width
    )
    local_two = descend_sum(far_two_terms, 2).astype(jnp.bfloat16)
    down_piece = jnp.dot(transfer_two[0, 0], local_two, preferred_element_type=jnp.float32)
    padded = lax.dynamic_update_slice_in_dim(
        jnp.zeros(coeff_one.shape, jnp.float32), down_piece, position_one * quarter, 0
    )
    far_one_terms = far_level(
        coeff_one, couple_one[0, 0], far_list_one[0, 0], 1, 1, grid_row, grid_col, grid_width
    )
    local_one = descend_sum(far_one_terms + padded, 1).astype(jnp.bfloat16)
    leaf_local = jnp.dot(transfer_one[0, 0], local_one, preferred_element_type=jnp.float32).astype(
        jnp.bfloat16
    )
    far_field = jnp.dot(basis[0, 0], leaf_local, preferred_element_type=jnp.float32)
    return (near_sum + far_field).astype(jnp.bfloat16)[None, None]


def solution(mesh):
    in_specs = (
        P("gx", "gy", None, None),
        P("gx", "gy", None, None),
        P("gx", "gy", None, None, None),
        P("gx", "gy", None),
        P("gx", "gy", None, None),
        P("gx", "gy", None, None),
        P("gx", "gy", None, None),
        P("gx", "gy", None, None, None),
        P("gx", "gy", None, None, None),
        P("gx", "gy", None),
        P("gx", "gy", None),
    )
    out_specs = P("gx", "gy", None, None)
    return jax.shard_map(shards, mesh=mesh, in_specs=in_specs, out_specs=out_specs, check_vma=False)
```

profile of v0, /device:TPU:105, one launch (start us, length us, event | category | flops | bytes accessed | tf_op | source)
XLA Modules:
  0.0 618.5 jit_solution(15756925674363579717)
XLA Ops:
  4.8 4.5 collective-permute-start
  25.6 5.1 collective-permute-start.3
  36.6 6.3 %collective-permute-start.9 = (bf16[160,144]{0,1:T(8,128)(2,1)S(1)}, bf16[160,144]{0,1:T(8,128)(2,1)S(1)}, u32[]{:S(2)}, u32[]{:S(2)}) collective-permute-start(bf16[160,144]{0,1:T(8,128)(2,1)S(1)} %add_convert_fusion.3), channel_id=1, source_target_pairs={{0,96},{16,112},{32,128},{48,144},{64,160},{80,176},{96,192},{112,... | collective-permute-start | bytes 138248 | tf_op jit(solution)/shard_map/ppermute | solution.py:14
  50.3 7.9 %collective-permute-start.10 = (bf16[160,144]{0,1:T(8,128)(2,1)S(1)}, bf16[160,144]{0,1:T(8,128)(2,1)S(1)}, u32[]{:S(2)}, u32[]{:S(2)}) collective-permute-start(bf16[160,144]{0,1:T(8,128)(2,1)S(1)} %collective-permute-done.9), channel_id=1, source_target_pairs={{0,6},{1,7},{2,8},{3,9},{4,10},{5,11},{6,12},{7,13},{8,14},{9,15},... | collective-permute-start | bytes 138248 | tf_op jit(solution)/shard_map/ppermute | solution.py:14
  61.1 4.0 collective-permute-start.11
  67.2 3.9 collective-permute-start.12
  74.4 3.7 collective-permute-done.14
  79.4 7.4 %collective-permute-done.15 = bf16[160,144]{0,1:T(8,128)(2,1)S(1)} collective-permute-done((bf16[160,144]{0,1:T(8,128)(2,1)S(1)}, bf16[160,144]{0,1:T(8,128)(2,1)S(1)}, u32[]{:S(2)}, u32[]{:S(2)}) %collective-permute-start.15) | collective-permute-done | bytes 46112 | tf_op jit(solution)/shard_map/ppermute | solution.py:14
  88.1 7.5 %collective-permute-start.30 = (bf16[160,144]{0,1:T(8,128)(2,1)S(1)}, bf16[160,144]{0,1:T(8,128)(2,1)S(1)}, u32[]{:S(2)}, u32[]{:S(2)}) collective-permute-start(bf16[160,144]{0,1:T(8,128)(2,1)S(1)} %add_convert_fusion.3), channel_id=1, source_target_pairs={{0,6},{1,7},{2,8},{3,9},{4,10},{5,11},{6,12},{7,13},{8,14},{9,15},... | collective-permute-start | bytes 138248 | tf_op jit(solution)/shard_map/ppermute | solution.py:14
  95.6 5.7 collective-permute-start.18
  102.7 6.3 %collective-permute-start.19 = (bf16[160,144]{0,1:T(8,128)(2,1)S(1)}, bf16[160,144]{0,1:T(8,128)(2,1)S(1)}, u32[]{:S(2)}, u32[]{:S(2)}) collective-permute-start(bf16[160,144]{0,1:T(8,128)(2,1)S(1)} %collective-permute-done.17), channel_id=1, source_target_pairs={{0,4},{1,5},{2,6},{3,7},{4,8},{5,9},{6,10},{7,11},{8,12},{9,13},{1... | collective-permute-start | bytes 138248 | tf_op jit(solution)/shard_map/ppermute | solution.py:14
  110.5 3.9 collective-permute-start.20
  118.2 3.3 collective-permute-done.22
  122.8 7.6 %collective-permute-done.23 = bf16[160,144]{0,1:T(8,128)(2,1)S(1)} collective-permute-done((bf16[160,144]{0,1:T(8,128)(2,1)S(1)}, bf16[160,144]{0,1:T(8,128)(2,1)S(1)}, u32[]{:S(2)}, u32[]{:S(2)}) %collective-permute-start.23) | collective-permute-done | bytes 46112 | tf_op jit(solution)/shard_map/ppermute | solution.py:14
  131.7 6.9 %collective-permute-start.31 = (bf16[160,144]{0,1:T(8,128)(2,1)S(1)}, bf16[160,144]{0,1:T(8,128)(2,1)S(1)}, u32[]{:S(2)}, u32[]{:S(2)}) collective-permute-start(bf16[160,144]{0,1:T(8,128)(2,1)S(1)} %add_convert_fusion.3), channel_id=1, source_target_pairs={{0,4},{1,5},{2,6},{3,7},{4,8},{5,9},{6,10},{7,11},{8,12},{9,13},{1... | collective-permute-start | bytes 138248 | tf_op jit(solution)/shard_map/ppermute | solution.py:14
  138.9 6.0 collective-permute-start.26
  146.4 5.3 collective-permute-start.27
  154.4 5.1 collective-permute-done.28
  160.8 8.0 %collective-permute-done.29 = bf16[160,144]{0,1:T(8,128)(2,1)S(1)} collective-permute-done((bf16[160,144]{0,1:T(8,128)(2,1)S(1)}, bf16[160,144]{0,1:T(8,128)(2,1)S(1)}, u32[]{:S(2)}, u32[]{:S(2)}) %collective-permute-start.29) | collective-permute-done | bytes 46112 | tf_op jit(solution)/shard_map/ppermute | solution.py:14
  171.5 6.6 %collective-permute-start.34 = (bf16[160,144]{0,1:T(8,128)(2,1)S(1)}, bf16[160,144]{0,1:T(8,128)(2,1)S(1)}, u32[]{:S(2)}, u32[]{:S(2)}) collective-permute-start(bf16[160,144]{0,1:T(8,128)(2,1)S(1)} %add_convert_fusion.3), channel_id=1, source_target_pairs={{32,0},{48,16},{64,32},{80,48},{96,64},{112,80},{128,96},{144,112}... | collective-permute-start | bytes 138248 | tf_op jit(solution)/shard_map/ppermute | solution.py:14
  178.2 4.7 collective-permute-start.39
  183.6 5.4 collective-permute-start.47
  189.0 4.4 collective-permute-start.35
  194.8 6.2 %collective-permute-start.36 = (bf16[160,144]{0,1:T(8,128)(2,1)S(1)}, bf16[160,144]{0,1:T(8,128)(2,1)S(1)}, u32[]{:S(2)}, u32[]{:S(2)}) collective-permute-start(bf16[160,144]{0,1:T(8,128)(2,1)S(1)} %collective-permute-done.34), channel_id=1, source_target_pairs={{0,4},{1,5},{2,6},{3,7},{4,8},{5,9},{6,10},{7,11},{8,12},{9,13},{1... | collective-permute-start | bytes 138248 | tf_op jit(solution)/shard_map/ppermute | solution.py:14
  202.4 22.3 %collective-permute-start.56 = (bf16[160,144]{0,1:T(8,128)(2,1)S(1)}, bf16[160,144]{0,1:T(8,128)(2,1)S(1)}, u32[]{:S(2)}, u32[]{:S(2)}) collective-permute-start(bf16[160,144]{0,1:T(8,128)(2,1)S(1)} %fusion.52), channel_id=1, source_target_pairs={{0,1},{1,0},{2,3},{3,2},{4,5},{5,4},{6,7},{7,6},{8,9},{9,8},{10,11... | collective-permute-start | bytes 138248 | tf_op jit(solution)/shard_map/ppermute | solution.py:8
  228.2 4.9 collective-permute-done.37
  233.2 9.8 %collective-permute-start.40 = (bf16[160,144]{0,1:T(8,128)(2,1)S(1)}, bf16[160,144]{0,1:T(8,128)(2,1)S(1)}, u32[]{:S(2)}, u32[]{:S(2)}) collective-permute-start(bf16[160,144]{0,1:T(8,128)(2,1)S(1)} %collective-permute-done.39), channel_id=1, source_target_pairs={{0,6},{1,7},{2,8},{3,9},{4,10},{5,11},{6,12},{7,13},{8,14},{9,15},... | collective-permute-start | bytes 138248 | tf_op jit(solution)/shard_map/ppermute | solution.py:14
  256.3 7.8 %collective-permute-start.48 = (bf16[160,144]{0,1:T(8,128)(2,1)S(1)}, bf16[160,144]{0,1:T(8,128)(2,1)S(1)}, u32[]{:S(2)}, u32[]{:S(2)}) collective-permute-start(bf16[160,144]{0,1:T(8,128)(2,1)S(1)} %collective-permute-done.47), channel_id=1, source_target_pairs={{0,6},{1,7},{2,8},{3,9},{4,10},{5,11},{6,12},{7,13},{8,14},{9,15},... | collective-permute-start | bytes 138248 | tf_op jit(solution)/shard_map/ppermute | solution.py:14
  264.1 4.0 collective-permute-start.49
  268.1 3.4 collective-permute-start.50
  276.8 3.8 collective-permute-done.57
  282.0 5.4 collective-permute-start.58
  287.4 4.5 collective-permute-done.58
  291.8 9.4 %collective-permute-start.59 = (bf16[160,144]{0,1:T(8,128)(2,1)S(1)}, bf16[160,144]{0,1:T(8,128)(2,1)S(1)}, u32[]{:S(2)}, u32[]{:S(2)}) collective-permute-start(bf16[160,144]{0,1:T(8,128)(2,1)S(1)} %collective-permute-done.58), channel_id=1, source_target_pairs={{0,12},{1,13},{2,14},{3,15},{16,28},{17,29},{18,30},{19,31},{32,44... | collective-permute-start | bytes 138248 | tf_op jit(solution)/shard_map/ppermute | solution.py:14
  305.9 7.9 %collective-permute-start.61 = (bf16[160,144]{0,1:T(8,128)(2,1)S(1)}, bf16[160,144]{0,1:T(8,128)(2,1)S(1)}, u32[]{:S(2)}, u32[]{:S(2)}) collective-permute-start(bf16[160,144]{0,1:T(8,128)(2,1)S(1)} %collective-permute-done.58), channel_id=1, source_target_pairs={{0,4},{1,5},{2,6},{3,7},{4,8},{5,9},{6,10},{7,11},{8,12},{9,13},{1... | collective-permute-start | bytes 138248 | tf_op jit(solution)/shard_map/ppermute | solution.py:14
  317.8 4.5 collective-permute-done.63
  324.3 7.1 %collective-permute-done.64 = bf16[160,144]{0,1:T(8,128)(2,1)S(1)} collective-permute-done((bf16[160,144]{0,1:T(8,128)(2,1)S(1)}, bf16[160,144]{0,1:T(8,128)(2,1)S(1)}, u32[]{:S(2)}, u32[]{:S(2)}) %collective-permute-start.64) | collective-permute-done | bytes 46112 | tf_op jit(solution)/shard_map/ppermute | solution.py:14
  338.5 3.2 collective-permute-start.67
  345.8 8.5 %collective-permute-start.69 = (bf16[160,144]{0,1:T(8,128)(2,1)S(1)}, bf16[160,144]{0,1:T(8,128)(2,1)S(1)}, u32[]{:S(2)}, u32[]{:S(2)}) collective-permute-start(bf16[160,144]{0,1:T(8,128)(2,1)S(1)} %collective-permute-done.66), channel_id=1, source_target_pairs={{0,4},{1,5},{2,6},{3,7},{4,8},{5,9},{6,10},{7,11},{8,12},{9,13},{1... | collective-permute-start | bytes 138248 | tf_op jit(solution)/shard_map/ppermute | solution.py:14
  358.5 4.5 collective-permute-done.71
  364.9 7.1 %collective-permute-done.72 = bf16[160,144]{0,1:T(8,128)(2,1)S(1)} collective-permute-done((bf16[160,144]{0,1:T(8,128)(2,1)S(1)}, bf16[160,144]{0,1:T(8,128)(2,1)S(1)}, u32[]{:S(2)}, u32[]{:S(2)}) %collective-permute-start.72) | collective-permute-done | bytes 46112 | tf_op jit(solution)/shard_map/ppermute | solution.py:14
  374.0 6.1 collective-permute-start.79
  388.7 5.8 collective-permute-done.77
  396.4 6.7 %collective-permute-done.78 = bf16[160,144]{0,1:T(8,128)(2,1)S(1)} collective-permute-done((bf16[160,144]{0,1:T(8,128)(2,1)S(1)}, bf16[160,144]{0,1:T(8,128)(2,1)S(1)}, u32[]{:S(2)}, u32[]{:S(2)}) %collective-permute-start.78) | collective-permute-done | bytes 46112 | tf_op jit(solution)/shard_map/ppermute | solution.py:14
  410.2 3.8 collective-permute-done.81
  414.0 5.3 collective-permute-start.83
  421.9 4.0 collective-permute-start.84
  433.7 5.9 collective-permute-done.86
  441.5 5.3 collective-permute-start.96
  446.9 6.5 %collective-permute-start.89 = (bf16[160,144]{0,1:T(8,128)(2,1)S(1)}, bf16[160,144]{0,1:T(8,128)(2,1)S(1)}, u32[]{:S(2)}, u32[]{:S(2)}) collective-permute-start(bf16[160,144]{0,1:T(8,128)(2,1)S(1)} %collective-permute-done.88), channel_id=1, source_target_pairs={{0,12},{1,13},{2,14},{3,15},{16,28},{17,29},{18,30},{19,31},{32,44... | collective-permute-start | bytes 138248 | tf_op jit(solution)/shard_map/ppermute | solution.py:14
  457.5 8.5 %collective-permute-start.91 = (bf16[160,144]{0,1:T(8,128)(2,1)S(1)}, bf16[160,144]{0,1:T(8,128)(2,1)S(1)}, u32[]{:S(2)}, u32[]{:S(2)}) collective-permute-start(bf16[160,144]{0,1:T(8,128)(2,1)S(1)} %collective-permute-done.88), channel_id=1, source_target_pairs={{0,4},{1,5},{2,6},{3,7},{4,8},{5,9},{6,10},{7,11},{8,12},{9,13},{1... | collective-permute-start | bytes 138248 | tf_op jit(solution)/shard_map/ppermute | solution.py:14
  469.9 4.4 collective-permute-done.93
  476.3 7.1 %collective-permute-done.94 = bf16[160,144]{0,1:T(8,128)(2,1)S(1)} collective-permute-done((bf16[160,144]{0,1:T(8,128)(2,1)S(1)}, bf16[160,144]{0,1:T(8,128)(2,1)S(1)}, u32[]{:S(2)}, u32[]{:S(2)}) %collective-permute-start.94) | collective-permute-done | bytes 46112 | tf_op jit(solution)/shard_map/ppermute | solution.py:14
  485.3 36.4 %collective-permute-start.1 = (bf16[2,512,144]{1,2,0:T(8,128)(2,1)}, bf16[2,512,144]{1,2,0:T(8,128)(2,1)}, u32[]{:S(2)}, u32[]{:S(2)}) collective-permute-start(bf16[2,512,144]{1,2,0:T(8,128)(2,1)} %pad_maximum_fusion.1), channel_id=1, source_target_pairs={{1,0},{2,1},{3,2},{4,3},{5,4},{6,5},{7,6},{8,7},{9,8},{10,9},{11,1... | collective-permute-start | bytes 884744 | tf_op jit(solution)/shard_map/ppermute | solution.py:14
  521.7 7.1 %collective-permute-start.97 = (bf16[160,144]{0,1:T(8,128)(2,1)S(1)}, bf16[160,144]{0,1:T(8,128)(2,1)S(1)}, u32[]{:S(2)}, u32[]{:S(2)}) collective-permute-start(bf16[160,144]{0,1:T(8,128)(2,1)S(1)} %collective-permute-done.96), channel_id=1, source_target_pairs={{0,12},{1,13},{2,14},{3,15},{16,28},{17,29},{18,30},{19,31},{32,44... | collective-permute-start | bytes 138248 | tf_op jit(solution)/shard_map/ppermute | solution.py:14
  533.7 8.3 %collective-permute-start.99 = (bf16[160,144]{0,1:T(8,128)(2,1)S(1)}, bf16[160,144]{0,1:T(8,128)(2,1)S(1)}, u32[]{:S(2)}, u32[]{:S(2)}) collective-permute-start(bf16[160,144]{0,1:T(8,128)(2,1)S(1)} %collective-permute-done.96), channel_id=1, source_target_pairs={{0,4},{1,5},{2,6},{3,7},{4,8},{5,9},{6,10},{7,11},{8,12},{9,13},{1... | collective-permute-start | bytes 138248 | tf_op jit(solution)/shard_map/ppermute | solution.py:14
  546.0 4.4 collective-permute-done.101
  552.3 7.1 %collective-permute-done.102 = bf16[160,144]{0,1:T(8,128)(2,1)S(1)} collective-permute-done((bf16[160,144]{0,1:T(8,128)(2,1)S(1)}, bf16[160,144]{0,1:T(8,128)(2,1)S(1)}, u32[]{:S(2)}, u32[]{:S(2)}) %collective-permute-start.102) | collective-permute-done | bytes 46112 | tf_op jit(solution)/shard_map/ppermute | solution.py:14
  561.3 5.3 collective-permute-done.103
  566.6 5.9 collective-permute-start.2
  577.0 4.8 collective-permute-start.104
  582.5 3.5 gather_fusion
  589.6 7.3 %collective-permute-start.106 = (bf16[160,144]{0,1:T(8,128)(2,1)S(1)}, bf16[160,144]{0,1:T(8,128)(2,1)S(1)}, u32[]{:S(2)}, u32[]{:S(2)}) collective-permute-start(bf16[160,144]{0,1:T(8,128)(2,1)S(1)} %fusion.59), channel_id=1, source_target_pairs={{0,2},{1,3},{2,0},{3,1},{4,6},{5,7},{6,4},{7,5},{8,10},{9,11},{10,... | collective-permute-start | bytes 138248 | tf_op jit(solution)/shard_map/ppermute | solution.py:8
  609.2 4.4 collective-permute-start.108
  (303 shorter events, 191.4 us)
Async XLA Ops:
  1.7 29.6 %collective-permute-start.7 = (bf16[160,144]{0,1:T(8,128)(2,1)S(1)}, bf16[160,144]{0,1:T(8,128)(2,1)S(1)}, u32[]{:S(2)}, u32[]{:S(2)}) collective-permute-start(bf16[160,144]{0,1:T(8,128)(2,1)S(1)} %get-tuple-element.15), channel_id=1, source_target_pairs={{0,16},{16,0},{32,48},{48,32},{64,80},{80,64},{96,112},{112,96},{1... | collective-permute-start | bytes 138248 | tf_op jit(solution)/shard_map/ppermute | solution.py:8
  4.8 45.5 %collective-permute-start = (bf16[512,144]{0,1:T(8,128)(2,1)}, bf16[512,144]{0,1:T(8,128)(2,1)}, u32[]{:S(2)}, u32[]{:S(2)}) collective-permute-start(bf16[512,144]{0,1:T(8,128)(2,1)} %bitcast.376), channel_id=1, source_target_pairs={{16,0},{32,16},{48,32},{64,48},{80,64},{96,80},{112,96},{128,112},... | collective-permute-start | bytes 442376 | tf_op jit(solution)/shard_map/ppermute | solution.py:14
  20.7 576.2 %collective-permute-start.4 = (bf16[3,512,144]{1,2,0:T(8,128)(2,1)}, bf16[3,512,144]{1,2,0:T(8,128)(2,1)}, u32[]{:S(2)}, u32[]{:S(2)}) collective-permute-start(bf16[3,512,144]{1,2,0:T(8,128)(2,1)} %pad_maximum_fusion), channel_id=1, source_target_pairs={{0,16},{16,32},{32,48},{48,64},{64,80},{80,96},{96,112},{112,128},... | collective-permute-start | bytes 1327112 | tf_op jit(solution)/shard_map/ppermute | solution.py:14
  25.6 590.6 %collective-permute-start.3 = (bf16[512,144]{0,1:T(8,128)(2,1)}, bf16[512,144]{0,1:T(8,128)(2,1)}, u32[]{:S(2)}, u32[]{:S(2)}) collective-permute-start(bf16[512,144]{0,1:T(8,128)(2,1)} %convolution_convert_fusion.3), channel_id=1, source_target_pairs={{0,1},{1,2},{2,3},{3,4},{4,5},{5,6},{6,7},{7,8},{8,9},{9,10},{10,1... | collective-permute-start | bytes 442376 | tf_op jit(solution)/shard_map/ppermute | solution.py:14
  34.7 8.2 %collective-permute-start.55 = (bf16[160,144]{0,1:T(8,128)(2,1)S(1)}, bf16[160,144]{0,1:T(8,128)(2,1)S(1)}, u32[]{:S(2)}, u32[]{:S(2)}) collective-permute-start(bf16[160,144]{0,1:T(8,128)(2,1)S(1)} %get-tuple-element.17), channel_id=1, source_target_pairs={{0,16},{16,0},{32,48},{48,32},{64,80},{80,64},{96,112},{112,96},{1... | collective-permute-start | bytes 138248 | tf_op jit(solution)/shard_map/ppermute | solution.py:8
  36.6 10.9 %collective-permute-start.9 = (bf16[160,144]{0,1:T(8,128)(2,1)S(1)}, bf16[160,144]{0,1:T(8,128)(2,1)S(1)}, u32[]{:S(2)}, u32[]{:S(2)}) collective-permute-start(bf16[160,144]{0,1:T(8,128)(2,1)S(1)} %add_convert_fusion.3), channel_id=1, source_target_pairs={{0,96},{16,112},{32,128},{48,144},{64,160},{80,176},{96,192},{112,... | collective-permute-start | bytes 138248 | tf_op jit(solution)/shard_map/ppermute | solution.py:14
  42.9 45.2 %collective-permute-start.17 = (bf16[160,144]{0,1:T(8,128)(2,1)S(1)}, bf16[160,144]{0,1:T(8,128)(2,1)S(1)}, u32[]{:S(2)}, u32[]{:S(2)}) collective-permute-start(bf16[160,144]{0,1:T(8,128)(2,1)S(1)} %add_convert_fusion.3), channel_id=1, source_target_pairs={{0,64},{16,80},{32,96},{48,112},{64,128},{80,144},{96,160},{112,17... | collective-permute-start | bytes 138248 | tf_op jit(solution)/shard_map/ppermute | solution.py:14
  47.6 84.1 %collective-permute-start.25 = (bf16[160,144]{0,1:T(8,128)(2,1)S(1)}, bf16[160,144]{0,1:T(8,128)(2,1)S(1)}, u32[]{:S(2)}, u32[]{:S(2)}) collective-permute-start(bf16[160,144]{0,1:T(8,128)(2,1)S(1)} %add_convert_fusion.3), channel_id=1, source_target_pairs={{0,32},{16,48},{32,64},{48,80},{64,96},{80,112},{96,128},{112,144}... | collective-permute-start | bytes 138248 | tf_op jit(solution)/shard_map/ppermute | solution.py:14
  50.3 10.8 %collective-permute-start.10 = (bf16[160,144]{0,1:T(8,128)(2,1)S(1)}, bf16[160,144]{0,1:T(8,128)(2,1)S(1)}, u32[]{:S(2)}, u32[]{:S(2)}) collective-permute-start(bf16[160,144]{0,1:T(8,128)(2,1)S(1)} %collective-permute-done.9), channel_id=1, source_target_pairs={{0,6},{1,7},{2,8},{3,9},{4,10},{5,11},{6,12},{7,13},{8,14},{9,15},... | collective-permute-start | bytes 138248 | tf_op jit(solution)/shard_map/ppermute | solution.py:14
  78.1 8.7 %collective-permute-start.15 = (bf16[160,144]{0,1:T(8,128)(2,1)S(1)}, bf16[160,144]{0,1:T(8,128)(2,1)S(1)}, u32[]{:S(2)}, u32[]{:S(2)}) collective-permute-start(bf16[160,144]{0,1:T(8,128)(2,1)S(1)} %collective-permute-done.9), channel_id=1, source_target_pairs={{4,0},{5,1},{6,2},{7,3},{8,4},{9,5},{10,6},{11,7},{12,8},{13,9},{1... | collective-permute-start | bytes 138248 | tf_op jit(solution)/shard_map/ppermute | solution.py:14
  86.8 8.8 %collective-permute-start.16 = (bf16[160,144]{0,1:T(8,128)(2,1)S(1)}, bf16[160,144]{0,1:T(8,128)(2,1)S(1)}, u32[]{:S(2)}, u32[]{:S(2)}) collective-permute-start(bf16[160,144]{0,1:T(8,128)(2,1)S(1)} %collective-permute-done.9), channel_id=1, source_target_pairs={{6,0},{7,1},{8,2},{9,3},{10,4},{11,5},{12,6},{13,7},{14,8},{15,9},... | collective-permute-start | bytes 138248 | tf_op jit(solution)/shard_map/ppermute | solution.py:14
  88.1 82.1 %collective-permute-start.30 = (bf16[160,144]{0,1:T(8,128)(2,1)S(1)}, bf16[160,144]{0,1:T(8,128)(2,1)S(1)}, u32[]{:S(2)}, u32[]{:S(2)}) collective-permute-start(bf16[160,144]{0,1:T(8,128)(2,1)S(1)} %add_convert_fusion.3), channel_id=1, source_target_pairs={{0,6},{1,7},{2,8},{3,9},{4,10},{5,11},{6,12},{7,13},{8,14},{9,15},... | collective-permute-start | bytes 138248 | tf_op jit(solution)/shard_map/ppermute | solution.py:14
  102.7 7.8 %collective-permute-start.19 = (bf16[160,144]{0,1:T(8,128)(2,1)S(1)}, bf16[160,144]{0,1:T(8,128)(2,1)S(1)}, u32[]{:S(2)}, u32[]{:S(2)}) collective-permute-start(bf16[160,144]{0,1:T(8,128)(2,1)S(1)} %collective-permute-done.17), channel_id=1, source_target_pairs={{0,4},{1,5},{2,6},{3,7},{4,8},{5,9},{6,10},{7,11},{8,12},{9,13},{1... | collective-permute-start | bytes 138248 | tf_op jit(solution)/shard_map/ppermute | solution.py:14
  121.5 8.9 %collective-permute-start.23 = (bf16[160,144]{0,1:T(8,128)(2,1)S(1)}, bf16[160,144]{0,1:T(8,128)(2,1)S(1)}, u32[]{:S(2)}, u32[]{:S(2)}) collective-permute-start(bf16[160,144]{0,1:T(8,128)(2,1)S(1)} %collective-permute-done.17), channel_id=1, source_target_pairs={{4,0},{5,1},{6,2},{7,3},{8,4},{9,5},{10,6},{11,7},{12,8},{13,9},{1... | collective-permute-start | bytes 138248 | tf_op jit(solution)/shard_map/ppermute | solution.py:14
  130.4 8.6 %collective-permute-start.24 = (bf16[160,144]{0,1:T(8,128)(2,1)S(1)}, bf16[160,144]{0,1:T(8,128)(2,1)S(1)}, u32[]{:S(2)}, u32[]{:S(2)}) collective-permute-start(bf16[160,144]{0,1:T(8,128)(2,1)S(1)} %collective-permute-done.17), channel_id=1, source_target_pairs={{6,0},{7,1},{8,2},{9,3},{10,4},{11,5},{12,6},{13,7},{14,8},{15,9},... | collective-permute-start | bytes 138248 | tf_op jit(solution)/shard_map/ppermute | solution.py:14
  131.7 39.8 %collective-permute-start.31 = (bf16[160,144]{0,1:T(8,128)(2,1)S(1)}, bf16[160,144]{0,1:T(8,128)(2,1)S(1)}, u32[]{:S(2)}, u32[]{:S(2)}) collective-permute-start(bf16[160,144]{0,1:T(8,128)(2,1)S(1)} %add_convert_fusion.3), channel_id=1, source_target_pairs={{0,4},{1,5},{2,6},{3,7},{4,8},{5,9},{6,10},{7,11},{8,12},{9,13},{1... | collective-permute-start | bytes 138248 | tf_op jit(solution)/shard_map/ppermute | solution.py:14
  159.5 9.3 %collective-permute-start.29 = (bf16[160,144]{0,1:T(8,128)(2,1)S(1)}, bf16[160,144]{0,1:T(8,128)(2,1)S(1)}, u32[]{:S(2)}, u32[]{:S(2)}) collective-permute-start(bf16[160,144]{0,1:T(8,128)(2,1)S(1)} %collective-permute-done.25), channel_id=1, source_target_pairs={{6,0},{7,1},{8,2},{9,3},{10,4},{11,5},{12,6},{13,7},{14,8},{15,9},... | collective-permute-start | bytes 138248 | tf_op jit(solution)/shard_map/ppermute | solution.py:14
  168.9 9.3 %collective-permute-start.32 = (bf16[160,144]{0,1:T(8,128)(2,1)S(1)}, bf16[160,144]{0,1:T(8,128)(2,1)S(1)}, u32[]{:S(2)}, u32[]{:S(2)}) collective-permute-start(bf16[160,144]{0,1:T(8,128)(2,1)S(1)} %add_convert_fusion.3), channel_id=1, source_target_pairs={{4,0},{5,1},{6,2},{7,3},{8,4},{9,5},{10,6},{11,7},{12,8},{13,9},{1... | collective-permute-start | bytes 138248 | tf_op jit(solution)/shard_map/ppermute | solution.py:14
  170.2 13.4 %collective-permute-start.33 = (bf16[160,144]{0,1:T(8,128)(2,1)S(1)}, bf16[160,144]{0,1:T(8,128)(2,1)S(1)}, u32[]{:S(2)}, u32[]{:S(2)}) collective-permute-start(bf16[160,144]{0,1:T(8,128)(2,1)S(1)} %add_convert_fusion.3), channel_id=1, source_target_pairs={{6,0},{7,1},{8,2},{9,3},{10,4},{11,5},{12,6},{13,7},{14,8},{15,9},... | collective-permute-start | bytes 138248 | tf_op jit(solution)/shard_map/ppermute | solution.py:14
  171.5 17.5 %collective-permute-start.34 = (bf16[160,144]{0,1:T(8,128)(2,1)S(1)}, bf16[160,144]{0,1:T(8,128)(2,1)S(1)}, u32[]{:S(2)}, u32[]{:S(2)}) collective-permute-start(bf16[160,144]{0,1:T(8,128)(2,1)S(1)} %add_convert_fusion.3), channel_id=1, source_target_pairs={{32,0},{48,16},{64,32},{80,48},{96,64},{112,80},{128,96},{144,112}... | collective-permute-start | bytes 138248 | tf_op jit(solution)/shard_map/ppermute | solution.py:14
  178.2 48.8 %collective-permute-start.39 = (bf16[160,144]{0,1:T(8,128)(2,1)S(1)}, bf16[160,144]{0,1:T(8,128)(2,1)S(1)}, u32[]{:S(2)}, u32[]{:S(2)}) collective-permute-start(bf16[160,144]{0,1:T(8,128)(2,1)S(1)} %add_convert_fusion.3), channel_id=1, source_target_pairs={{64,0},{80,16},{96,32},{112,48},{128,64},{144,80},{160,96},{176,11... | collective-permute-start | bytes 138248 | tf_op jit(solution)/shard_map/ppermute | solution.py:14
  183.6 70.9 %collective-permute-start.47 = (bf16[160,144]{0,1:T(8,128)(2,1)S(1)}, bf16[160,144]{0,1:T(8,128)(2,1)S(1)}, u32[]{:S(2)}, u32[]{:S(2)}) collective-permute-start(bf16[160,144]{0,1:T(8,128)(2,1)S(1)} %add_convert_fusion.3), channel_id=1, source_target_pairs={{96,0},{112,16},{128,32},{144,48},{160,64},{176,80},{192,96},{208,... | collective-permute-start | bytes 138248 | tf_op jit(solution)/shard_map/ppermute | solution.py:14
  194.8 7.6 %collective-permute-start.36 = (bf16[160,144]{0,1:T(8,128)(2,1)S(1)}, bf16[160,144]{0,1:T(8,128)(2,1)S(1)}, u32[]{:S(2)}, u32[]{:S(2)}) collective-permute-start(bf16[160,144]{0,1:T(8,128)(2,1)S(1)} %collective-permute-done.34), channel_id=1, source_target_pairs={{0,4},{1,5},{2,6},{3,7},{4,8},{5,9},{6,10},{7,11},{8,12},{9,13},{1... | collective-permute-start | bytes 138248 | tf_op jit(solution)/shard_map/ppermute | solution.py:14
  202.4 23.2 %collective-permute-start.56 = (bf16[160,144]{0,1:T(8,128)(2,1)S(1)}, bf16[160,144]{0,1:T(8,128)(2,1)S(1)}, u32[]{:S(2)}, u32[]{:S(2)}) collective-permute-start(bf16[160,144]{0,1:T(8,128)(2,1)S(1)} %fusion.52), channel_id=1, source_target_pairs={{0,1},{1,0},{2,3},{3,2},{4,5},{5,4},{6,7},{7,6},{8,9},{9,8},{10,11... | collective-permute-start | bytes 138248 | tf_op jit(solution)/shard_map/ppermute | solution.py:8
  225.6 7.6 %collective-permute-start.37 = (bf16[160,144]{0,1:T(8,128)(2,1)S(1)}, bf16[160,144]{0,1:T(8,128)(2,1)S(1)}, u32[]{:S(2)}, u32[]{:S(2)}) collective-permute-start(bf16[160,144]{0,1:T(8,128)(2,1)S(1)} %collective-permute-done.34), channel_id=1, source_target_pairs={{4,0},{5,1},{6,2},{7,3},{8,4},{9,5},{10,6},{11,7},{12,8},{13,9},{1... | collective-permute-start | bytes 138248 | tf_op jit(solution)/shard_map/ppermute | solution.py:14
  226.9 16.0 %collective-permute-start.38 = (bf16[160,144]{0,1:T(8,128)(2,1)S(1)}, bf16[160,144]{0,1:T(8,128)(2,1)S(1)}, u32[]{:S(2)}, u32[]{:S(2)}) collective-permute-start(bf16[160,144]{0,1:T(8,128)(2,1)S(1)} %collective-permute-done.34), channel_id=1, source_target_pairs={{6,0},{7,1},{8,2},{9,3},{10,4},{11,5},{12,6},{13,7},{14,8},{15,9},... | collective-permute-start | bytes 138248 | tf_op jit(solution)/shard_map/ppermute | solution.py:14
  233.2 12.9 %collective-permute-start.40 = (bf16[160,144]{0,1:T(8,128)(2,1)S(1)}, bf16[160,144]{0,1:T(8,128)(2,1)S(1)}, u32[]{:S(2)}, u32[]{:S(2)}) collective-permute-start(bf16[160,144]{0,1:T(8,128)(2,1)S(1)} %collective-permute-done.39), channel_id=1, source_target_pairs={{0,6},{1,7},{2,8},{3,9},{4,10},{5,11},{6,12},{7,13},{8,14},{9,15},... | collective-permute-start | bytes 138248 | tf_op jit(solution)/shard_map/ppermute | solution.py:14
  253.2 10.9 %collective-permute-start.45 = (bf16[160,144]{0,1:T(8,128)(2,1)S(1)}, bf16[160,144]{0,1:T(8,128)(2,1)S(1)}, u32[]{:S(2)}, u32[]{:S(2)}) collective-permute-start(bf16[160,144]{0,1:T(8,128)(2,1)S(1)} %collective-permute-done.39), channel_id=1, source_target_pairs={{4,0},{5,1},{6,2},{7,3},{8,4},{9,5},{10,6},{11,7},{12,8},{13,9},{1... | collective-permute-start | bytes 138248 | tf_op jit(solution)/shard_map/ppermute | solution.py:14
  254.5 13.6 %collective-permute-start.46 = (bf16[160,144]{0,1:T(8,128)(2,1)S(1)}, bf16[160,144]{0,1:T(8,128)(2,1)S(1)}, u32[]{:S(2)}, u32[]{:S(2)}) collective-permute-start(bf16[160,144]{0,1:T(8,128)(2,1)S(1)} %collective-permute-done.39), channel_id=1, source_target_pairs={{6,0},{7,1},{8,2},{9,3},{10,4},{11,5},{12,6},{13,7},{14,8},{15,9},... | collective-permute-start | bytes 138248 | tf_op jit(solution)/shard_map/ppermute | solution.py:14
  256.3 15.2 %collective-permute-start.48 = (bf16[160,144]{0,1:T(8,128)(2,1)S(1)}, bf16[160,144]{0,1:T(8,128)(2,1)S(1)}, u32[]{:S(2)}, u32[]{:S(2)}) collective-permute-start(bf16[160,144]{0,1:T(8,128)(2,1)S(1)} %collective-permute-done.47), channel_id=1, source_target_pairs={{0,6},{1,7},{2,8},{3,9},{4,10},{5,11},{6,12},{7,13},{8,14},{9,15},... | collective-permute-start | bytes 138248 | tf_op jit(solution)/shard_map/ppermute | solution.py:14
  271.6 10.4 %collective-permute-start.52 = (bf16[160,144]{0,1:T(8,128)(2,1)S(1)}, bf16[160,144]{0,1:T(8,128)(2,1)S(1)}, u32[]{:S(2)}, u32[]{:S(2)}) collective-permute-start(bf16[160,144]{0,1:T(8,128)(2,1)S(1)} %collective-permute-done.47), channel_id=1, source_target_pairs={{2,0},{3,1},{4,2},{5,3},{6,4},{7,5},{8,6},{9,7},{10,8},{11,9},{12,... | collective-permute-start | bytes 138248 | tf_op jit(solution)/shard_map/ppermute | solution.py:14
  273.5 27.7 %collective-permute-start.53 = (bf16[160,144]{0,1:T(8,128)(2,1)S(1)}, bf16[160,144]{0,1:T(8,128)(2,1)S(1)}, u32[]{:S(2)}, u32[]{:S(2)}) collective-permute-start(bf16[160,144]{0,1:T(8,128)(2,1)S(1)} %collective-permute-done.47), channel_id=1, source_target_pairs={{4,0},{5,1},{6,2},{7,3},{8,4},{9,5},{10,6},{11,7},{12,8},{13,9},{1... | collective-permute-start | bytes 138248 | tf_op jit(solution)/shard_map/ppermute | solution.py:14
  280.6 296.4 %collective-permute-start.54 = (bf16[160,144]{0,1:T(8,128)(2,1)S(1)}, bf16[160,144]{0,1:T(8,128)(2,1)S(1)}, u32[]{:S(2)}, u32[]{:S(2)}) collective-permute-start(bf16[160,144]{0,1:T(8,128)(2,1)S(1)} %collective-permute-done.47), channel_id=1, source_target_pairs={{6,0},{7,1},{8,2},{9,3},{10,4},{11,5},{12,6},{13,7},{14,8},{15,9},... | collective-permute-start | bytes 138248 | tf_op jit(solution)/shard_map/ppermute | solution.py:14
  282.0 9.8 %collective-permute-start.58 = (bf16[160,144]{0,1:T(8,128)(2,1)S(1)}, bf16[160,144]{0,1:T(8,128)(2,1)S(1)}, u32[]{:S(2)}, u32[]{:S(2)}) collective-permute-start(bf16[160,144]{0,1:T(8,128)(2,1)S(1)} %add_convert_fusion.2), channel_id=1, source_target_pairs={{0,96},{16,112},{32,128},{48,144},{64,160},{80,176},{96,192},{112,... | collective-permute-start | bytes 138248 | tf_op jit(solution)/shard_map/ppermute | solution.py:14
  291.8 11.4 %collective-permute-start.59 = (bf16[160,144]{0,1:T(8,128)(2,1)S(1)}, bf16[160,144]{0,1:T(8,128)(2,1)S(1)}, u32[]{:S(2)}, u32[]{:S(2)}) collective-permute-start(bf16[160,144]{0,1:T(8,128)(2,1)S(1)} %collective-permute-done.58), channel_id=1, source_target_pairs={{0,12},{1,13},{2,14},{3,15},{16,28},{17,29},{18,30},{19,31},{32,44... | collective-permute-start | bytes 138248 | tf_op jit(solution)/shard_map/ppermute | solution.py:14
  301.3 32.0 %collective-permute-start.66 = (bf16[160,144]{0,1:T(8,128)(2,1)S(1)}, bf16[160,144]{0,1:T(8,128)(2,1)S(1)}, u32[]{:S(2)}, u32[]{:S(2)}) collective-permute-start(bf16[160,144]{0,1:T(8,128)(2,1)S(1)} %add_convert_fusion.2), channel_id=1, source_target_pairs={{0,64},{16,80},{32,96},{48,112},{64,128},{80,144},{96,160},{112,17... | collective-permute-start | bytes 138248 | tf_op jit(solution)/shard_map/ppermute | solution.py:14
  305.9 9.4 %collective-permute-start.61 = (bf16[160,144]{0,1:T(8,128)(2,1)S(1)}, bf16[160,144]{0,1:T(8,128)(2,1)S(1)}, u32[]{:S(2)}, u32[]{:S(2)}) collective-permute-start(bf16[160,144]{0,1:T(8,128)(2,1)S(1)} %collective-permute-done.58), channel_id=1, source_target_pairs={{0,4},{1,5},{2,6},{3,7},{4,8},{5,9},{6,10},{7,11},{8,12},{9,13},{1... | collective-permute-start | bytes 138248 | tf_op jit(solution)/shard_map/ppermute | solution.py:14
  322.3 9.0 %collective-permute-start.64 = (bf16[160,144]{0,1:T(8,128)(2,1)S(1)}, bf16[160,144]{0,1:T(8,128)(2,1)S(1)}, u32[]{:S(2)}, u32[]{:S(2)}) collective-permute-start(bf16[160,144]{0,1:T(8,128)(2,1)S(1)} %collective-permute-done.58), channel_id=1, source_target_pairs={{8,0},{9,1},{10,2},{11,3},{12,4},{13,5},{14,6},{15,7},{24,16},{25,... | collective-permute-start | bytes 138248 | tf_op jit(solution)/shard_map/ppermute | solution.py:14
  333.3 40.8 %collective-permute-start.74 = (bf16[160,144]{0,1:T(8,128)(2,1)S(1)}, bf16[160,144]{0,1:T(8,128)(2,1)S(1)}, u32[]{:S(2)}, u32[]{:S(2)}) collective-permute-start(bf16[160,144]{0,1:T(8,128)(2,1)S(1)} %add_convert_fusion.2), channel_id=1, source_target_pairs={{0,32},{16,48},{32,64},{48,80},{64,96},{80,112},{96,128},{112,144}... | collective-permute-start | bytes 138248 | tf_op jit(solution)/shard_map/ppermute | solution.py:14
  345.8 10.2 %collective-permute-start.69 = (bf16[160,144]{0,1:T(8,128)(2,1)S(1)}, bf16[160,144]{0,1:T(8,128)(2,1)S(1)}, u32[]{:S(2)}, u32[]{:S(2)}) collective-permute-start(bf16[160,144]{0,1:T(8,128)(2,1)S(1)} %collective-permute-done.66), channel_id=1, source_target_pairs={{0,4},{1,5},{2,6},{3,7},{4,8},{5,9},{6,10},{7,11},{8,12},{9,13},{1... | collective-permute-start | bytes 138248 | tf_op jit(solution)/shard_map/ppermute | solution.py:14
  363.0 9.0 %collective-permute-start.72 = (bf16[160,144]{0,1:T(8,128)(2,1)S(1)}, bf16[160,144]{0,1:T(8,128)(2,1)S(1)}, u32[]{:S(2)}, u32[]{:S(2)}) collective-permute-start(bf16[160,144]{0,1:T(8,128)(2,1)S(1)} %collective-permute-done.66), channel_id=1, source_target_pairs={{8,0},{9,1},{10,2},{11,3},{12,4},{13,5},{14,6},{15,7},{24,16},{25,... | collective-permute-start | bytes 138248 | tf_op jit(solution)/shard_map/ppermute | solution.py:14
  372.1 8.0 %collective-permute-start.73 = (bf16[160,144]{0,1:T(8,128)(2,1)S(1)}, bf16[160,144]{0,1:T(8,128)(2,1)S(1)}, u32[]{:S(2)}, u32[]{:S(2)}) collective-permute-start(bf16[160,144]{0,1:T(8,128)(2,1)S(1)} %collective-permute-done.66), channel_id=1, source_target_pairs={{12,0},{13,1},{14,2},{15,3},{28,16},{29,17},{30,18},{31,19},{44,32... | collective-permute-start | bytes 138248 | tf_op jit(solution)/shard_map/ppermute | solution.py:14
  374.0 31.0 %collective-permute-start.79 = (bf16[160,144]{0,1:T(8,128)(2,1)S(1)}, bf16[160,144]{0,1:T(8,128)(2,1)S(1)}, u32[]{:S(2)}, u32[]{:S(2)}) collective-permute-start(bf16[160,144]{0,1:T(8,128)(2,1)S(1)} %add_convert_fusion.2), channel_id=1, source_target_pairs={{0,12},{1,13},{2,14},{3,15},{16,28},{17,29},{18,30},{19,31},{32,44... | collective-permute-start | bytes 138248 | tf_op jit(solution)/shard_map/ppermute | solution.py:14
  385.5 9.0 %collective-permute-start.77 = (bf16[160,144]{0,1:T(8,128)(2,1)S(1)}, bf16[160,144]{0,1:T(8,128)(2,1)S(1)}, u32[]{:S(2)}, u32[]{:S(2)}) collective-permute-start(bf16[160,144]{0,1:T(8,128)(2,1)S(1)} %collective-permute-done.74), channel_id=1, source_target_pairs={{8,0},{9,1},{10,2},{11,3},{12,4},{13,5},{14,6},{15,7},{24,16},{25,... | collective-permute-start | bytes 138248 | tf_op jit(solution)/shard_map/ppermute | solution.py:14
  394.5 8.6 %collective-permute-start.78 = (bf16[160,144]{0,1:T(8,128)(2,1)S(1)}, bf16[160,144]{0,1:T(8,128)(2,1)S(1)}, u32[]{:S(2)}, u32[]{:S(2)}) collective-permute-start(bf16[160,144]{0,1:T(8,128)(2,1)S(1)} %collective-permute-done.74), channel_id=1, source_target_pairs={{12,0},{13,1},{14,2},{15,3},{28,16},{29,17},{30,18},{31,19},{44,32... | collective-permute-start | bytes 138248 | tf_op jit(solution)/shard_map/ppermute | solution.py:14
  405.0 9.0 %collective-permute-start.81 = (bf16[160,144]{0,1:T(8,128)(2,1)S(1)}, bf16[160,144]{0,1:T(8,128)(2,1)S(1)}, u32[]{:S(2)}, u32[]{:S(2)}) collective-permute-start(bf16[160,144]{0,1:T(8,128)(2,1)S(1)} %add_convert_fusion.2), channel_id=1, source_target_pairs={{8,0},{9,1},{10,2},{11,3},{12,4},{13,5},{14,6},{15,7},{24,16},{25,... | collective-permute-start | bytes 138248 | tf_op jit(solution)/shard_map/ppermute | solution.py:14
  407.0 13.0 %collective-permute-start.82 = (bf16[160,144]{0,1:T(8,128)(2,1)S(1)}, bf16[160,144]{0,1:T(8,128)(2,1)S(1)}, u32[]{:S(2)}, u32[]{:S(2)}) collective-permute-start(bf16[160,144]{0,1:T(8,128)(2,1)S(1)} %add_convert_fusion.2), channel_id=1, source_target_pairs={{12,0},{13,1},{14,2},{15,3},{28,16},{29,17},{30,18},{31,19},{44,32... | collective-permute-start | bytes 138248 | tf_op jit(solution)/shard_map/ppermute | solution.py:14
  414.0 7.9 %collective-permute-start.83 = (bf16[160,144]{0,1:T(8,128)(2,1)S(1)}, bf16[160,144]{0,1:T(8,128)(2,1)S(1)}, u32[]{:S(2)}, u32[]{:S(2)}) collective-permute-start(bf16[160,144]{0,1:T(8,128)(2,1)S(1)} %add_convert_fusion.2), channel_id=1, source_target_pairs={{32,0},{48,16},{64,32},{80,48},{96,64},{112,80},{128,96},{144,112}... | collective-permute-start | bytes 138248 | tf_op jit(solution)/shard_map/ppermute | solution.py:14
  420.0 21.5 %collective-permute-start.88 = (bf16[160,144]{0,1:T(8,128)(2,1)S(1)}, bf16[160,144]{0,1:T(8,128)(2,1)S(1)}, u32[]{:S(2)}, u32[]{:S(2)}) collective-permute-start(bf16[160,144]{0,1:T(8,128)(2,1)S(1)} %add_convert_fusion.2), channel_id=1, source_target_pairs={{64,0},{80,16},{96,32},{112,48},{128,64},{144,80},{160,96},{176,11... | collective-permute-start | bytes 138248 | tf_op jit(solution)/shard_map/ppermute | solution.py:14
  430.5 9.1 %collective-permute-start.86 = (bf16[160,144]{0,1:T(8,128)(2,1)S(1)}, bf16[160,144]{0,1:T(8,128)(2,1)S(1)}, u32[]{:S(2)}, u32[]{:S(2)}) collective-permute-start(bf16[160,144]{0,1:T(8,128)(2,1)S(1)} %collective-permute-done.83), channel_id=1, source_target_pairs={{8,0},{9,1},{10,2},{11,3},{12,4},{13,5},{14,6},{15,7},{24,16},{25,... | collective-permute-start | bytes 138248 | tf_op jit(solution)/shard_map/ppermute | solution.py:14
  441.5 43.7 %collective-permute-start.96 = (bf16[160,144]{0,1:T(8,128)(2,1)S(1)}, bf16[160,144]{0,1:T(8,128)(2,1)S(1)}, u32[]{:S(2)}, u32[]{:S(2)}) collective-permute-start(bf16[160,144]{0,1:T(8,128)(2,1)S(1)} %add_convert_fusion.2), channel_id=1, source_target_pairs={{96,0},{112,16},{128,32},{144,48},{160,64},{176,80},{192,96},{208,... | collective-permute-start | bytes 138248 | tf_op jit(solution)/shard_map/ppermute | solution.py:14
  446.9 7.9 %collective-permute-start.89 = (bf16[160,144]{0,1:T(8,128)(2,1)S(1)}, bf16[160,144]{0,1:T(8,128)(2,1)S(1)}, u32[]{:S(2)}, u32[]{:S(2)}) collective-permute-start(bf16[160,144]{0,1:T(8,128)(2,1)S(1)} %collective-permute-done.88), channel_id=1, source_target_pairs={{0,12},{1,13},{2,14},{3,15},{16,28},{17,29},{18,30},{19,31},{32,44... | collective-permute-start | bytes 138248 | tf_op jit(solution)/shard_map/ppermute | solution.py:14
  457.5 9.9 %collective-permute-start.91 = (bf16[160,144]{0,1:T(8,128)(2,1)S(1)}, bf16[160,144]{0,1:T(8,128)(2,1)S(1)}, u32[]{:S(2)}, u32[]{:S(2)}) collective-permute-start(bf16[160,144]{0,1:T(8,128)(2,1)S(1)} %collective-permute-done.88), channel_id=1, source_target_pairs={{0,4},{1,5},{2,6},{3,7},{4,8},{5,9},{6,10},{7,11},{8,12},{9,13},{1... | collective-permute-start | bytes 138248 | tf_op jit(solution)/shard_map/ppermute | solution.py:14
  474.3 9.0 %collective-permute-start.94 = (bf16[160,144]{0,1:T(8,128)(2,1)S(1)}, bf16[160,144]{0,1:T(8,128)(2,1)S(1)}, u32[]{:S(2)}, u32[]{:S(2)}) collective-permute-start(bf16[160,144]{0,1:T(8,128)(2,1)S(1)} %collective-permute-done.88), channel_id=1, source_target_pairs={{8,0},{9,1},{10,2},{11,3},{12,4},{13,5},{14,6},{15,7},{24,16},{25,... | collective-permute-start | bytes 138248 | tf_op jit(solution)/shard_map/ppermute | solution.py:14
  483.3 38.4 %collective-permute-start.95 = (bf16[160,144]{0,1:T(8,128)(2,1)S(1)}, bf16[160,144]{0,1:T(8,128)(2,1)S(1)}, u32[]{:S(2)}, u32[]{:S(2)}) collective-permute-start(bf16[160,144]{0,1:T(8,128)(2,1)S(1)} %collective-permute-done.88), channel_id=1, source_target_pairs={{12,0},{13,1},{14,2},{15,3},{28,16},{29,17},{30,18},{31,19},{44,32... | collective-permute-start | bytes 138248 | tf_op jit(solution)/shard_map/ppermute | solution.py:14
  485.3 118.8 %collective-permute-start.1 = (bf16[2,512,144]{1,2,0:T(8,128)(2,1)}, bf16[2,512,144]{1,2,0:T(8,128)(2,1)}, u32[]{:S(2)}, u32[]{:S(2)}) collective-permute-start(bf16[2,512,144]{1,2,0:T(8,128)(2,1)} %pad_maximum_fusion.1), channel_id=1, source_target_pairs={{1,0},{2,1},{3,2},{4,3},{5,4},{6,5},{7,6},{8,7},{9,8},{10,9},{11,1... | collective-permute-start | bytes 884744 | tf_op jit(solution)/shard_map/ppermute | solution.py:14
  521.7 8.9 %collective-permute-start.97 = (bf16[160,144]{0,1:T(8,128)(2,1)S(1)}, bf16[160,144]{0,1:T(8,128)(2,1)S(1)}, u32[]{:S(2)}, u32[]{:S(2)}) collective-permute-start(bf16[160,144]{0,1:T(8,128)(2,1)S(1)} %collective-permute-done.96), channel_id=1, source_target_pairs={{0,12},{1,13},{2,14},{3,15},{16,28},{17,29},{18,30},{19,31},{32,44... | collective-permute-start | bytes 138248 | tf_op jit(solution)/shard_map/ppermute | solution.py:14
  533.7 9.7 %collective-permute-start.99 = (bf16[160,144]{0,1:T(8,128)(2,1)S(1)}, bf16[160,144]{0,1:T(8,128)(2,1)S(1)}, u32[]{:S(2)}, u32[]{:S(2)}) collective-permute-start(bf16[160,144]{0,1:T(8,128)(2,1)S(1)} %collective-permute-done.96), channel_id=1, source_target_pairs={{0,4},{1,5},{2,6},{3,7},{4,8},{5,9},{6,10},{7,11},{8,12},{9,13},{1... | collective-permute-start | bytes 138248 | tf_op jit(solution)/shard_map/ppermute | solution.py:14
  550.4 9.0 %collective-permute-start.102 = (bf16[160,144]{0,1:T(8,128)(2,1)S(1)}, bf16[160,144]{0,1:T(8,128)(2,1)S(1)}, u32[]{:S(2)}, u32[]{:S(2)}) collective-permute-start(bf16[160,144]{0,1:T(8,128)(2,1)S(1)} %collective-permute-done.96), channel_id=1, source_target_pairs={{8,0},{9,1},{10,2},{11,3},{12,4},{13,5},{14,6},{15,7},{24,16},{25,... | collective-permute-start | bytes 138248 | tf_op jit(solution)/shard_map/ppermute | solution.py:14
  566.6 49.6 %collective-permute-start.2 = (bf16[512,144]{0,1:T(8,128)(2,1)}, bf16[512,144]{0,1:T(8,128)(2,1)}, u32[]{:S(2)}, u32[]{:S(2)}) collective-permute-start(bf16[512,144]{0,1:T(8,128)(2,1)} %collective-permute-done), channel_id=1, source_target_pairs={{0,1},{1,2},{2,3},{3,4},{4,5},{5,6},{6,7},{7,8},{8,9},{9,10},{10,1... | collective-permute-start | bytes 442376 | tf_op jit(solution)/shard_map/ppermute | solution.py:14
  577.0 9.0 %collective-permute-start.104 = (bf16[160,144]{0,1:T(8,128)(2,1)S(1)}, bf16[160,144]{0,1:T(8,128)(2,1)S(1)}, u32[]{:S(2)}, u32[]{:S(2)}) collective-permute-start(bf16[160,144]{0,1:T(8,128)(2,1)S(1)} %get-tuple-element.19), channel_id=1, source_target_pairs={{0,16},{16,0},{32,48},{48,32},{64,80},{80,64},{96,112},{112,96},{1... | collective-permute-start | bytes 138248 | tf_op jit(solution)/shard_map/ppermute | solution.py:8
  589.6 11.0 %collective-permute-start.106 = (bf16[160,144]{0,1:T(8,128)(2,1)S(1)}, bf16[160,144]{0,1:T(8,128)(2,1)S(1)}, u32[]{:S(2)}, u32[]{:S(2)}) collective-permute-start(bf16[160,144]{0,1:T(8,128)(2,1)S(1)} %fusion.59), channel_id=1, source_target_pairs={{0,2},{1,3},{2,0},{3,1},{4,6},{5,7},{6,4},{7,5},{8,10},{9,11},{10,... | collective-permute-start | bytes 138248 | tf_op jit(solution)/shard_map/ppermute | solution.py:8
  598.6 17.6 %collective-permute-start.6 = (bf16[512,144]{0,1:T(8,128)(2,1)}, bf16[512,144]{0,1:T(8,128)(2,1)}, u32[]{:S(2)}, u32[]{:S(2)}) collective-permute-start(bf16[512,144]{0,1:T(8,128)(2,1)} %get-tuple-element.14), channel_id=1, source_target_pairs={{0,1},{1,2},{2,3},{3,4},{4,5},{5,6},{6,7},{7,8},{8,9},{9,10},{10,1... | collective-permute-start | bytes 442376 | tf_op jit(solution)/shard_map/ppermute | solution.py:14
  600.5 15.7 %collective-permute-start.5 = (bf16[512,144]{0,1:T(8,128)(2,1)}, bf16[512,144]{0,1:T(8,128)(2,1)}, u32[]{:S(2)}, u32[]{:S(2)}) collective-permute-start(bf16[512,144]{0,1:T(8,128)(2,1)} %get-tuple-element.13), channel_id=1, source_target_pairs={{1,0},{2,1},{3,2},{4,3},{5,4},{6,5},{7,6},{8,7},{9,8},{10,9},{11,1... | collective-permute-start | bytes 442376 | tf_op jit(solution)/shard_map/ppermute | solution.py:14
  (54 other events, 680.9 us)
where the time goes:
time: 621 us; the launch traced here: 619 us
  starting transfers between devices  386 us (62%)
  waiting for transfers between devices  163 us (26%)
  local copies, waits for them, and re-layouts  39 us (6%)
  matrix products  16.8 us (3%)
  between operations  9.64 us (2%)
    ppermute x99, starting transfers between devices, from_behind(): lax.ppermute(value, axis, [(source, source + steps) for source in range(f...  334 us
    ppermute x99, waiting for transfers between devices, from_behind(): lax.ppermute(value, axis, [(source, source + steps) for source in range(f...  155 us
    ppermute x10, starting transfers between devices, swapped(): lax.ppermute(array, axis, [(i, i ^ 1 << apart) for i in range(lax.axis_si...  51.5 us
    unnamed x108, local copies, waits for them, and re-layouts  29 us
  transfers between devices with their start and end apart: 109, of which 56 were waited for; matrix products, arithmetic and copies ran while one was open for 9% of the time, Pallas kernels for 0%

commit v1 on v0

v1 whole, which is shorter than its diff:
```python
import functools

import jax
import jax.numpy as jnp
from jax import lax
from jax.experimental import pallas as pl
from jax.experimental.pallas import tpu as pltpu
from jax.sharding import Mesh, PartitionSpec as P

AXES = ("y", "xh", "xl", "zh", "zl", "c")
F32, BF16, I32 = jnp.float32, jnp.bfloat16, jnp.int32
RANK, CHUNK, PAD = 160, 36, 40
SLOTS = (7, 4)
VMEM = pl.BlockSpec(memory_space=pltpu.VMEM)
SMEM = pl.BlockSpec(memory_space=pltpu.SMEM)


def call(body, outs, scratch, specs, flops, moved):
    return pl.pallas_call(
        body,
        out_shape=outs,
        in_specs=specs,
        out_specs=jax.tree.map(lambda _: VMEM, outs),
        scratch_shapes=scratch,
        compiler_params=pltpu.CompilerParams(vmem_limit_bytes=24 * 2**20),
        cost_estimate=pl.CostEstimate(flops=flops, bytes_accessed=moved, transcendentals=0),
    )


def shape(*dims, dtype=BF16):
    return jax.ShapeDtypeStruct(dims, dtype)


def mul(a, b):
    return lax.dot_general(a, b, (((1,), (0,)), ((), ())), preferred_element_type=F32)


def mul_t(a, b):
    return lax.dot_general(a, b, (((1,), (1,)), ((), ())), preferred_element_type=F32)


def spreader(groups, cols, transposed=False):
    dims = (cols, groups * PAD) if transposed else (groups * PAD, cols)
    padded = lax.broadcasted_iota(I32, dims, 1 if transposed else 0)
    dense = lax.broadcasted_iota(I32, dims, 0 if transposed else 1)
    hit = jnp.zeros(dims, jnp.bool_)
    for g in range(groups):
        inside = (padded >= PAD * g) & (padded < PAD * g + CHUNK)
        hit = hit | (inside & (dense == padded - (PAD - CHUNK) * g))
    return jnp.where(hit, 1.0, 0.0).astype(BF16)


def packed(a, b, tail, wide):
    wide[0, :, :RANK] = a
    wide[1, :, :RANK] = b
    rest = wide[0, :, 128:] + pltpu.roll(wide[1, :, 128:], 32, 1)
    return jnp.concatenate([wide[0, :, :128], wide[1, :, :128], rest, tail], axis=0).astype(BF16)


def up_body(x_ref, basis_ref, one_ref, two_ref, far_one_ref, far_two_ref, out_ref, wide, tail):
    wide[...] = jnp.zeros_like(wide)
    tail[...] = jnp.zeros_like(tail)
    tail[0:1, : SLOTS[0]] = far_one_ref[...]
    tail[1:2, : SLOTS[1]] = far_two_ref[...]
    last = tail[...].astype(F32)
    leaf = mul_t(x_ref[...], basis_ref[...]).astype(BF16)
    up = mul(leaf, one_ref[...]).astype(BF16)
    chunks = mul(spreader(4, 144), up)
    quarter = two_ref[...].astype(F32)
    for q in range(4):
        block = packed(chunks[PAD * q : PAD * (q + 1)], quarter, last, wide)
        for xh in range(2):
            for zl in range(2):
                out_ref[xh * 8 + (q // 2) * 4 + zl * 2 + q % 2] = block


def merge_body(me_ref, got_ref, window_ref, level_ref, lists_ref, wide, levels):
    me = me_ref[0]
    own = (me // 32) % 2 * 2 + me // 2 % 2
    groups = []
    for xh in range(2):
        second = jnp.zeros((PAD, RANK), F32)
        for zl in range(2):
            main = jnp.zeros((PAD, 128), F32)
            rest = jnp.zeros((PAD, 128), F32)
            for q in range(4):
                block = got_ref[xh * 8 + (q // 2) * 4 + zl * 2 + q % 2].astype(F32)
                main += block[:PAD]
                rest += block[2 * PAD : 3 * PAD]
                rows = slice(PAD * q, PAD * (q + 1))
                levels[xh * 2 + zl, rows, :128] = block[PAD : 2 * PAD]
                levels[xh * 2 + zl, rows, 128:] = pltpu.roll(block[2 * PAD : 3 * PAD], 96, 1)
            wide[:, :128] = main
            wide[:, 128:] = rest
            first = wide[:, :RANK]
            groups.append(first)
            second += mul(first.astype(BF16), levels[xh * 2 + zl, :, :RANK].astype(BF16))
        groups.append(second)
    stack = jnp.concatenate(groups, axis=0).astype(BF16)
    window_ref[...] = lax.dot_general(
        stack, spreader(6, 256), (((0,), (0,)), ((), ())), preferred_element_type=F32
    ).astype(BF16)
    level_ref[...] = levels[own, :, :RANK].astype(BF16)
    for q in range(4):
        place = (me // 32) % 2 * 8 + (q // 2) * 4 + me // 2 % 2 * 2 + q % 2
        tail = got_ref[place, 112:, :].astype(F32)
        lists_ref[q : q + 1, :] = tail[8:9].astype(I32)
        lists_ref[4 + q : 5 + q, :] = tail[9:10].astype(I32)


def pack_body(one_ref, two_ref, out_ref, wide):
    wide[...] = jnp.zeros_like(wide)
    for k in range(sum(SLOTS)):
        block = one_ref[k] if k < SLOTS[0] else two_ref[k - SLOTS[0]]
        out_ref[k, :RANK, :] = block[:, :128]
        wide[:, :32] = block[:, 128:].astype(F32)
        rest = wide[0:PAD]
        for r in range(1, 4):
            rest += pltpu.roll(wide[PAD * r : PAD * (r + 1)], 32 * r, 1)
        out_ref[k, RANK:, :] = rest.astype(BF16)


def couple_body(me_ref, lists_ref, up_ref, mid_ref, down_ref, own_ref, beside_ref, across_ref, out_ref, rows, total, matrix, wide):
    me = me_ref[0]
    y = me // 64
    q_own = me // 16 % 2 * 2 + me % 2
    rows[0] = up_ref[...]
    rows[1] = mid_ref[...]
    rows[2] = down_ref[...]
    total[...] = jnp.zeros_like(total)
    lane = lax.broadcasted_iota(I32, (RANK, 256), 1)
    slots = sum(SLOTS)

    def step(k, source, offset, q):
        second = k >= SLOTS[0]
        code = lists_ref[jnp.where(second, 4 + q, q), jnp.where(second, k - SLOTS[0], k)]
        valid = code >= 0
        safe = jnp.where(valid, code, y * jnp.where(second, 8, 16))
        width = jnp.where(second, 4, 8)
        row, col = safe // width, safe % width
        zh = jnp.where(second, col, col // 2)
        group = row % 2 * 3 + jnp.where(second, 2, col % 2)
        low = jnp.where(valid, group * CHUNK, 512)
        block = rows[row // 2 - y + 1, zh]
        block = jnp.where((lane >= low) & (lane < low + CHUNK), block.astype(F32), 0.0).astype(BF16)
        matrix[:, :128] = source[offset + k, :RANK, :].astype(F32)
        rest = source[offset + k, RANK:, :].astype(F32)
        for r in range(4):
            matrix[PAD * r : PAD * (r + 1), 128:] = rest if r == 0 else pltpu.roll(rest, 128 - 32 * r, 1)
        total[...] += mul(matrix[:, :RANK].astype(BF16), block)

    def every(k, carry):
        step(k, own_ref, 0, q_own)
        step(k, beside_ref, 0, q_own ^ 2)
        step(k, across_ref, 0, q_own ^ 1)
        step(k, across_ref, slots, q_own ^ 3)
        return carry

    lax.fori_loop(0, slots, every, 0)
    high = total[...].astype(BF16)
    low = (total[...] - high.astype(F32)).astype(BF16)
    r = lax.broadcasted_iota(I32, (PAD, 256), 0)
    c = lax.broadcasted_iota(I32, (PAD, 256), 1)
    results = []
    for members in ((0, 1, 3, 4), (2, 5)):
        hit = jnp.zeros((PAD, 256), jnp.bool_)
        for g in members:
            hit = hit | ((c == r + CHUNK * g) & (r < CHUNK))
        picker = jnp.where(hit, 1.0, 0.0).astype(BF16)
        results.append(mul_t(picker, high) + mul_t(picker, low))
    wide[...] = jnp.zeros_like(wide)
    block = packed(results[0], results[1], jnp.zeros((8, 128), F32), wide)
    for d in range(8):
        out_ref[d] = block


def down_body(me_ref, got_ref, level_ref, one_ref, basis_ref, near_ref, out_ref, wide, local):
    me = me_ref[0]
    zl_own = me // 2 % 2
    for q in range(4):
        base = q // 2 * 4 + q % 2
        mine = got_ref[base + zl_own * 2].astype(F32)
        both = got_ref[base].astype(F32) + got_ref[base + 2].astype(F32)
        wide[:, :128] = both[PAD : 2 * PAD]
        wide[:, 128:] = pltpu.roll(both[2 * PAD : 3 * PAD], 96, 1)
        second = wide[:, :RANK].astype(BF16)
        wide[:, :128] = mine[:PAD]
        wide[:, 128:] = mine[2 * PAD : 3 * PAD]
        local[PAD * q : PAD * (q + 1), :] = wide[:, :RANK] + mul_t(second, level_ref[...])
    one = mul(spreader(4, 144, True), local[...].astype(BF16)).astype(BF16)
    leaf = mul_t(one, one_ref[...]).astype(BF16)
    out_ref[...] = (near_ref[...] + mul(leaf, basis_ref[...])).astype(BF16)


def slot_of(list_ref, me, apart):
    found = jnp.int32(0)
    for k in range(1, 4):
        found = jnp.where(list_ref[0, k] == me + apart, k, found)
    return found


def mirror_body(me_ref, list_ref, x_ref, blocks_ref, left_ref, right_ref, below_ref):
    me = me_ref[0]
    x = x_ref[...]
    left_ref[0] = x
    right_ref[0] = x
    right_ref[1] = mul(x, blocks_ref[slot_of(list_ref, me, 1)]).astype(BF16)
    left_ref[1] = mul(x, blocks_ref[slot_of(list_ref, me, 15)]).astype(BF16)
    below_ref[...] = mul(x, blocks_ref[slot_of(list_ref, me, 16)]).astype(BF16)
    right_ref[2] = mul(x, blocks_ref[slot_of(list_ref, me, 17)]).astype(BF16)


def turn_body(x_ref, below_ref, from_right_ref, from_left_ref, rise_ref, sink_ref):
    rise_ref[0] = from_left_ref[0]
    rise_ref[1] = x_ref[...]
    rise_ref[2] = from_right_ref[0]
    sink_ref[...] = (
        below_ref[...].astype(F32) + from_left_ref[2].astype(F32) + from_right_ref[1].astype(F32)
    ).astype(BF16)


def near_body(me_ref, list_ref, x_ref, self_ref, blocks_ref, from_right_ref, from_left_ref, risen_ref, sunk_ref, out_ref):
    me = me_ref[0]
    total = mul_t(x_ref[...], self_ref[...])
    total += mul_t(from_right_ref[0], blocks_ref[slot_of(list_ref, me, 1)])
    total += mul_t(risen_ref[0], blocks_ref[slot_of(list_ref, me, 15)])
    total += mul_t(risen_ref[1], blocks_ref[slot_of(list_ref, me, 16)])
    total += mul_t(risen_ref[2], blocks_ref[slot_of(list_ref, me, 17)])
    out_ref[...] = total + from_left_ref[1].astype(F32) + sunk_ref[...].astype(F32)


def shards(
    right_sides,
    near_self,
    near_blocks,
    near_list,
    basis,
    transfer_one,
    transfer_two,
    couple_one,
    couple_two,
    far_list_one,
    far_list_two,
):
    me = lax.axis_index(AXES).astype(I32).reshape(1)
    x = right_sides[0, 0].T
    vectors = basis[0, 0].T
    one = transfer_one[0, 0]
    blocks = near_blocks[0, 0]
    links = near_list[0]

    message = call(
        up_body,
        shape(16, 128, 128),
        [pltpu.VMEM((2, PAD, 256), F32), pltpu.VMEM((8, 128), I32)],
        [VMEM] * 6,
        50 * 10**6,
        10**6,
    )(x, vectors, one, transfer_two[0, 0], far_list_one[0], far_list_two[0])
    got = lax.all_to_all(message, ("xh", "xl", "zl", "c"), 0, 0)
    window, level, lists = call(
        merge_body,
        (shape(RANK, 256), shape(RANK, RANK), shape(8, 128, dtype=I32)),
        [pltpu.VMEM((PAD, 256), F32), pltpu.VMEM((4, RANK, 256), F32)],
        [SMEM, VMEM],
        50 * 10**6,
        10**6,
    )(me, got)

    own = call(
        pack_body,
        shape(sum(SLOTS), RANK + PAD, 128),
        [pltpu.VMEM((RANK, 128), F32)],
        [VMEM] * 2,
        10**6,
        15 * 10**5,
    )(couple_one[0, 0], couple_two[0, 0])
    beside = lax.ppermute(own, "xl", [(0, 1), (1, 0)])
    across = lax.ppermute(jnp.concatenate([own, beside]), "c", [(0, 1), (1, 0)])

    left, right, below = call(
        mirror_body,
        (shape(2, 144, 512), shape(3, 144, 512), shape(144, 512)),
        [],
        [SMEM, SMEM, VMEM, VMEM],
        3 * 10**8,
        3 * 10**6,
    )(me, links, x, blocks)
    across_gy = ("zh", "zl", "c")
    along_gx = ("y", "xh", "xl")
    from_right = lax.ppermute(left, across_gy, [(i + 1, i) for i in range(15)])
    from_left = lax.ppermute(right, across_gy, [(i, i + 1) for i in range(15)])
    rise, sink = call(
        turn_body, (shape(3, 144, 512), shape(144, 512)), [], [VMEM] * 4, 10**6, 2 * 10**6
    )(x, below, from_right, from_left)
    risen = lax.ppermute(rise, along_gx, [(i + 1, i) for i in range(31)])
    sunk = lax.ppermute(sink, along_gx, [(i, i + 1) for i in range(31)])

    plane = lax.all_gather(window, "zh")
    above = lax.ppermute(plane, "y", [(i, i + 1) for i in range(7)])
    under = lax.ppermute(plane, "y", [(i + 1, i) for i in range(7)])

    near = call(
        near_body,
        shape(144, 512, dtype=F32),
        [],
        [SMEM, SMEM] + [VMEM] * 7,
        4 * 10**8,
        4 * 10**6,
    )(me, links, x, near_self[0, 0], blocks, from_right, from_left, risen, sunk)

    partial = call(
        couple_body,
        shape(8, 128, 128),
        [
            pltpu.VMEM((3, 4, RANK, 256), BF16),
            pltpu.VMEM((RANK, 256), F32),
            pltpu.VMEM((RANK, 256), F32),
            pltpu.VMEM((2, PAD, 256), F32),
        ],
        [SMEM, SMEM] + [VMEM] * 6,
        6 * 10**8,
        4 * 10**6,
    )(me, lists, above, plane, under, own, beside, across)
    sums = lax.all_to_all(partial, ("xl", "zl", "c"), 0, 0)
    applied = call(
        down_body,
        shape(144, 512),
        [pltpu.VMEM((PAD, 256), F32), pltpu.VMEM((RANK, RANK), F32)],
        [SMEM] + [VMEM] * 5,
        50 * 10**6,
        10**6,
    )(me, sums, level, one, vectors, near)
    return applied.T[None, None]


def solution(mesh):
    split = Mesh(mesh.devices.reshape(8, 2, 2, 4, 2, 2), AXES)
    rows, cols = AXES[:3], AXES[3:]

    def spec(rank):
        return P(rows, cols, *[None] * (rank - 2))

    ranks = (4, 4, 5, 3, 4, 4, 4, 5, 5, 3, 3)
    return jax.shard_map(
        shards, mesh=split, in_specs=tuple(map(spec, ranks)), out_specs=spec(4), check_vma=False
    )
```

time: 621 us -> 105 us (0.17)
  the two profiles are of different devices: /device:TPU:105 before, /device:TPU:33 now
where the time goes in v1:
time: 105 us
  starting transfers between devices  38 us (36%)
  waiting for transfers between devices  20.4 us (19%)
  blocking collectives  19.8 us (19%)
  Pallas kernels  15.2 us (14%)
  local copies, waits for them, and re-layouts  9.65 us (9%)
  other arithmetic  1.1 us (1%)
    all_gather x1, blocking collectives, shards(): plane = lax.all_gather(window, 'zh')  19.8 us
    unnamed x42, local copies, waits for them, and re-layouts  9.65 us
    ppermute x1, waiting for transfers between devices, shards(): sunk = lax.ppermute(sink, along_gx, [(i, i + 1) for i in range(31)])  8.16 us
    all_to_all x1, starting transfers between devices, shards(): got = lax.all_to_all(message, ('xh', 'xl', 'zl', 'c'), 0, 0)  6.78 us
    ppermute x1, waiting for transfers between devices, shards(): from_right = lax.ppermute(left, across_gy, [(i + 1, i) for i in range(15)])  6.61 us
    ppermute x1, starting transfers between devices, shards(): across = lax.ppermute(jnp.concatenate([own, beside]), 'c', [(0, 1), (1, 0)])  5.92 us
    ppermute x1, waiting for transfers between devices, shards(): beside = lax.ppermute(own, 'xl', [(0, 1), (1, 0)])  5.65 us
    pallas_call x1, Pallas kernels, shards(): call(couple_body, shape(8, 128, 128), [pltpu.VMEM((3, 4, RANK, 256), BF16...  4.94 us
  transfers between devices with their start and end apart: 10, of which 3 were waited for; matrix products, arithmetic and copies ran while one was open for 1% of the time, Pallas kernels for 13%

profile of v1, /device:TPU:33, one launch (start us, length us, event | category | flops | bytes accessed | tf_op | source)
XLA Modules:
  0.0 104.5 jit_solution(18180074057186177996)
XLA Ops:
  0.0 0.0 copy-start.1
  0.0 0.0 copy-start.5
  0.0 0.0 copy-start.6
  0.0 1.1 %copy-done.6 = bf16[1,1,7,160,160]{4,3,2,1,0:T(8,128)(2,1)S(1)} copy-done((bf16[1,1,7,160,160]{4,3,2,1,0:T(8,128)(2,1)S(1)}, bf16[1,1,7,160,160]{4,3,2,1,0:T(8,128)(2,1)}, u32[]{:S(2)}) %copy-start.6) | copy-done | bytes 358424
  1.1 0.0 copy-start.10
  1.1 1.0 copy-done.10
  2.1 0.0 copy-start.8
  2.1 0.0 copy-start.15
  2.1 0.0 copy-start.17
  2.1 0.0 copy-start.18
  2.1 0.3 shard_map.111.own_ref
  2.4 3.1 %collective-permute-start.2 = (bf16[11,200,128]{2,1,0:T(8,128)(2,1)S(1)}, bf16[11,200,128]{2,1,0:T(8,128)(2,1)S(1)}, u32[]{:S(2)}, u32[]{:S(2)}) collective-permute-start(bf16[11,200,128]{2,1,0:T(8,128)(2,1)S(1)} %shard_map.111.own_ref), channel_id=1, source_target_pairs={{0,16},{16,0},{1,17},{17,1},{2,18},{18,2},{3,19},{19,3},{4,20},{20... | collective-permute-start | bytes 1689608 | tf_op jit(solution)/shard_map/ppermute | solution.py:278
  5.5 0.0 copy-done.1
  5.6 0.0 copy-done.5
  5.6 0.0 copy-done.8
  5.6 0.0 copy-done.15
  5.6 0.0 copy-done.17
  5.6 0.0 copy-done.18
  5.6 1.4 %shard_map.109 = bf16[16,128,128]{2,1,0:T(8,128)(2,1)} custom-call(bf16[144,512]{1,0:T(8,128)(2,1)S(1)} %bitcast.22, bf16[160,512]{1,0:T(8,128)(2,1)S(1)} %bitcast.29, bf16[160,160]{1,0:T(8,128)(2,1)S(1)} %bitcast.33, bf16[40,160]{1,0:T(8,128)(2,1)S(1)} %bitcast.36, s32[1,7]{1,0:T(1,128)S(1)} %bitcast.39, s32[1,4]{1,0:T(1,128)S(1)} %bitcast.40), custom_call_target="tpu_custom_call" | custom-call | flops 50000000 | bytes 1000000 | tf_op jit(solution)/shard_map/pallas_call | solution.py:252
  7.0 6.8 %all-to-all-start = ((bf16[16,128,128]{2,1,0:T(8,128)(2,1)}), bf16[16,128,128]{2,1,0:T(8,128)(2,1)}, u32[]{:S(2)}, u32[]{:S(2)}) async-start(bf16[16,128,128]{2,1,0:T(8,128)(2,1)} %shard_map.109), calls=%async_computation | async-start | bytes 1048576 | tf_op jit(solution)/shard_map/all_to_all | solution.py:260
  13.7 0.0 copy-start
  13.8 0.0 copy-start.16
  13.8 5.7 %collective-permute-done.2.beside_ref = bf16[11,200,128]{2,1,0:T(8,128)(2,1)S(1)} collective-permute-done((bf16[11,200,128]{2,1,0:T(8,128)(2,1)S(1)}, bf16[11,200,128]{2,1,0:T(8,128)(2,1)S(1)}, u32[]{:S(2)}, u32[]{:S(2)}) %collective-permute-start.2) | collective-permute-done | bytes 563232 | tf_op jit(solution)/shard_map/ppermute | solution.py:278
  19.4 1.1 %pad_maximum_fusion = bf16[22,200,128]{2,1,0:T(8,128)(2,1)} fusion(bf16[11,200,128]{2,1,0:T(8,128)(2,1)S(1)} %collective-permute-done.2.beside_ref, bf16[11,200,128]{2,1,0:T(8,128)(2,1)S(1)} %shard_map.111.own_ref), kind=kLoop, calls=%fused_computation | loop fusion | flops 563200 | bytes 2252800 | tf_op jit(solution)/shard_map/concatenate | solution.py:279
  20.5 5.9 %collective-permute-start.3 = (bf16[22,200,128]{2,1,0:T(8,128)(2,1)}, bf16[22,200,128]{2,1,0:T(8,128)(2,1)}, u32[]{:S(2)}, u32[]{:S(2)}) collective-permute-start(bf16[22,200,128]{2,1,0:T(8,128)(2,1)} %pad_maximum_fusion), channel_id=1, source_target_pairs={{0,1},{1,0},{2,3},{3,2},{4,5},{5,4},{6,7},{7,6},{8,9},{9,8},{10,11... | collective-permute-start | bytes 3379208 | tf_op jit(solution)/shard_map/ppermute | solution.py:279
  26.5 0.0 copy-done
  26.5 0.0 copy-done.16
  26.5 1.8 %shard_map.113 = (bf16[2,144,512]{2,1,0:T(8,128)(2,1)S(1)}, bf16[3,144,512]{2,1,0:T(8,128)(2,1)}, bf16[144,512]{1,0:T(8,128)(2,1)S(1)}) custom-call(s32[1]{0:T(128)} %bitcast.me_ref, s32[1,4]{1,0:T(1,128)S(1)} %bitcast.37, bf16[144,512]{1,0:T(8,128)(2,1)S(1)} %bitcast.23, bf16[4,512,512]{2,1,0:T(8,128)(2,1)S(1)} %bitcast.20), custom_call_target="tpu_custom_call" | custom-call | flops 300000000 | bytes 3000000 | tf_op jit(solution)/shard_map/pallas_call | solution.py:281
  28.3 0.7 copy-done.11
  29.0 0.7 copy-done.19
  29.7 3.9 %collective-permute-start.5 = (bf16[3,144,512]{2,1,0:T(8,128)(2,1)}, bf16[3,144,512]{2,1,0:T(8,128)(2,1)}, u32[]{:S(2)}, u32[]{:S(2)}) collective-permute-start(bf16[3,144,512]{2,1,0:T(8,128)(2,1)} %get-tuple-element.17), channel_id=1, source_target_pairs={{0,1},{1,2},{2,3},{3,4},{4,5},{5,6},{6,7},{7,8},{8,9},{9,10},{10,1... | collective-permute-start | bytes 1327112 | tf_op jit(solution)/shard_map/ppermute | solution.py:292
  33.6 0.0 all-to-all-done.got_ref
  33.6 1.5 %shard_map.110 = (bf16[160,256]{1,0:T(8,128)(2,1)S(1)}, bf16[160,160]{1,0:T(8,128)(2,1)S(1)}, s32[8,128]{1,0:T(8,128)S(1)}) custom-call(s32[1]{0:T(128)} %bitcast.me_ref, bf16[16,128,128]{2,1,0:T(8,128)(2,1)} %all-to-all-done.got_ref), custom_call_target="tpu_custom_call" | custom-call | flops 50000000 | bytes 1000000 | tf_op jit(solution)/shard_map/pallas_call | solution.py:261
  35.1 0.0 copy-start.13
  35.1 19.8 %all-gather = bf16[640,256]{1,0:T(8,128)(2,1)S(1)} all-gather(bf16[160,256]{1,0:T(8,128)(2,1)S(1)} %get-tuple-element.14), channel_id=2, replica_groups=mesh['y'=8,'xh'=2,'xl'=2,'zh'=4,'zl'=2,'c'=2] {'zh'}, dimensions={0}, use_global_device_ids=true | all-gather | bytes 409600 | tf_op jit(solution)/shard_map/all_gather | solution.py:299
  54.9 2.3 %collective-permute-start = (bf16[4,160,256]{2,1,0:T(8,128)(2,1)S(1)}, bf16[4,160,256]{2,1,0:T(8,128)(2,1)S(1)}, u32[]{:S(2)}, u32[]{:S(2)}) collective-permute-start(bf16[4,160,256]{2,1,0:T(8,128)(2,1)S(1)} %bitcast.26), channel_id=1, source_target_pairs={{0,64},{64,128},{128,192},{192,256},{256,320},{320,384},{384,448},... | collective-permute-start | bytes 983048 | tf_op jit(solution)/shard_map/ppermute | solution.py:300
  57.1 4.2 %collective-permute-start.1 = (bf16[4,160,256]{2,1,0:T(8,128)(2,1)S(1)}, bf16[4,160,256]{2,1,0:T(8,128)(2,1)S(1)}, u32[]{:S(2)}, u32[]{:S(2)}) collective-permute-start(bf16[4,160,256]{2,1,0:T(8,128)(2,1)S(1)} %bitcast.27), channel_id=1, source_target_pairs={{64,0},{128,64},{192,128},{256,192},{320,256},{384,320},{448,384},... | collective-permute-start | bytes 983048 | tf_op jit(solution)/shard_map/ppermute | solution.py:301
  61.4 0.0 copy-done.13
  61.4 1.9 %collective-permute-start.4 = (bf16[2,144,512]{2,1,0:T(8,128)(2,1)}, bf16[2,144,512]{2,1,0:T(8,128)(2,1)S(1)}, u32[]{:S(2)}, u32[]{:S(2)}) collective-permute-start(bf16[2,144,512]{2,1,0:T(8,128)(2,1)} %copy-done.19), channel_id=1, source_target_pairs={{1,0},{2,1},{3,2},{4,3},{5,4},{6,5},{7,6},{8,7},{9,8},{10,9},{11,1... | collective-permute-start | bytes 884744 | tf_op jit(solution)/shard_map/ppermute | solution.py:291
  63.3 6.6 %collective-permute-done.4.from_right_ref = bf16[2,144,512]{2,1,0:T(8,128)(2,1)S(1)} collective-permute-done((bf16[2,144,512]{2,1,0:T(8,128)(2,1)}, bf16[2,144,512]{2,1,0:T(8,128)(2,1)S(1)}, u32[]{:S(2)}, u32[]{:S(2)}) %collective-permute-start.4) | collective-permute-done | bytes 294944 | tf_op jit(solution)/shard_map/ppermute | solution.py:291
  69.9 0.0 collective-permute-done.5.from_left_ref
  69.9 1.0 copy-done.12
  70.9 1.8 %shard_map.114 = (bf16[3,144,512]{2,1,0:T(8,128)(2,1)}, bf16[144,512]{1,0:T(8,128)(2,1)S(1)}) custom-call(bf16[144,512]{1,0:T(8,128)(2,1)S(1)} %bitcast.24, bf16[144,512]{1,0:T(8,128)(2,1)S(1)} %copy-done.12, bf16[2,144,512]{2,1,0:T(8,128)(2,1)S(1)} %collective-permute-done.4.from_right_ref, bf16[3,144,512]{2,1,0:T(8,128)(2,1)} %collective-permute-done.5.from_left_ref), custom_call_target="tpu_custom_call" | custom-call | flops 1000000 | bytes 2000000 | tf_op jit(solution)/shard_map/pallas_call | solution.py:293
  72.7 0.7 copy-done.20
  73.4 4.1 %collective-permute-start.6 = (bf16[3,144,512]{2,1,0:T(8,128)(2,1)}, bf16[3,144,512]{2,1,0:T(8,128)(2,1)}, u32[]{:S(2)}, u32[]{:S(2)}) collective-permute-start(bf16[3,144,512]{2,1,0:T(8,128)(2,1)} %get-tuple-element.19), channel_id=1, source_target_pairs={{16,0},{32,16},{48,32},{64,48},{80,64},{96,80},{112,96},{128,112},... | collective-permute-start | bytes 1327112 | tf_op jit(solution)/shard_map/ppermute | solution.py:296
  77.5 0.0 collective-permute-done.up_ref
  77.5 0.0 collective-permute-done.1.down_ref
  77.5 0.0 copy-done.2
  77.5 0.0 collective-permute-done.3.across_ref
  77.5 4.9 %shard_map.112 = bf16[8,128,128]{2,1,0:T(8,128)(2,1)S(1)} custom-call(s32[1]{0:T(128)} %bitcast.me_ref, s32[8,128]{1,0:T(8,128)S(1)} %get-tuple-element.13.lists_ref, bf16[4,160,256]{2,1,0:T(8,128)(2,1)S(1)} %collective-permute-done.up_ref, bf16[4,160,256]{2,1,0:T(8,128)(2,1)S(1)} %bitcast.28, bf16[4,160,256]{2,1,0:T(8,128)(2,1)S(1)} %collective-permute-done.1.down_ref, ...), custom_call_target="tpu_custom_call" | custom-call | flops 600000000 | bytes 4000000 | tf_op jit(solution)/shard_map/pallas_call | solution.py:312
  82.5 0.0 copy-start.4
  82.5 0.7 copy-done.4
  83.2 3.4 %all-to-all-start.1 = ((bf16[8,128,128]{2,1,0:T(8,128)(2,1)}), bf16[8,128,128]{2,1,0:T(8,128)(2,1)S(1)}, u32[]{:S(2)}, u32[]{:S(2)}) async-start(bf16[8,128,128]{2,1,0:T(8,128)(2,1)} %copy-done.4), calls=%async_computation.1 | async-start | bytes 524288 | tf_op jit(solution)/shard_map/all_to_all | solution.py:325
  86.5 2.5 %collective-permute-start.7 = (bf16[144,512]{1,0:T(8,128)(2,1)}, bf16[144,512]{1,0:T(8,128)(2,1)S(1)}, u32[]{:S(2)}, u32[]{:S(2)}) collective-permute-start(bf16[144,512]{1,0:T(8,128)(2,1)} %copy-done.20), channel_id=1, source_target_pairs={{0,16},{16,32},{32,48},{48,64},{64,80},{80,96},{96,112},{112,128},... | collective-permute-start | bytes 442376 | tf_op jit(solution)/shard_map/ppermute | solution.py:297
  89.1 8.2 %collective-permute-done.7.sunk_ref = bf16[144,512]{1,0:T(8,128)(2,1)S(1)} collective-permute-done((bf16[144,512]{1,0:T(8,128)(2,1)}, bf16[144,512]{1,0:T(8,128)(2,1)S(1)}, u32[]{:S(2)}, u32[]{:S(2)}) %collective-permute-start.7) | collective-permute-done | bytes 147488 | tf_op jit(solution)/shard_map/ppermute | solution.py:297
  97.2 0.0 collective-permute-done.6.risen_ref
  97.2 1.0 copy-done.3
  98.2 1.0 copy-done.7
  99.2 2.1 %shard_map.115.near_ref = f32[144,512]{1,0:T(8,128)S(1)} custom-call(s32[1]{0:T(128)} %bitcast.me_ref, s32[1,4]{1,0:T(1,128)S(1)} %bitcast.38, bf16[144,512]{1,0:T(8,128)(2,1)S(1)} %bitcast.25, bf16[512,512]{1,0:T(8,128)(2,1)S(1)} %bitcast.32, bf16[4,512,512]{2,1,0:T(8,128)(2,1)S(1)} %bitcast.21, bf16[2,144,512]{2,1,0:T(8,128)(2,1)S(1)} %copy-done.3, ...), custom_call_target="tpu_custom_call" | custom-call | flops 400000000 | bytes 4000000 | tf_op jit(solution)/shard_map/pallas_call | solution.py:303
  101.4 0.0 all-to-all-done.1.got_ref
  101.4 0.0 copy-start.9
  101.4 0.9 copy-done.9
  102.3 0.9 copy-done.14
  103.2 1.3 %shard_map.116 = bf16[144,512]{1,0:T(8,128)(2,1)} custom-call(s32[1]{0:T(128)} %bitcast.me_ref, bf16[8,128,128]{2,1,0:T(8,128)(2,1)S(1)} %all-to-all-done.1.got_ref, bf16[160,160]{1,0:T(8,128)(2,1)S(1)} %copy-done.14, bf16[160,160]{1,0:T(8,128)(2,1)S(1)} %bitcast.34, bf16[160,512]{1,0:T(8,128)(2,1)S(1)} %bitcast.30, f32[144,512]{1,0:T(8,128)S(1)} %shard_map.115.near_ref), custom_call_target="tpu_custom_call" | custom-call | flops 50000000 | bytes 1000000 | tf_op jit(solution)/shard_map/pallas_call | solution.py:326
  (8 shorter events, 0.0 us)
Async XLA Ops:
  0.0 5.5 %copy-start.1 = (bf16[1,1,512,144]{2,3,1,0:T(8,128)(2,1)S(1)}, bf16[1,1,512,144]{2,3,1,0:T(8,128)(2,1)}, u32[]{:S(2)}) copy-start(bf16[1,1,512,144]{2,3,1,0:T(8,128)(2,1)} %param.11) | copy-start | bytes 442372
  0.0 5.6 %copy-start.5 = (bf16[1,1,512,160]{2,3,1,0:T(8,128)(2,1)S(1)}, bf16[1,1,512,160]{2,3,1,0:T(8,128)(2,1)}, u32[]{:S(2)}) copy-start(bf16[1,1,512,160]{2,3,1,0:T(8,128)(2,1)} %param.15) | copy-start | bytes 491524
  0.0 1.1 %copy-start.6 = (bf16[1,1,7,160,160]{4,3,2,1,0:T(8,128)(2,1)S(1)}, bf16[1,1,7,160,160]{4,3,2,1,0:T(8,128)(2,1)}, u32[]{:S(2)}) copy-start(bf16[1,1,7,160,160]{4,3,2,1,0:T(8,128)(2,1)} %param.18) | copy-start | bytes 1075204
  1.1 1.0 copy-start.10
  2.1 3.5 %copy-start.8 = (bf16[1,1,160,160]{3,2,1,0:T(8,128)(2,1)S(1)}, bf16[1,1,160,160]{3,2,1,0:T(8,128)(2,1)}, u32[]{:S(2)}) copy-start(bf16[1,1,160,160]{3,2,1,0:T(8,128)(2,1)} %param.16) | copy-start | bytes 153604
  2.1 3.5 %copy-start.15 = (bf16[1,1,40,160]{3,2,1,0:T(8,128)(2,1)S(1)}, bf16[1,1,40,160]{3,2,1,0:T(8,128)(2,1)}, u32[]{:S(2)}) copy-start(bf16[1,1,40,160]{3,2,1,0:T(8,128)(2,1)} %param.17) | copy-start | bytes 38404
  2.1 3.5 %copy-start.17 = (s32[1,1,7]{2,1,0:T(1,128)S(1)}, s32[1,1,7]{2,1,0:T(1,128)}, u32[]{:S(2)}) copy-start(s32[1,1,7]{2,1,0:T(1,128)} %param.20) | copy-start | bytes 88
  2.1 3.5 %copy-start.18 = (s32[1,1,4]{2,1,0:T(1,128)S(1)}, s32[1,1,4]{2,1,0:T(1,128)}, u32[]{:S(2)}) copy-start(s32[1,1,4]{2,1,0:T(1,128)} %param.21) | copy-start | bytes 52
  2.4 17.0 %collective-permute-start.2 = (bf16[11,200,128]{2,1,0:T(8,128)(2,1)S(1)}, bf16[11,200,128]{2,1,0:T(8,128)(2,1)S(1)}, u32[]{:S(2)}, u32[]{:S(2)}) collective-permute-start(bf16[11,200,128]{2,1,0:T(8,128)(2,1)S(1)} %shard_map.111.own_ref), channel_id=1, source_target_pairs={{0,16},{16,0},{1,17},{17,1},{2,18},{18,2},{3,19},{19,3},{4,20},{20... | collective-permute-start | bytes 1689608 | tf_op jit(solution)/shard_map/ppermute | solution.py:278
  7.0 26.6 %all-to-all-start = ((bf16[16,128,128]{2,1,0:T(8,128)(2,1)}), bf16[16,128,128]{2,1,0:T(8,128)(2,1)}, u32[]{:S(2)}, u32[]{:S(2)}) async-start(bf16[16,128,128]{2,1,0:T(8,128)(2,1)} %shard_map.109), calls=%async_computation | async-start | bytes 1048576 | tf_op jit(solution)/shard_map/all_to_all | solution.py:260
  13.7 12.7 %copy-start = (bf16[1,1,4,512,512]{4,3,2,1,0:T(8,128)(2,1)S(1)}, bf16[1,1,4,512,512]{4,3,2,1,0:T(8,128)(2,1)}, u32[]{:S(2)}) copy-start(bf16[1,1,4,512,512]{4,3,2,1,0:T(8,128)(2,1)} %param.13) | copy-start | bytes 6291460
  13.8 12.7 %copy-start.16 = (s32[1,1,4]{2,1,0:T(1,128)S(1)}, s32[1,1,4]{2,1,0:T(1,128)}, u32[]{:S(2)}) copy-start(s32[1,1,4]{2,1,0:T(1,128)} %param.14) | copy-start | bytes 52
  20.5 57.0 %collective-permute-start.3 = (bf16[22,200,128]{2,1,0:T(8,128)(2,1)}, bf16[22,200,128]{2,1,0:T(8,128)(2,1)}, u32[]{:S(2)}, u32[]{:S(2)}) collective-permute-start(bf16[22,200,128]{2,1,0:T(8,128)(2,1)} %pad_maximum_fusion), channel_id=1, source_target_pairs={{0,1},{1,0},{2,3},{3,2},{4,5},{5,4},{6,7},{7,6},{8,9},{9,8},{10,11... | collective-permute-start | bytes 3379208 | tf_op jit(solution)/shard_map/ppermute | solution.py:279
  28.3 0.7 copy-start.11
  28.9 0.7 copy-start.19
  29.7 40.2 %collective-permute-start.5 = (bf16[3,144,512]{2,1,0:T(8,128)(2,1)}, bf16[3,144,512]{2,1,0:T(8,128)(2,1)}, u32[]{:S(2)}, u32[]{:S(2)}) collective-permute-start(bf16[3,144,512]{2,1,0:T(8,128)(2,1)} %get-tuple-element.17), channel_id=1, source_target_pairs={{0,1},{1,2},{2,3},{3,4},{4,5},{5,6},{6,7},{7,8},{8,9},{9,10},{10,1... | collective-permute-start | bytes 1327112 | tf_op jit(solution)/shard_map/ppermute | solution.py:292
  35.1 26.3 %copy-start.13 = (bf16[160,160]{1,0:T(8,128)(2,1)}, bf16[160,160]{1,0:T(8,128)(2,1)S(1)}, u32[]{:S(2)}) copy-start(bf16[160,160]{1,0:T(8,128)(2,1)S(1)} %get-tuple-element.15.level_ref) | copy-start | bytes 153604
  54.9 22.6 %collective-permute-start = (bf16[4,160,256]{2,1,0:T(8,128)(2,1)S(1)}, bf16[4,160,256]{2,1,0:T(8,128)(2,1)S(1)}, u32[]{:S(2)}, u32[]{:S(2)}) collective-permute-start(bf16[4,160,256]{2,1,0:T(8,128)(2,1)S(1)} %bitcast.26), channel_id=1, source_target_pairs={{0,64},{64,128},{128,192},{192,256},{256,320},{320,384},{384,448},... | collective-permute-start | bytes 983048 | tf_op jit(solution)/shard_map/ppermute | solution.py:300
  57.1 20.3 %collective-permute-start.1 = (bf16[4,160,256]{2,1,0:T(8,128)(2,1)S(1)}, bf16[4,160,256]{2,1,0:T(8,128)(2,1)S(1)}, u32[]{:S(2)}, u32[]{:S(2)}) collective-permute-start(bf16[4,160,256]{2,1,0:T(8,128)(2,1)S(1)} %bitcast.27), channel_id=1, source_target_pairs={{64,0},{128,64},{192,128},{256,192},{320,256},{384,320},{448,384},... | collective-permute-start | bytes 983048 | tf_op jit(solution)/shard_map/ppermute | solution.py:301
  61.4 8.5 %collective-permute-start.4 = (bf16[2,144,512]{2,1,0:T(8,128)(2,1)}, bf16[2,144,512]{2,1,0:T(8,128)(2,1)S(1)}, u32[]{:S(2)}, u32[]{:S(2)}) collective-permute-start(bf16[2,144,512]{2,1,0:T(8,128)(2,1)} %copy-done.19), channel_id=1, source_target_pairs={{1,0},{2,1},{3,2},{4,3},{5,4},{6,5},{7,6},{8,7},{9,8},{10,9},{11,1... | collective-permute-start | bytes 884744 | tf_op jit(solution)/shard_map/ppermute | solution.py:291
  69.9 7.6 %copy-start.2 = (bf16[2,144,512]{2,1,0:T(8,128)(2,1)}, bf16[2,144,512]{2,1,0:T(8,128)(2,1)S(1)}, u32[]{:S(2)}) copy-start(bf16[2,144,512]{2,1,0:T(8,128)(2,1)S(1)} %collective-permute-done.4.from_right_ref) | copy-start | bytes 884740
  69.9 1.0 copy-start.12
  72.7 0.7 copy-start.20
  73.4 23.8 %collective-permute-start.6 = (bf16[3,144,512]{2,1,0:T(8,128)(2,1)}, bf16[3,144,512]{2,1,0:T(8,128)(2,1)}, u32[]{:S(2)}, u32[]{:S(2)}) collective-permute-start(bf16[3,144,512]{2,1,0:T(8,128)(2,1)} %get-tuple-element.19), channel_id=1, source_target_pairs={{16,0},{32,16},{48,32},{64,48},{80,64},{96,80},{112,96},{128,112},... | collective-permute-start | bytes 1327112 | tf_op jit(solution)/shard_map/ppermute | solution.py:296
  82.5 0.7 copy-start.4
  83.2 18.2 %all-to-all-start.1 = ((bf16[8,128,128]{2,1,0:T(8,128)(2,1)}), bf16[8,128,128]{2,1,0:T(8,128)(2,1)S(1)}, u32[]{:S(2)}, u32[]{:S(2)}) async-start(bf16[8,128,128]{2,1,0:T(8,128)(2,1)} %copy-done.4), calls=%async_computation.1 | async-start | bytes 524288 | tf_op jit(solution)/shard_map/all_to_all | solution.py:325
  86.5 10.7 %collective-permute-start.7 = (bf16[144,512]{1,0:T(8,128)(2,1)}, bf16[144,512]{1,0:T(8,128)(2,1)S(1)}, u32[]{:S(2)}, u32[]{:S(2)}) collective-permute-start(bf16[144,512]{1,0:T(8,128)(2,1)} %copy-done.20), channel_id=1, source_target_pairs={{0,16},{16,32},{32,48},{48,64},{64,80},{80,96},{96,112},{112,128},... | collective-permute-start | bytes 442376 | tf_op jit(solution)/shard_map/ppermute | solution.py:297
  97.2 1.0 copy-start.3
  98.2 1.0 copy-start.7
  101.4 0.9 copy-start.9
  102.3 0.9 copy-start.14

commit v2 on v1

v2 whole, which is shorter than its diff:
```python
import functools

import jax
import jax.numpy as jnp
from jax import lax
from jax.experimental import pallas as pl
from jax.experimental.pallas import tpu as pltpu
from jax.sharding import Mesh, PartitionSpec as P

AXES = ("y", "xh", "xl", "zh", "zl", "c")
F32, BF16, I32 = jnp.float32, jnp.bfloat16, jnp.int32
RANK, CHUNK, PAD = 160, 36, 40
SLOTS = (7, 4)
VMEM = pl.BlockSpec(memory_space=pltpu.VMEM)
SMEM = pl.BlockSpec(memory_space=pltpu.SMEM)
ANY = pl.BlockSpec(memory_space=pl.ANY)
SLABS = 8


class Stage:
    def __init__(self, body, outs, scratch, args, lists=(), scalars=(), repeats=None):
        self.body, self.outs, self.scratch, self.args = body, outs, scratch, list(args)
        self.lists, self.scalars, self.repeats = list(lists), list(scalars), repeats or {}
        self.ready = [
            shape(max(self.repeats[o]) + 1, *out.shape[1:], dtype=out.dtype) if o in self.repeats else out
            for o, out in enumerate(outs)
        ]


def fused(*stages, flops=10**8, limit=60):
    shared = []

    def index(array):
        for i, held in enumerate(shared):
            if held is array:
                return i
        shared.append(array)
        return len(shared) - 1

    uses = [[index(a) for a in stage.args] for stage in stages]
    lists = [a for stage in stages for a in stage.lists]
    scalars = [a for stage in stages for a in stage.scalars]
    outs = [o for stage in stages for o in stage.outs]
    ready = [o for stage in stages for o in stage.ready]
    n_copies = sum(len(stage.repeats.get(o, (0,))) for stage in stages for o in range(len(stage.outs)))

    def run(*refs):
        refs = list(refs)

        def take(n):
            taken = refs[:n]
            del refs[:n]
            return taken

        ins, tables, plain, results = take(len(shared)), take(len(lists)), take(len(scalars)), take(len(outs))
        held, read, buffers, in_sems, out_sems = take(len(shared)), take(len(lists)), take(len(outs)), *take(2)
        fetch = [
            pltpu.make_async_copy(source, target, in_sems.at[i])
            for i, (source, target) in enumerate(zip(ins + tables, held + read))
        ]
        for copy in fetch:
            copy.start()
        for copy in fetch[len(shared) :]:
            copy.wait()
        arrived, leaving = set(), []
        for stage, use in zip(stages, uses):
            for i in use:
                if i not in arrived:
                    fetch[i].wait()
                    arrived.add(i)
            mine = [buffers.pop(0) for _ in stage.outs]
            targets = [results.pop(0) for _ in stage.outs]
            heads = [plain.pop(0) for _ in stage.scalars] + [read.pop(0) for _ in stage.lists]
            stage.body(*heads, *[held[i] for i in use], *mine, *take(len(stage.scratch)))
            for o in range(len(stage.outs)):
                pairs = [(mine[o], targets[o])]
                if o in stage.repeats:
                    pairs = [(mine[o].at[part], targets[o].at[d]) for d, part in enumerate(stage.repeats[o])]
                for source, target in pairs:
                    leaving.append(pltpu.make_async_copy(source, target, out_sems.at[len(leaving)]))
                    leaving[-1].start()
        for copy in leaving:
            copy.wait()

    buffers = [pltpu.VMEM(a.shape, a.dtype) for a in shared]
    buffers += [pltpu.SMEM(a.shape, a.dtype) for a in lists]
    buffers += [pltpu.VMEM(a.shape, a.dtype) for a in ready]
    buffers += [pltpu.SemaphoreType.DMA((len(shared) + len(lists),)), pltpu.SemaphoreType.DMA((n_copies,))]
    moved = sum(a.size * a.dtype.itemsize for a in [*shared, *outs])
    return pl.pallas_call(
        run,
        out_shape=outs,
        in_specs=[ANY] * (len(shared) + len(lists)) + [SMEM] * len(scalars),
        out_specs=[ANY] * len(outs),
        scratch_shapes=buffers + [b for stage in stages for b in stage.scratch],
        compiler_params=pltpu.CompilerParams(vmem_limit_bytes=limit * 2**20),
        cost_estimate=pl.CostEstimate(flops=flops, bytes_accessed=moved, transcendentals=0),
    )(*shared, *lists, *scalars)


def call(body, outs, scratch, specs, flops, moved):
    return pl.pallas_call(
        body,
        out_shape=outs,
        in_specs=specs,
        out_specs=jax.tree.map(lambda _: VMEM, outs),
        scratch_shapes=scratch,
        compiler_params=pltpu.CompilerParams(vmem_limit_bytes=16 * 2**20),
        cost_estimate=pl.CostEstimate(flops=flops, bytes_accessed=moved, transcendentals=0),
    )


def after(value, *others):
    return lax.optimization_barrier((value, *others))[0]


def shape(*dims, dtype=BF16):
    return jax.ShapeDtypeStruct(dims, dtype)


def mul(a, b):
    return lax.dot_general(a, b, (((1,), (0,)), ((), ())), preferred_element_type=F32)


def mul_t(a, b):
    return lax.dot_general(a, b, (((1,), (1,)), ((), ())), preferred_element_type=F32)


def spreader(groups, cols, transposed=False):
    dims = (cols, groups * PAD) if transposed else (groups * PAD, cols)
    padded = lax.broadcasted_iota(I32, dims, 1 if transposed else 0)
    dense = lax.broadcasted_iota(I32, dims, 0 if transposed else 1)
    hit = jnp.zeros(dims, jnp.bool_)
    for g in range(groups):
        inside = (padded >= PAD * g) & (padded < PAD * g + CHUNK)
        hit = hit | (inside & (dense == padded - (PAD - CHUNK) * g))
    return jnp.where(hit, 1.0, 0.0).astype(BF16)


def packed(a, b, tail, wide):
    wide[0, :, :RANK] = a
    wide[1, :, :RANK] = b
    rest = wide[0, :, 128:] + pltpu.roll(wide[1, :, 128:], 32, 1)
    return jnp.concatenate([wide[0, :, :128], wide[1, :, :128], rest, tail], axis=0).astype(BF16)


def up_body(far_one_ref, far_two_ref, x_ref, basis_ref, one_ref, two_ref, out_ref, wide):
    wide[...] = jnp.zeros_like(wide)
    row = lax.broadcasted_iota(I32, (8, 128), 0)
    lane = lax.broadcasted_iota(I32, (8, 128), 1)
    tail = jnp.full((8, 128), -1.0, F32)
    for r, ref in enumerate((far_one_ref, far_two_ref)):
        for k in range(SLOTS[r]):
            tail = jnp.where((row == r) & (lane == k), ref[0, k].astype(F32), tail)
    leaf = mul_t(x_ref[...], basis_ref[...]).astype(BF16)
    up = mul(leaf, one_ref[...]).astype(BF16)
    chunks = mul(spreader(4, 144), up)
    quarter = two_ref[...].astype(F32)
    for q in range(4):
        out_ref[q] = packed(chunks[PAD * q : PAD * (q + 1)], quarter, tail, wide)


def merge_body(me_ref, got_ref, window_ref, level_ref, lists_ref, wide, levels):
    me = me_ref[0]
    own = (me // 32) % 2 * 2 + me // 2 % 2
    lane = lax.broadcasted_iota(I32, (PAD, 128), 1)
    rests = [jnp.zeros((PAD, 128), F32)] * 2

    def deposit(level, place, main, rest):
        window_ref[0, 5 * level + place] = main.astype(BF16)
        rest = jnp.where(lane < 32, rest, 0.0)
        rests[level] = rests[level] + (pltpu.roll(rest, 32 * place, 1) if place else rest)

    for xh in range(2):
        second = jnp.zeros((PAD, RANK), F32)
        for zl in range(2):
            main = jnp.zeros((PAD, 128), F32)
            rest = jnp.zeros((PAD, 128), F32)
            for q in range(4):
                block = got_ref[xh * 8 + (q // 2) * 4 + zl * 2 + q % 2].astype(F32)
                main += block[:PAD]
                rest += block[2 * PAD : 3 * PAD]
                rows = slice(PAD * q, PAD * (q + 1))
                levels[xh * 2 + zl, rows, :128] = block[PAD : 2 * PAD]
                levels[xh * 2 + zl, rows, 128:] = pltpu.roll(block[2 * PAD : 3 * PAD], 96, 1)
            wide[:, :128] = main
            wide[:, 128:] = rest
            first = wide[:, :RANK]
            deposit(0, xh * 2 + zl, main, rest)
            second += mul(first.astype(BF16), levels[xh * 2 + zl, :, :RANK].astype(BF16))
        wide[:, :RANK] = second
        deposit(1, xh, wide[:, :128], wide[:, 128:])
    window_ref[0, 4] = rests[0].astype(BF16)
    window_ref[0, 7] = rests[1].astype(BF16)
    level_ref[...] = levels[own, :, :RANK].astype(BF16)
    for q in range(4):
        place = (me // 32) % 2 * 8 + (q // 2) * 4 + me // 2 % 2 * 2 + q % 2
        tail = got_ref[place, 112:, :].astype(F32)
        lists_ref[q : q + 1, :] = tail[8:9].astype(I32)
        lists_ref[4 + q : 5 + q, :] = tail[9:10].astype(I32)


def pack_body(one_ref, two_ref, out_ref, wide):
    wide[...] = jnp.zeros_like(wide)
    for g in range(3):
        rest = jnp.zeros((RANK, 128), F32)
        for s in range(4):
            lanes = slice(128 * s, 128 * (s + 1))
            if 4 * g + s == SLOTS[0]:
                out_ref[g, :, lanes] = jnp.zeros((RANK, 128), BF16)
                continue
            block = one_ref[4 * g + s] if g < 2 else two_ref[s]
            out_ref[g, :, lanes] = block[:, :128]
            wide[:, :32] = block[:, 128:].astype(F32)
            rest += wide[...] if s == 0 else pltpu.roll(wide[...], 32 * s, 1)
        out_ref[g, :, 512:] = rest.astype(BF16)


def couple_body(me_ref, lists_ref, up_ref, mid_ref, down_ref, own_ref, beside_ref, across_ref, opposite_ref, out_ref, rows, stack, wide):
    me = me_ref[0]
    y = me // 64
    q_own = me // 16 % 2 * 2 + me % 2
    rows[0] = up_ref[...]
    rows[1] = mid_ref[...]
    rows[2] = down_ref[...]
    lane = lax.broadcasted_iota(I32, (PAD, 128), 1)
    sources = ((own_ref, q_own), (beside_ref, q_own ^ 2), (across_ref, q_own ^ 1), (opposite_ref, q_own ^ 3))
    totals = [jnp.zeros((PAD, RANK), F32)] * 2
    for g in range(3):
        level = g // 2
        for which, (ref, q) in enumerate(sources):
            rest = jnp.zeros((PAD, 128), F32)
            for s in range(4):
                if 4 * g + s == SLOTS[0]:
                    stack[which, g, :, 128 * s : 128 * (s + 1)] = jnp.zeros((PAD, 128), BF16)
                    continue
                code = lists_ref[4 + q, s] if level else lists_ref[q, 4 * g + s]
                valid = code >= 0
                safe = jnp.where(valid, code, y * (8 if level else 16))
                row, col = (safe // 4, safe % 4) if level else (safe // 8, safe % 8)
                zh, place = (col, row % 2) if level else (col // 2, row % 2 * 2 + col % 2)
                plane = row // 2 - y + 1
                main = rows[plane, zh, 5 * level + place].astype(F32)
                stack[which, g, :, 128 * s : 128 * (s + 1)] = jnp.where(valid, main, 0.0).astype(BF16)
                turned = pltpu.roll(rows[plane, zh, 4 + 3 * level].astype(F32), (s + 4 - place) % 4 * 32, 1)
                inside = (lane >= 32 * s) & (lane < jnp.where(valid, 32 * (s + 1), 0))
                rest = jnp.where(inside, turned, rest)
            stack[which, g, :, 512:] = rest.astype(BF16)
            totals[level] = totals[level] + mul_t(stack[which, g], ref[g])
    wide[...] = jnp.zeros_like(wide)
    block = packed(totals[0], totals[1], jnp.zeros((8, 128), F32), wide)
    for d in range(8):
        out_ref[d] = block


def down_body(me_ref, got_ref, level_ref, one_ref, basis_ref, near_ref, out_ref, wide, local):
    me = me_ref[0]
    zl_own = me // 2 % 2
    for q in range(4):
        base = q // 2 * 4 + q % 2
        mine = got_ref[base + zl_own * 2].astype(F32)
        both = got_ref[base].astype(F32) + got_ref[base + 2].astype(F32)
        wide[:, :128] = both[PAD : 2 * PAD]
        wide[:, 128:] = pltpu.roll(both[2 * PAD : 3 * PAD], 96, 1)
        second = wide[:, :RANK].astype(BF16)
        wide[:, :128] = mine[:PAD]
        wide[:, 128:] = mine[2 * PAD : 3 * PAD]
        local[PAD * q : PAD * (q + 1), :] = wide[:, :RANK] + mul_t(second, level_ref[...])
    one = mul(spreader(4, 144, True), local[...].astype(BF16)).astype(BF16)
    leaf = mul_t(one, one_ref[...]).astype(BF16)
    out_ref[...] = (near_ref[...] + mul(leaf, basis_ref[...])).astype(BF16)


def slot_of(list_ref, me, apart):
    found = jnp.int32(0)
    for k in range(1, 4):
        found = jnp.where(list_ref[0, k] == me + apart, k, found)
    return found


def mirror_body(me_ref, list_ref, x_ref, blocks_ref, left_ref, right_ref, below_ref):
    me = me_ref[0]
    x = x_ref[...]
    left_ref[0] = x
    right_ref[0] = x
    right_ref[1] = mul(x, blocks_ref[slot_of(list_ref, me, 1)]).astype(BF16)
    left_ref[1] = mul(x, blocks_ref[slot_of(list_ref, me, 15)]).astype(BF16)
    below_ref[...] = mul(x, blocks_ref[slot_of(list_ref, me, 16)]).astype(BF16)
    right_ref[2] = mul(x, blocks_ref[slot_of(list_ref, me, 17)]).astype(BF16)


def turn_body(x_ref, below_ref, from_right_ref, from_left_ref, rise_ref, sink_ref):
    rise_ref[0] = from_left_ref[0]
    rise_ref[1] = x_ref[...]
    rise_ref[2] = from_right_ref[0]
    sink_ref[...] = (
        below_ref[...].astype(F32) + from_left_ref[2].astype(F32) + from_right_ref[1].astype(F32)
    ).astype(BF16)


def near_body(me_ref, list_ref, x_ref, self_ref, blocks_ref, from_right_ref, from_left_ref, risen_ref, sunk_ref, out_ref):
    me = me_ref[0]
    total = mul_t(x_ref[...], self_ref[...])
    total += mul_t(from_right_ref[0], blocks_ref[slot_of(list_ref, me, 1)])
    total += mul_t(risen_ref[0], blocks_ref[slot_of(list_ref, me, 15)])
    total += mul_t(risen_ref[1], blocks_ref[slot_of(list_ref, me, 16)])
    total += mul_t(risen_ref[2], blocks_ref[slot_of(list_ref, me, 17)])
    out_ref[...] = total + from_left_ref[1].astype(F32) + sunk_ref[...].astype(F32)


def shards(
    right_sides,
    near_self,
    near_blocks,
    near_list,
    basis,
    transfer_one,
    transfer_two,
    couple_one,
    couple_two,
    far_list_one,
    far_list_two,
):
    me = lax.axis_index(AXES).astype(I32).reshape(1)
    x = right_sides[0, 0].T
    vectors = basis[0, 0].T
    one = transfer_one[0, 0]
    blocks = near_blocks[0, 0]
    links = near_list[0]

    across_gy = ("zh", "zl", "c")
    along_gx = ("y", "xh", "xl")
    swap = [(0, 1), (1, 0)]

    message, left, right, below, own = fused(
        Stage(
            up_body,
            [shape(16, 128, 128)],
            [pltpu.VMEM((2, PAD, 256), F32)],
            [x, vectors, one, transfer_two[0, 0]],
            lists=[far_list_one[0], far_list_two[0]],
            repeats={0: [d // 4 % 2 * 2 + d % 2 for d in range(16)]},
        ),
        Stage(
            mirror_body,
            [shape(2, 144, 512), shape(3, 144, 512), shape(144, 512)],
            [],
            [x, blocks],
            lists=[links],
            scalars=[me],
        ),
        Stage(
            pack_body, [shape(3, RANK, 640)], [pltpu.VMEM((RANK, 128), F32)], [couple_one[0, 0], couple_two[0, 0]]
        ),
        flops=4 * 10**8,
    )
    got = lax.all_to_all(message, ("xh", "xl", "zl", "c"), 0, 0)
    from_right = lax.ppermute(left, across_gy, [(i + 1, i) for i in range(15)])
    from_left = lax.ppermute(right, across_gy, [(i, i + 1) for i in range(15)])
    beside = lax.ppermute(own, "xl", swap)
    across = lax.ppermute(own, "c", swap)
    got, across = lax.optimization_barrier((got, across))
    window, level, codes, rise, sink = fused(
        Stage(
            merge_body,
            [shape(4, SLABS, PAD, 128), shape(RANK, RANK), shape(8, 128, dtype=I32)],
            [pltpu.VMEM((PAD, 256), F32), pltpu.VMEM((4, RANK, 256), F32)],
            [got],
            scalars=[me],
            repeats={0: [0] * 4},
        ),
        Stage(
            turn_body, [shape(3, 144, 512), shape(144, 512)], [], [x, below, from_right, from_left]
        ),
    )
    plane = lax.all_to_all(window, "zh", 0, 0)
    risen = lax.ppermute(rise, along_gx, [(i + 1, i) for i in range(31)])
    sunk = lax.ppermute(sink, along_gx, [(i, i + 1) for i in range(31)])

    plane, beside, risen, sunk = lax.optimization_barrier((plane, beside, risen, sunk))
    opposite = lax.ppermute(beside, "c", swap)
    above = lax.ppermute(plane, "y", [(i, i + 1) for i in range(7)])
    under = lax.ppermute(plane, "y", [(i + 1, i) for i in range(7)])
    near = call(
        near_body, shape(144, 512, dtype=F32), [], [SMEM, SMEM] + [VMEM] * 7, 4 * 10**8, 4 * 10**6
    )(me, links, x, near_self[0, 0], blocks, from_right, from_left, risen, sunk)
    codes = after(codes, near)
    partial = call(
        couple_body,
        shape(8, 128, 128),
        [
            pltpu.VMEM((3, 4, SLABS, PAD, 128), BF16),
            pltpu.VMEM((4, 3, PAD, 640), BF16),
            pltpu.VMEM((2, PAD, 256), F32),
        ],
        [SMEM, SMEM] + [VMEM] * 7,
        6 * 10**8,
        4 * 10**6,
    )(me, codes, above, plane, under, own, beside, across, opposite)
    sums = lax.all_to_all(partial, ("xl", "zl", "c"), 0, 0)
    applied = call(
        down_body,
        shape(144, 512),
        [pltpu.VMEM((PAD, 256), F32), pltpu.VMEM((RANK, RANK), F32)],
        [SMEM] + [VMEM] * 5,
        10**8,
        10**6,
    )(me, sums, level, one, vectors, near)
    return applied.T[None, None]


def solution(mesh):
    split = Mesh(mesh.devices.reshape(8, 2, 2, 4, 2, 2), AXES)
    rows, cols = AXES[:3], AXES[3:]

    def spec(rank):
        return P(rows, cols, *[None] * (rank - 2))

    ranks = (4, 4, 5, 3, 4, 4, 4, 5, 5, 3, 3)
    return jax.shard_map(
        shards, mesh=split, in_specs=tuple(map(spec, ranks)), out_specs=spec(4), check_vma=False
    )
```

time: 105 us -> 87.9 us (0.84)
  the two profiles are of different devices: /device:TPU:33 before, /device:TPU:28 now
where the time goes in v2:
time: 87.9 us; the launch traced here: 87.2 us
  starting transfers between devices  43.1 us (49%)
  waiting for transfers between devices  13.7 us (16%)
  Pallas kernels  11.7 us (13%)
  blocking collectives  11.3 us (13%)
  local copies, waits for them, and re-layouts  7.06 us (8%)
    all_to_all x1, starting transfers between devices, shards(): plane = lax.all_to_all(window, 'zh', 0, 0)  13.2 us
    all_to_all x1, blocking collectives, shards(): sums = lax.all_to_all(partial, ('xl', 'zl', 'c'), 0, 0)  11.3 us
    unnamed x38, local copies, waits for them, and re-layouts  7.06 us
    all_to_all x1, starting transfers between devices, shards(): got = lax.all_to_all(message, ('xh', 'xl', 'zl', 'c'), 0, 0)  6.9 us
    pallas_call x2, Pallas kernels, fused(): pl.pallas_call(run, out_shape=outs, in_specs=[ANY] * (len(shared) + len(l...  6.25 us
    ppermute x1, waiting for transfers between devices, shards(): under = lax.ppermute(plane, 'y', [(i + 1, i) for i in range(7)])  5.33 us
    ppermute x1, waiting for transfers between devices, shards(): sunk = lax.ppermute(sink, along_gx, [(i, i + 1) for i in range(31)])  4.75 us
    ppermute x1, starting transfers between devices, shards(): above = lax.ppermute(plane, 'y', [(i, i + 1) for i in range(7)])  4.7 us
  transfers between devices with their start and end apart: 11, of which 4 were waited for; matrix products, arithmetic and copies ran while one was open for 0% of the time, Pallas kernels for 5%

profile of v2, /device:TPU:28, one launch (start us, length us, event | category | flops | bytes accessed | tf_op | source)
XLA Modules:
  0.0 87.2 jit_solution(7016198053074615842)
XLA Ops:
  0.0 3.8 %shard_map.109 = (bf16[16,128,128]{2,1,0:T(8,128)(2,1)}, bf16[2,144,512]{2,1,0:T(8,128)(2,1)}, bf16[3,144,512]{2,1,0:T(8,128)(2,1)}, bf16[144,512]{1,0:T(8,128)(2,1)}, bf16[3,160,640]{2,1,0:T(8,128)(2,1)}) custom-call(bf16[144,512]{1,0:T(8,128)(2,1)} %bitcast.21, bf16[160,512]{1,0:T(8,128)(2,1)} %bitcast.24, bf16[160,160]{1,0:T(8,128)(2,1)} %bitcast.27, ...), custom_call_target="tpu_custom_call" | custom-call | flops 400000000 | bytes 5059072 | tf_op jit(solution)/shard_map/pallas_call | solution.py:90
  3.8 0.0 copy-start
  3.8 0.0 copy-start.3
  3.8 0.0 copy-start.10
  3.8 0.0 copy-start.18
  3.9 6.9 %all-to-all-start = ((bf16[16,128,128]{2,1,0:T(8,128)(2,1)}), bf16[16,128,128]{2,1,0:T(8,128)(2,1)}, u32[]{:S(2)}, u32[]{:S(2)}) async-start(bf16[16,128,128]{2,1,0:T(8,128)(2,1)} %get-tuple-element.22), calls=%async_computation | async-start | bytes 1048576 | tf_op jit(solution)/shard_map/all_to_all | solution.py:357
  10.8 2.0 %collective-permute-start = (bf16[3,160,640]{2,1,0:T(8,128)(2,1)}, bf16[3,160,640]{2,1,0:T(8,128)(2,1)S(1)}, u32[]{:S(2)}, u32[]{:S(2)}) collective-permute-start(bf16[3,160,640]{2,1,0:T(8,128)(2,1)} %get-tuple-element.23.own_ref), channel_id=1, source_target_pairs={{0,1},{1,0},{2,3},{3,2},{4,5},{5,4},{6,7},{7,6},{8,9},{9,8},{10,11... | collective-permute-start | bytes 1843208 | tf_op jit(solution)/shard_map/ppermute | solution.py:361
  12.8 2.3 %collective-permute-start.2 = (bf16[3,144,512]{2,1,0:T(8,128)(2,1)}, bf16[3,144,512]{2,1,0:T(8,128)(2,1)S(1)}, u32[]{:S(2)}, u32[]{:S(2)}) collective-permute-start(bf16[3,144,512]{2,1,0:T(8,128)(2,1)} %get-tuple-element.27), channel_id=1, source_target_pairs={{0,1},{1,2},{2,3},{3,4},{4,5},{5,6},{6,7},{7,8},{8,9},{9,10},{10,1... | collective-permute-start | bytes 1327112 | tf_op jit(solution)/shard_map/ppermute | solution.py:359
  15.1 1.3 %collective-permute-start.1 = (bf16[2,144,512]{2,1,0:T(8,128)(2,1)}, bf16[2,144,512]{2,1,0:T(8,128)(2,1)S(1)}, u32[]{:S(2)}, u32[]{:S(2)}) collective-permute-start(bf16[2,144,512]{2,1,0:T(8,128)(2,1)} %get-tuple-element.26), channel_id=1, source_target_pairs={{1,0},{2,1},{3,2},{4,3},{5,4},{6,5},{7,6},{8,7},{9,8},{10,9},{11,1... | collective-permute-start | bytes 884744 | tf_op jit(solution)/shard_map/ppermute | solution.py:358
  16.4 3.1 %collective-permute-start.3 = (bf16[3,160,640]{2,1,0:T(8,128)(2,1)}, bf16[3,160,640]{2,1,0:T(8,128)(2,1)}, u32[]{:S(2)}, u32[]{:S(2)}) collective-permute-start(bf16[3,160,640]{2,1,0:T(8,128)(2,1)} %get-tuple-element.23.own_ref), channel_id=1, source_target_pairs={{0,16},{16,0},{1,17},{17,1},{2,18},{18,2},{3,19},{19,3},{4,20},{20... | collective-permute-start | bytes 1843208 | tf_op jit(solution)/shard_map/ppermute | solution.py:360
  19.5 0.0 collective-permute-done.across_ref
  19.5 0.0 copy-start.8
  19.5 0.8 copy-done.8
  20.3 0.0 all-to-all-done.refs_0_
  20.3 0.0 collective-permute-done.1.refs_3_.from_right_ref
  20.3 0.0 copy-start.4
  20.4 0.0 collective-permute-done.2.refs_4_.from_left_ref
  20.4 0.0 copy-start.1
  20.4 0.7 copy-done.4
  21.0 0.2 copy-done.1
  21.2 2.5 %shard_map.110 = (bf16[4,8,40,128]{3,2,1,0:T(8,128)(2,1)}, bf16[160,160]{1,0:T(8,128)(2,1)}, s32[8,128]{1,0:T(8,128)}, bf16[3,144,512]{2,1,0:T(8,128)(2,1)}, bf16[144,512]{1,0:T(8,128)(2,1)}) custom-call(bf16[16,128,128]{2,1,0:T(8,128)(2,1)} %all-to-all-done.refs_0_, bf16[144,512]{1,0:T(8,128)(2,1)} %bitcast.22, bf16[144,512]{1,0:T(8,128)(2,1)} %get-tuple-element.25.refs_2_, ...), custom_call_target="tpu_custom_call" | custom-call | flops 100000000 | bytes 2529280 | tf_op jit(solution)/shard_map/pallas_call | solution.py:90
  23.7 13.2 %all-to-all-start.1 = ((bf16[4,8,40,128]{3,2,1,0:T(8,128)(2,1)}), bf16[4,8,40,128]{3,2,1,0:T(8,128)(2,1)S(1)}, u32[]{:S(2)}, u32[]{:S(2)}) async-start(bf16[4,8,40,128]{3,2,1,0:T(8,128)(2,1)} %get-tuple-element.29), calls=%async_computation.1 | async-start | bytes 655360 | tf_op jit(solution)/shard_map/all_to_all | solution.py:376
  36.9 2.5 %collective-permute-start.4 = (bf16[3,144,512]{2,1,0:T(8,128)(2,1)}, bf16[3,144,512]{2,1,0:T(8,128)(2,1)S(1)}, u32[]{:S(2)}, u32[]{:S(2)}) collective-permute-start(bf16[3,144,512]{2,1,0:T(8,128)(2,1)} %get-tuple-element.30), channel_id=1, source_target_pairs={{16,0},{32,16},{48,32},{64,48},{80,64},{96,80},{112,96},{128,112},... | collective-permute-start | bytes 1327112 | tf_op jit(solution)/shard_map/ppermute | solution.py:377
  39.3 3.4 %collective-permute-start.5 = (bf16[144,512]{1,0:T(8,128)(2,1)}, bf16[144,512]{1,0:T(8,128)(2,1)S(1)}, u32[]{:S(2)}, u32[]{:S(2)}) collective-permute-start(bf16[144,512]{1,0:T(8,128)(2,1)} %get-tuple-element.31), channel_id=1, source_target_pairs={{0,16},{16,32},{32,48},{48,64},{64,80},{80,96},{96,112},{112,128},... | collective-permute-start | bytes 442376 | tf_op jit(solution)/shard_map/ppermute | solution.py:378
  42.7 0.0 collective-permute-done.3.beside_ref
  42.7 4.7 %collective-permute-done.5.sunk_ref = bf16[144,512]{1,0:T(8,128)(2,1)S(1)} collective-permute-done((bf16[144,512]{1,0:T(8,128)(2,1)}, bf16[144,512]{1,0:T(8,128)(2,1)S(1)}, u32[]{:S(2)}, u32[]{:S(2)}) %collective-permute-start.5) | collective-permute-done | bytes 147488 | tf_op jit(solution)/shard_map/ppermute | solution.py:378
  47.5 0.0 copy-start.14
  47.5 0.7 copy-done.14
  48.1 3.5 %collective-permute-done.4.risen_ref = bf16[3,144,512]{2,1,0:T(8,128)(2,1)S(1)} collective-permute-done((bf16[3,144,512]{2,1,0:T(8,128)(2,1)}, bf16[3,144,512]{2,1,0:T(8,128)(2,1)S(1)}, u32[]{:S(2)}, u32[]{:S(2)}) %collective-permute-start.4) | collective-permute-done | bytes 442400 | tf_op jit(solution)/shard_map/ppermute | solution.py:377
  51.6 0.0 copy-start.11
  51.6 0.8 copy-done.11
  52.4 0.0 all-to-all-done.1.mid_ref
  52.4 1.9 %collective-permute-start.8 = (bf16[3,160,640]{2,1,0:T(8,128)(2,1)}, bf16[3,160,640]{2,1,0:T(8,128)(2,1)S(1)}, u32[]{:S(2)}, u32[]{:S(2)}) collective-permute-start(bf16[3,160,640]{2,1,0:T(8,128)(2,1)} %collective-permute-done.3.beside_ref), channel_id=1, source_target_pairs={{0,1},{1,0},{2,3},{3,2},{4,5},{5,4},{6,7},{7,6},{8,9},{9,8},{10,11... | collective-permute-start | bytes 1843208 | tf_op jit(solution)/shard_map/ppermute | solution.py:381
  54.3 4.7 %collective-permute-start.6 = (bf16[4,8,40,128]{3,2,1,0:T(8,128)(2,1)S(1)}, bf16[4,8,40,128]{3,2,1,0:T(8,128)(2,1)S(1)}, u32[]{:S(2)}, u32[]{:S(2)}) collective-permute-start(bf16[4,8,40,128]{3,2,1,0:T(8,128)(2,1)S(1)} %all-to-all-done.1.mid_ref), channel_id=1, source_target_pairs={{0,64},{64,128},{128,192},{192,256},{256,320},{320,384},{384,448},... | collective-permute-start | bytes 983048 | tf_op jit(solution)/shard_map/ppermute | solution.py:382
  59.0 1.9 %collective-permute-start.7 = (bf16[4,8,40,128]{3,2,1,0:T(8,128)(2,1)S(1)}, bf16[4,8,40,128]{3,2,1,0:T(8,128)(2,1)S(1)}, u32[]{:S(2)}, u32[]{:S(2)}) collective-permute-start(bf16[4,8,40,128]{3,2,1,0:T(8,128)(2,1)S(1)} %all-to-all-done.1.mid_ref), channel_id=1, source_target_pairs={{64,0},{128,64},{192,128},{256,192},{320,256},{384,320},{448,384},... | collective-permute-start | bytes 983048 | tf_op jit(solution)/shard_map/ppermute | solution.py:383
  60.9 0.0 copy-done
  60.9 0.0 copy-done.3
  60.9 0.0 copy-done.10
  60.9 0.0 copy-done.18
  61.0 0.0 copy-start.2
  61.0 1.0 %copy-done.2 = bf16[3,144,512]{2,1,0:T(8,128)(2,1)S(1)} copy-done((bf16[3,144,512]{2,1,0:T(8,128)(2,1)S(1)}, bf16[3,144,512]{2,1,0:T(8,128)(2,1)}, u32[]{:S(2)}) %copy-start.2) | copy-done | bytes 442392
  62.0 0.0 copy-start.5
  62.0 1.0 %copy-done.5 = bf16[2,144,512]{2,1,0:T(8,128)(2,1)S(1)} copy-done((bf16[2,144,512]{2,1,0:T(8,128)(2,1)S(1)}, bf16[2,144,512]{2,1,0:T(8,128)(2,1)}, u32[]{:S(2)}) %copy-start.5) | copy-done | bytes 294936
  62.9 0.0 copy-start.12
  62.9 1.0 %copy-done.12 = bf16[3,144,512]{2,1,0:T(8,128)(2,1)S(1)} copy-done((bf16[3,144,512]{2,1,0:T(8,128)(2,1)S(1)}, bf16[3,144,512]{2,1,0:T(8,128)(2,1)}, u32[]{:S(2)}) %copy-start.12) | copy-done | bytes 442392
  63.9 0.0 copy-start.15
  63.9 0.9 %copy-done.15 = bf16[144,512]{1,0:T(8,128)(2,1)S(1)} copy-done((bf16[144,512]{1,0:T(8,128)(2,1)S(1)}, bf16[144,512]{1,0:T(8,128)(2,1)}, u32[]{:S(2)}) %copy-start.15) | copy-done | bytes 147480
  64.9 0.0 copy-start.7
  64.9 1.5 %shard_map.111.near_ref = f32[144,512]{1,0:T(8,128)S(1)} custom-call(s32[1]{0:T(128)} %bitcast.refs_10_.refs_5_.me_ref, s32[1,4]{1,0:T(1,128)S(1)} %bitcast.30, bf16[144,512]{1,0:T(8,128)(2,1)S(1)} %bitcast.23, bf16[512,512]{1,0:T(8,128)(2,1)S(1)} %bitcast.26, bf16[4,512,512]{2,1,0:T(8,128)(2,1)S(1)} %bitcast.20, bf16[2,144,512]{2,1,0:T(8,128)(2,1)S(1)} %copy-done.5, ...), custom_call_target="tpu_custom_call" | custom-call | flops 400000000 | bytes 4000000 | tf_op jit(solution)/shard_map/pallas_call | solution.py:384
  66.4 0.0 copy-start.6
  66.4 0.0 copy-start.13
  66.4 0.0 copy-start.16
  66.4 0.2 collective-permute-done.6.up_ref
  66.6 5.3 %collective-permute-done.7.down_ref = bf16[4,8,40,128]{3,2,1,0:T(8,128)(2,1)S(1)} collective-permute-done((bf16[4,8,40,128]{3,2,1,0:T(8,128)(2,1)S(1)}, bf16[4,8,40,128]{3,2,1,0:T(8,128)(2,1)S(1)}, u32[]{:S(2)}, u32[]{:S(2)}) %collective-permute-start.7) | collective-permute-done | bytes 327712 | tf_op jit(solution)/shard_map/ppermute | solution.py:383
  71.9 0.0 collective-permute-done.8.opposite_ref
  71.9 0.0 copy-done.7
  71.9 0.0 copy-done.9
  71.9 0.0 copy-done.17
  71.9 2.6 %shard_map.112 = bf16[8,128,128]{2,1,0:T(8,128)(2,1)S(1)} custom-call(s32[1]{0:T(128)} %bitcast.refs_10_.refs_5_.me_ref, s32[8,128]{1,0:T(8,128)S(1)} %copy-done.17, bf16[4,8,40,128]{3,2,1,0:T(8,128)(2,1)S(1)} %collective-permute-done.6.up_ref, bf16[4,8,40,128]{3,2,1,0:T(8,128)(2,1)S(1)} %all-to-all-done.1.mid_ref, ...), custom_call_target="tpu_custom_call" | custom-call | flops 600000000 | bytes 4000000 | tf_op jit(solution)/shard_map/pallas_call | solution.py:388
  74.5 11.3 %all_to_all.15.got_ref = bf16[8,128,128]{2,1,0:T(8,128)(2,1)S(1)} all-to-all(bf16[8,128,128]{2,1,0:T(8,128)(2,1)S(1)} %shard_map.112), channel_id=1, replica_groups=mesh['y'=8,'xh'=2,'xl'=2,'zh'=4,'zl'=2,'c'=2] {'xl','zl','c'}, dimensions={0} | all-to-all | bytes 524288 | tf_op jit(solution)/shard_map/all_to_all | solution.py:400
  85.8 0.0 copy-done.6
  85.8 0.0 copy-done.13
  85.8 0.0 copy-done.16
  85.8 1.4 %shard_map.113 = bf16[144,512]{1,0:T(8,128)(2,1)} custom-call(s32[1]{0:T(128)} %bitcast.refs_10_.refs_5_.me_ref, bf16[8,128,128]{2,1,0:T(8,128)(2,1)S(1)} %all_to_all.15.got_ref, bf16[160,160]{1,0:T(8,128)(2,1)S(1)} %copy-done.16, bf16[160,160]{1,0:T(8,128)(2,1)S(1)} %bitcast.28, bf16[160,512]{1,0:T(8,128)(2,1)S(1)} %bitcast.25, ...), custom_call_target="tpu_custom_call" | custom-call | flops 100000000 | bytes 1000000 | tf_op jit(solution)/shard_map/pallas_call | solution.py:401
  (2 shorter events, 0.0 us)
Async XLA Ops:
  3.8 57.1 %copy-start = (bf16[1,1,4,512,512]{4,3,2,1,0:T(8,128)(2,1)S(1)}, bf16[1,1,4,512,512]{4,3,2,1,0:T(8,128)(2,1)}, u32[]{:S(2)}) copy-start(bf16[1,1,4,512,512]{4,3,2,1,0:T(8,128)(2,1)} %param.13) | copy-start | bytes 6291460
  3.8 57.1 %copy-start.3 = (bf16[1,1,512,144]{2,3,1,0:T(8,128)(2,1)S(1)}, bf16[1,1,512,144]{2,3,1,0:T(8,128)(2,1)}, u32[]{:S(2)}) copy-start(bf16[1,1,512,144]{2,3,1,0:T(8,128)(2,1)} %param.11) | copy-start | bytes 442372
  3.8 57.1 %copy-start.10 = (bf16[1,1,512,512]{3,2,1,0:T(8,128)(2,1)S(1)}, bf16[1,1,512,512]{3,2,1,0:T(8,128)(2,1)}, u32[]{:S(2)}) copy-start(bf16[1,1,512,512]{3,2,1,0:T(8,128)(2,1)} %param.12) | copy-start | bytes 1572868
  3.8 57.1 %copy-start.18 = (s32[1,1,4]{2,1,0:T(1,128)S(1)}, s32[1,1,4]{2,1,0:T(1,128)}, u32[]{:S(2)}) copy-start(s32[1,1,4]{2,1,0:T(1,128)} %param.14) | copy-start | bytes 52
  3.9 16.5 %all-to-all-start = ((bf16[16,128,128]{2,1,0:T(8,128)(2,1)}), bf16[16,128,128]{2,1,0:T(8,128)(2,1)}, u32[]{:S(2)}, u32[]{:S(2)}) async-start(bf16[16,128,128]{2,1,0:T(8,128)(2,1)} %get-tuple-element.22), calls=%async_computation | async-start | bytes 1048576 | tf_op jit(solution)/shard_map/all_to_all | solution.py:357
  10.8 8.7 %collective-permute-start = (bf16[3,160,640]{2,1,0:T(8,128)(2,1)}, bf16[3,160,640]{2,1,0:T(8,128)(2,1)S(1)}, u32[]{:S(2)}, u32[]{:S(2)}) collective-permute-start(bf16[3,160,640]{2,1,0:T(8,128)(2,1)} %get-tuple-element.23.own_ref), channel_id=1, source_target_pairs={{0,1},{1,0},{2,3},{3,2},{4,5},{5,4},{6,7},{7,6},{8,9},{9,8},{10,11... | collective-permute-start | bytes 1843208 | tf_op jit(solution)/shard_map/ppermute | solution.py:361
  12.8 7.6 %collective-permute-start.2 = (bf16[3,144,512]{2,1,0:T(8,128)(2,1)}, bf16[3,144,512]{2,1,0:T(8,128)(2,1)S(1)}, u32[]{:S(2)}, u32[]{:S(2)}) collective-permute-start(bf16[3,144,512]{2,1,0:T(8,128)(2,1)} %get-tuple-element.27), channel_id=1, source_target_pairs={{0,1},{1,2},{2,3},{3,4},{4,5},{5,6},{6,7},{7,8},{8,9},{9,10},{10,1... | collective-permute-start | bytes 1327112 | tf_op jit(solution)/shard_map/ppermute | solution.py:359
  15.1 5.2 %collective-permute-start.1 = (bf16[2,144,512]{2,1,0:T(8,128)(2,1)}, bf16[2,144,512]{2,1,0:T(8,128)(2,1)S(1)}, u32[]{:S(2)}, u32[]{:S(2)}) collective-permute-start(bf16[2,144,512]{2,1,0:T(8,128)(2,1)} %get-tuple-element.26), channel_id=1, source_target_pairs={{1,0},{2,1},{3,2},{4,3},{5,4},{6,5},{7,6},{8,7},{9,8},{10,9},{11,1... | collective-permute-start | bytes 884744 | tf_op jit(solution)/shard_map/ppermute | solution.py:358
  16.4 26.3 %collective-permute-start.3 = (bf16[3,160,640]{2,1,0:T(8,128)(2,1)}, bf16[3,160,640]{2,1,0:T(8,128)(2,1)}, u32[]{:S(2)}, u32[]{:S(2)}) collective-permute-start(bf16[3,160,640]{2,1,0:T(8,128)(2,1)} %get-tuple-element.23.own_ref), channel_id=1, source_target_pairs={{0,16},{16,0},{1,17},{17,1},{2,18},{18,2},{3,19},{19,3},{4,20},{20... | collective-permute-start | bytes 1843208 | tf_op jit(solution)/shard_map/ppermute | solution.py:360
  19.5 0.8 copy-start.8
  20.3 0.7 copy-start.4
  20.4 0.9 copy-start.1
  23.7 28.7 %all-to-all-start.1 = ((bf16[4,8,40,128]{3,2,1,0:T(8,128)(2,1)}), bf16[4,8,40,128]{3,2,1,0:T(8,128)(2,1)S(1)}, u32[]{:S(2)}, u32[]{:S(2)}) async-start(bf16[4,8,40,128]{3,2,1,0:T(8,128)(2,1)} %get-tuple-element.29), calls=%async_computation.1 | async-start | bytes 655360 | tf_op jit(solution)/shard_map/all_to_all | solution.py:376
  36.9 14.7 %collective-permute-start.4 = (bf16[3,144,512]{2,1,0:T(8,128)(2,1)}, bf16[3,144,512]{2,1,0:T(8,128)(2,1)S(1)}, u32[]{:S(2)}, u32[]{:S(2)}) collective-permute-start(bf16[3,144,512]{2,1,0:T(8,128)(2,1)} %get-tuple-element.30), channel_id=1, source_target_pairs={{16,0},{32,16},{48,32},{64,48},{80,64},{96,80},{112,96},{128,112},... | collective-permute-start | bytes 1327112 | tf_op jit(solution)/shard_map/ppermute | solution.py:377
  39.3 8.1 %collective-permute-start.5 = (bf16[144,512]{1,0:T(8,128)(2,1)}, bf16[144,512]{1,0:T(8,128)(2,1)S(1)}, u32[]{:S(2)}, u32[]{:S(2)}) collective-permute-start(bf16[144,512]{1,0:T(8,128)(2,1)} %get-tuple-element.31), channel_id=1, source_target_pairs={{0,16},{16,32},{32,48},{48,64},{64,80},{80,96},{96,112},{112,128},... | collective-permute-start | bytes 442376 | tf_op jit(solution)/shard_map/ppermute | solution.py:378
  47.5 0.7 copy-start.14
  51.6 0.8 copy-start.11
  52.4 19.6 %collective-permute-start.8 = (bf16[3,160,640]{2,1,0:T(8,128)(2,1)}, bf16[3,160,640]{2,1,0:T(8,128)(2,1)S(1)}, u32[]{:S(2)}, u32[]{:S(2)}) collective-permute-start(bf16[3,160,640]{2,1,0:T(8,128)(2,1)} %collective-permute-done.3.beside_ref), channel_id=1, source_target_pairs={{0,1},{1,0},{2,3},{3,2},{4,5},{5,4},{6,7},{7,6},{8,9},{9,8},{10,11... | collective-permute-start | bytes 1843208 | tf_op jit(solution)/shard_map/ppermute | solution.py:381
  54.3 12.3 %collective-permute-start.6 = (bf16[4,8,40,128]{3,2,1,0:T(8,128)(2,1)S(1)}, bf16[4,8,40,128]{3,2,1,0:T(8,128)(2,1)S(1)}, u32[]{:S(2)}, u32[]{:S(2)}) collective-permute-start(bf16[4,8,40,128]{3,2,1,0:T(8,128)(2,1)S(1)} %all-to-all-done.1.mid_ref), channel_id=1, source_target_pairs={{0,64},{64,128},{128,192},{192,256},{256,320},{320,384},{384,448},... | collective-permute-start | bytes 983048 | tf_op jit(solution)/shard_map/ppermute | solution.py:382
  59.0 12.9 %collective-permute-start.7 = (bf16[4,8,40,128]{3,2,1,0:T(8,128)(2,1)S(1)}, bf16[4,8,40,128]{3,2,1,0:T(8,128)(2,1)S(1)}, u32[]{:S(2)}, u32[]{:S(2)}) collective-permute-start(bf16[4,8,40,128]{3,2,1,0:T(8,128)(2,1)S(1)} %all-to-all-done.1.mid_ref), channel_id=1, source_target_pairs={{64,0},{128,64},{192,128},{256,192},{320,256},{384,320},{448,384},... | collective-permute-start | bytes 983048 | tf_op jit(solution)/shard_map/ppermute | solution.py:383
  61.0 1.0 %copy-start.2 = (bf16[3,144,512]{2,1,0:T(8,128)(2,1)S(1)}, bf16[3,144,512]{2,1,0:T(8,128)(2,1)}, u32[]{:S(2)}) copy-start(bf16[3,144,512]{2,1,0:T(8,128)(2,1)} %copy-done.1) | copy-start | bytes 1327108
  62.0 1.0 %copy-start.5 = (bf16[2,144,512]{2,1,0:T(8,128)(2,1)S(1)}, bf16[2,144,512]{2,1,0:T(8,128)(2,1)}, u32[]{:S(2)}) copy-start(bf16[2,144,512]{2,1,0:T(8,128)(2,1)} %copy-done.4) | copy-start | bytes 884740
  62.9 1.0 %copy-start.12 = (bf16[3,144,512]{2,1,0:T(8,128)(2,1)S(1)}, bf16[3,144,512]{2,1,0:T(8,128)(2,1)}, u32[]{:S(2)}) copy-start(bf16[3,144,512]{2,1,0:T(8,128)(2,1)} %copy-done.11) | copy-start | bytes 1327108
  63.9 0.9 %copy-start.15 = (bf16[144,512]{1,0:T(8,128)(2,1)S(1)}, bf16[144,512]{1,0:T(8,128)(2,1)}, u32[]{:S(2)}) copy-start(bf16[144,512]{1,0:T(8,128)(2,1)} %copy-done.14) | copy-start | bytes 442372
  64.9 7.1 %copy-start.7 = (bf16[3,160,640]{2,1,0:T(8,128)(2,1)S(1)}, bf16[3,160,640]{2,1,0:T(8,128)(2,1)}, u32[]{:S(2)}) copy-start(bf16[3,160,640]{2,1,0:T(8,128)(2,1)} %get-tuple-element.23.own_ref) | copy-start | bytes 1843204
  64.9 7.1 %copy-start.9 = (bf16[3,160,640]{2,1,0:T(8,128)(2,1)S(1)}, bf16[3,160,640]{2,1,0:T(8,128)(2,1)}, u32[]{:S(2)}) copy-start(bf16[3,160,640]{2,1,0:T(8,128)(2,1)} %copy-done.8) | copy-start | bytes 1843204
  64.9 7.1 %copy-start.17 = (s32[8,128]{1,0:T(8,128)S(1)}, s32[8,128]{1,0:T(8,128)}, u32[]{:S(2)}) copy-start(s32[8,128]{1,0:T(8,128)} %get-tuple-element.34.lists_ref) | copy-start | bytes 12292
  66.4 19.4 %copy-start.6 = (bf16[1,1,512,160]{2,3,1,0:T(8,128)(2,1)S(1)}, bf16[1,1,512,160]{2,3,1,0:T(8,128)(2,1)}, u32[]{:S(2)}) copy-start(bf16[1,1,512,160]{2,3,1,0:T(8,128)(2,1)} %param.15) | copy-start | bytes 491524
  66.4 19.4 %copy-start.13 = (bf16[1,1,160,160]{3,2,1,0:T(8,128)(2,1)S(1)}, bf16[1,1,160,160]{3,2,1,0:T(8,128)(2,1)}, u32[]{:S(2)}) copy-start(bf16[1,1,160,160]{3,2,1,0:T(8,128)(2,1)} %param.16) | copy-start | bytes 153604
  66.4 19.4 %copy-start.16 = (bf16[160,160]{1,0:T(8,128)(2,1)S(1)}, bf16[160,160]{1,0:T(8,128)(2,1)}, u32[]{:S(2)}) copy-start(bf16[160,160]{1,0:T(8,128)(2,1)} %get-tuple-element.38.level_ref) | copy-start | bytes 153604

commit v3 on v2

--- a/solution.py
+++ b/solution.py
@@ -358,9 +358,7 @@
     from_right = lax.ppermute(left, across_gy, [(i + 1, i) for i in range(15)])
     from_left = lax.ppermute(right, across_gy, [(i, i + 1) for i in range(15)])
     beside = lax.ppermute(own, "xl", swap)
-    across = lax.ppermute(own, "c", swap)
-    got, across = lax.optimization_barrier((got, across))
-    window, level, codes, rise, sink = fused(
+    window, level, codes = fused(
         Stage(
             merge_body,
             [shape(4, SLABS, PAD, 128), shape(RANK, RANK), shape(8, 128, dtype=I32)],
@@ -369,20 +367,21 @@
             scalars=[me],
             repeats={0: [0] * 4},
         ),
-        Stage(
-            turn_body, [shape(3, 144, 512), shape(144, 512)], [], [x, below, from_right, from_left]
-        ),
     )
     plane = lax.all_to_all(window, "zh", 0, 0)
+    below, late, _ = lax.optimization_barrier((below, own, window))
+    rise, sink = fused(
+        Stage(turn_body, [shape(3, 144, 512), shape(144, 512)], [], [x, below, from_right, from_left])
+    )
     risen = lax.ppermute(rise, along_gx, [(i + 1, i) for i in range(31)])
     sunk = lax.ppermute(sink, along_gx, [(i, i + 1) for i in range(31)])
-
-    plane, beside, risen, sunk = lax.optimization_barrier((plane, beside, risen, sunk))
+    across = lax.ppermute(late, "c", swap)
+    beside, _ = lax.optimization_barrier((beside, plane))
     opposite = lax.ppermute(beside, "c", swap)
     above = lax.ppermute(plane, "y", [(i, i + 1) for i in range(7)])
     under = lax.ppermute(plane, "y", [(i + 1, i) for i in range(7)])
     near = call(
-        near_body, shape(144, 512, dtype=F32), [], [SMEM, SMEM] + [VMEM] * 7, 4 * 10**8, 4 * 10**6
+        near_body, shape(144, 512, dtype=F32), [], [SMEM, SMEM] + [VMEM] * 7, 5 * 10**9, 4 * 10**6
     )(me, links, x, near_self[0, 0], blocks, from_right, from_left, risen, sunk)
     codes = after(codes, near)
     partial = call(

time: 87.9 us -> 76.9 us (0.87)
  the two profiles are of different devices: /device:TPU:28 before, /device:TPU:36 now
where the time goes in v3:
time: 76.9 us; the launch traced here: 76.1 us
  starting transfers between devices  40.2 us (52%)
  Pallas kernels  14.3 us (19%)
  blocking collectives  11.6 us (15%)
  waiting for transfers between devices  7.01 us (9%)
  local copies, waits for them, and re-layouts  2.73 us (4%)
    all_to_all x1, blocking collectives, shards(): sums = lax.all_to_all(partial, ('xl', 'zl', 'c'), 0, 0)  11.6 us
    all_to_all x1, starting transfers between devices, shards(): plane = lax.all_to_all(window, 'zh', 0, 0)  10.6 us
    pallas_call x3, Pallas kernels, fused(): pl.pallas_call(run, out_shape=outs, in_specs=[ANY] * (len(shared) + len(l...  8.11 us
    all_to_all x1, starting transfers between devices, shards(): got = lax.all_to_all(message, ('xh', 'xl', 'zl', 'c'), 0, 0)  6.91 us
    ppermute x1, starting transfers between devices, shards(): sunk = lax.ppermute(sink, along_gx, [(i, i + 1) for i in range(31)])  3.92 us
    ppermute x1, starting transfers between devices, shards(): above = lax.ppermute(plane, 'y', [(i, i + 1) for i in range(7)])  3.49 us
    ppermute x1, waiting for transfers between devices, shards(): above = lax.ppermute(plane, 'y', [(i, i + 1) for i in range(7)])  3.3 us
    ppermute x1, starting transfers between devices, shards(): beside = lax.ppermute(own, 'xl', swap)  3.07 us
  transfers between devices with their start and end apart: 11, of which 4 were waited for; matrix products, arithmetic and copies ran while one was open for 0% of the time, Pallas kernels for 9%

profile of v3, /device:TPU:36, one launch (start us, length us, event | category | flops | bytes accessed | tf_op | source)
XLA Modules:
  0.0 76.1 jit_solution(11014522163802055568)
XLA Ops:
  0.0 3.8 %shard_map.109 = (bf16[16,128,128]{2,1,0:T(8,128)(2,1)}, bf16[2,144,512]{2,1,0:T(8,128)(2,1)}, bf16[3,144,512]{2,1,0:T(8,128)(2,1)}, bf16[144,512]{1,0:T(8,128)(2,1)}, bf16[3,160,640]{2,1,0:T(8,128)(2,1)}) custom-call(bf16[144,512]{1,0:T(8,128)(2,1)} %bitcast.23, bf16[160,512]{1,0:T(8,128)(2,1)} %bitcast.21, bf16[160,160]{1,0:T(8,128)(2,1)} %bitcast.26, ...), custom_call_target="tpu_custom_call" | custom-call | flops 400000000 | bytes 5059072 | tf_op jit(solution)/shard_map/pallas_call | solution.py:90
  3.8 0.0 copy-start.2
  3.8 0.0 copy-start
  3.8 0.0 copy-start.3
  3.8 0.0 copy-start.9
  3.8 6.9 %all-to-all-start = ((bf16[16,128,128]{2,1,0:T(8,128)(2,1)}), bf16[16,128,128]{2,1,0:T(8,128)(2,1)}, u32[]{:S(2)}, u32[]{:S(2)}) async-start(bf16[16,128,128]{2,1,0:T(8,128)(2,1)} %get-tuple-element.19), calls=%async_computation | async-start | bytes 1048576 | tf_op jit(solution)/shard_map/all_to_all | solution.py:357
  10.7 2.8 %collective-permute-start.1 = (bf16[3,144,512]{2,1,0:T(8,128)(2,1)}, bf16[3,144,512]{2,1,0:T(8,128)(2,1)}, u32[]{:S(2)}, u32[]{:S(2)}) collective-permute-start(bf16[3,144,512]{2,1,0:T(8,128)(2,1)} %get-tuple-element.22), channel_id=1, source_target_pairs={{0,1},{1,2},{2,3},{3,4},{4,5},{5,6},{6,7},{7,8},{8,9},{9,10},{10,1... | collective-permute-start | bytes 1327112 | tf_op jit(solution)/shard_map/ppermute | solution.py:359
  13.6 3.1 %collective-permute-start.6 = (bf16[3,160,640]{2,1,0:T(8,128)(2,1)}, bf16[3,160,640]{2,1,0:T(8,128)(2,1)}, u32[]{:S(2)}, u32[]{:S(2)}) collective-permute-start(bf16[3,160,640]{2,1,0:T(8,128)(2,1)} %get-tuple-element.31.own_ref), channel_id=1, source_target_pairs={{0,16},{16,0},{1,17},{17,1},{2,18},{18,2},{3,19},{19,3},{4,20},{20... | collective-permute-start | bytes 1843208 | tf_op jit(solution)/shard_map/ppermute | solution.py:360
  16.6 1.3 %collective-permute-start = (bf16[2,144,512]{2,1,0:T(8,128)(2,1)}, bf16[2,144,512]{2,1,0:T(8,128)(2,1)S(1)}, u32[]{:S(2)}, u32[]{:S(2)}) collective-permute-start(bf16[2,144,512]{2,1,0:T(8,128)(2,1)} %get-tuple-element.21), channel_id=1, source_target_pairs={{1,0},{2,1},{3,2},{4,3},{5,4},{6,5},{7,6},{8,7},{9,8},{10,9},{11,1... | collective-permute-start | bytes 884744 | tf_op jit(solution)/shard_map/ppermute | solution.py:358
  17.9 1.2 %all-to-all-done.refs_0_ = bf16[16,128,128]{2,1,0:T(8,128)(2,1)} async-done(((bf16[16,128,128]{2,1,0:T(8,128)(2,1)}), bf16[16,128,128]{2,1,0:T(8,128)(2,1)}, u32[]{:S(2)}, u32[]{:S(2)}) %all-to-all-start) | async-done | bytes 524320 | tf_op jit(solution)/shard_map/all_to_all | solution.py:357
  19.1 2.2 %shard_map.110 = (bf16[4,8,40,128]{3,2,1,0:T(8,128)(2,1)}, bf16[160,160]{1,0:T(8,128)(2,1)}, s32[8,128]{1,0:T(8,128)}) custom-call(bf16[16,128,128]{2,1,0:T(8,128)(2,1)} %all-to-all-done.refs_0_, s32[1]{0:T(128)} %bitcast.refs_10_.refs_1_.me_ref), custom_call_target="tpu_custom_call" | custom-call | flops 100000000 | bytes 907264 | tf_op jit(solution)/shard_map/pallas_call | solution.py:90
  21.3 10.6 %all-to-all-start.1 = ((bf16[4,8,40,128]{3,2,1,0:T(8,128)(2,1)}), bf16[4,8,40,128]{3,2,1,0:T(8,128)(2,1)S(1)}, u32[]{:S(2)}, u32[]{:S(2)}) async-start(bf16[4,8,40,128]{3,2,1,0:T(8,128)(2,1)} %get-tuple-element.25), calls=%async_computation.1 | async-start | bytes 655360 | tf_op jit(solution)/shard_map/all_to_all | solution.py:371
  31.9 0.0 collective-permute-done.refs_2_.from_right_ref
  31.9 0.0 copy-start.5
  31.9 0.0 collective-permute-done.1.refs_3_.from_left_ref
  32.0 0.7 copy-done.5
  32.6 2.1 %shard_map.111 = (bf16[3,144,512]{2,1,0:T(8,128)(2,1)}, bf16[144,512]{1,0:T(8,128)(2,1)}) custom-call(bf16[144,512]{1,0:T(8,128)(2,1)} %bitcast.24, bf16[144,512]{1,0:T(8,128)(2,1)} %get-tuple-element.26.refs_1_, bf16[2,144,512]{2,1,0:T(8,128)(2,1)} %copy-done.5, bf16[3,144,512]{2,1,0:T(8,128)(2,1)} %collective-permute-done.1.refs_3_.from_left_ref), custom_call_target="tpu_custom_call" | custom-call | flops 100000000 | bytes 1622016 | tf_op jit(solution)/shard_map/pallas_call | solution.py:90
  34.8 1.9 %collective-permute-start.2 = (bf16[3,144,512]{2,1,0:T(8,128)(2,1)}, bf16[3,144,512]{2,1,0:T(8,128)(2,1)}, u32[]{:S(2)}, u32[]{:S(2)}) collective-permute-start(bf16[3,144,512]{2,1,0:T(8,128)(2,1)} %get-tuple-element.27), channel_id=1, source_target_pairs={{16,0},{32,16},{48,32},{64,48},{80,64},{96,80},{112,96},{128,112},... | collective-permute-start | bytes 1327112 | tf_op jit(solution)/shard_map/ppermute | solution.py:376
  36.7 3.9 %collective-permute-start.3 = (bf16[144,512]{1,0:T(8,128)(2,1)}, bf16[144,512]{1,0:T(8,128)(2,1)S(1)}, u32[]{:S(2)}, u32[]{:S(2)}) collective-permute-start(bf16[144,512]{1,0:T(8,128)(2,1)} %get-tuple-element.28), channel_id=1, source_target_pairs={{0,16},{16,32},{32,48},{48,64},{64,80},{80,96},{96,112},{112,128},... | collective-permute-start | bytes 442376 | tf_op jit(solution)/shard_map/ppermute | solution.py:377
  40.6 0.0 copy-done.2
  40.7 1.9 %collective-permute-start.7 = (bf16[3,160,640]{2,1,0:T(8,128)(2,1)S(1)}, bf16[3,160,640]{2,1,0:T(8,128)(2,1)}, u32[]{:S(2)}, u32[]{:S(2)}) collective-permute-start(bf16[3,160,640]{2,1,0:T(8,128)(2,1)S(1)} %copy-done.2), channel_id=1, source_target_pairs={{0,1},{1,0},{2,3},{3,2},{4,5},{5,4},{6,7},{7,6},{8,9},{9,8},{10,11... | collective-permute-start | bytes 1843208 | tf_op jit(solution)/shard_map/ppermute | solution.py:378
  42.6 0.0 collective-permute-done.6.beside_ref
  42.6 0.6 all-to-all-done.1.mid_ref
  43.2 1.9 %collective-permute-start.8 = (bf16[3,160,640]{2,1,0:T(8,128)(2,1)}, bf16[3,160,640]{2,1,0:T(8,128)(2,1)S(1)}, u32[]{:S(2)}, u32[]{:S(2)}) collective-permute-start(bf16[3,160,640]{2,1,0:T(8,128)(2,1)} %collective-permute-done.6.beside_ref), channel_id=1, source_target_pairs={{0,1},{1,0},{2,3},{3,2},{4,5},{5,4},{6,7},{7,6},{8,9},{9,8},{10,11... | collective-permute-start | bytes 1843208 | tf_op jit(solution)/shard_map/ppermute | solution.py:380
  45.1 2.4 %collective-permute-start.5 = (bf16[4,8,40,128]{3,2,1,0:T(8,128)(2,1)S(1)}, bf16[4,8,40,128]{3,2,1,0:T(8,128)(2,1)S(1)}, u32[]{:S(2)}, u32[]{:S(2)}) collective-permute-start(bf16[4,8,40,128]{3,2,1,0:T(8,128)(2,1)S(1)} %all-to-all-done.1.mid_ref), channel_id=1, source_target_pairs={{64,0},{128,64},{192,128},{256,192},{320,256},{384,320},{448,384},... | collective-permute-start | bytes 983048 | tf_op jit(solution)/shard_map/ppermute | solution.py:382
  47.5 0.0 collective-permute-done.3.sunk_ref
  47.5 3.5 %collective-permute-start.4 = (bf16[4,8,40,128]{3,2,1,0:T(8,128)(2,1)S(1)}, bf16[4,8,40,128]{3,2,1,0:T(8,128)(2,1)S(1)}, u32[]{:S(2)}, u32[]{:S(2)}) collective-permute-start(bf16[4,8,40,128]{3,2,1,0:T(8,128)(2,1)S(1)} %all-to-all-done.1.mid_ref), channel_id=1, source_target_pairs={{0,64},{64,128},{128,192},{192,256},{256,320},{320,384},{384,448},... | collective-permute-start | bytes 983048 | tf_op jit(solution)/shard_map/ppermute | solution.py:381
  51.0 0.0 collective-permute-done.2.risen_ref
  51.0 0.0 copy-done
  51.0 0.0 copy-done.3
  51.0 0.0 copy-done.9
  51.0 0.0 copy-start.6
  51.1 1.0 %copy-done.6 = bf16[2,144,512]{2,1,0:T(8,128)(2,1)S(1)} copy-done((bf16[2,144,512]{2,1,0:T(8,128)(2,1)S(1)}, bf16[2,144,512]{2,1,0:T(8,128)(2,1)}, u32[]{:S(2)}) %copy-start.6) | copy-done | bytes 294936
  52.0 0.0 copy-start.10
  52.0 1.0 %copy-done.10 = bf16[1,1,512,512]{3,2,1,0:T(8,128)(2,1)S(1)} copy-done((bf16[1,1,512,512]{3,2,1,0:T(8,128)(2,1)S(1)}, bf16[1,1,512,512]{3,2,1,0:T(8,128)(2,1)}, u32[]{:S(2)}) %copy-start.10) | copy-done | bytes 524312
  53.1 0.0 copy-start.8
  53.1 2.2 %shard_map.112.near_ref = f32[144,512]{1,0:T(8,128)S(1)} custom-call(s32[1]{0:T(128)} %bitcast.refs_10_.refs_1_.me_ref, s32[1,4]{1,0:T(1,128)S(1)} %bitcast.29, bf16[144,512]{1,0:T(8,128)(2,1)S(1)} %bitcast.25, bf16[512,512]{1,0:T(8,128)(2,1)S(1)} %bitcast.30, bf16[4,512,512]{2,1,0:T(8,128)(2,1)S(1)} %bitcast.20, bf16[2,144,512]{2,1,0:T(8,128)(2,1)S(1)} %copy-done.6, ...), custom_call_target="tpu_custom_call" | custom-call | flops 5000000000 | bytes 4000000 | tf_op jit(solution)/shard_map/pallas_call | solution.py:383
  55.2 0.0 copy-start.1
  55.2 0.0 copy-start.4
  55.2 0.0 copy-start.7
  55.2 0.0 collective-permute-done.7.across_ref
  55.3 1.9 %collective-permute-done.5.down_ref = bf16[4,8,40,128]{3,2,1,0:T(8,128)(2,1)S(1)} collective-permute-done((bf16[4,8,40,128]{3,2,1,0:T(8,128)(2,1)S(1)}, bf16[4,8,40,128]{3,2,1,0:T(8,128)(2,1)S(1)}, u32[]{:S(2)}, u32[]{:S(2)}) %collective-permute-start.5) | collective-permute-done | bytes 327712 | tf_op jit(solution)/shard_map/ppermute | solution.py:382
  57.1 3.3 %collective-permute-done.4.up_ref = bf16[4,8,40,128]{3,2,1,0:T(8,128)(2,1)S(1)} collective-permute-done((bf16[4,8,40,128]{3,2,1,0:T(8,128)(2,1)S(1)}, bf16[4,8,40,128]{3,2,1,0:T(8,128)(2,1)S(1)}, u32[]{:S(2)}, u32[]{:S(2)}) %collective-permute-start.4) | collective-permute-done | bytes 327712 | tf_op jit(solution)/shard_map/ppermute | solution.py:381
  60.4 0.0 collective-permute-done.8.opposite_ref
  60.4 0.0 copy-done.8
  60.4 2.7 %shard_map.113 = bf16[8,128,128]{2,1,0:T(8,128)(2,1)S(1)} custom-call(s32[1]{0:T(128)} %bitcast.refs_10_.refs_1_.me_ref, s32[8,128]{1,0:T(8,128)S(1)} %copy-done.8, bf16[4,8,40,128]{3,2,1,0:T(8,128)(2,1)S(1)} %collective-permute-done.4.up_ref, bf16[4,8,40,128]{3,2,1,0:T(8,128)(2,1)S(1)} %all-to-all-done.1.mid_ref, ...), custom_call_target="tpu_custom_call" | custom-call | flops 600000000 | bytes 4000000 | tf_op jit(solution)/shard_map/pallas_call | solution.py:387
  63.2 11.6 %all_to_all.15.got_ref = bf16[8,128,128]{2,1,0:T(8,128)(2,1)S(1)} all-to-all(bf16[8,128,128]{2,1,0:T(8,128)(2,1)S(1)} %shard_map.113), channel_id=1, replica_groups=mesh['y'=8,'xh'=2,'xl'=2,'zh'=4,'zl'=2,'c'=2] {'xl','zl','c'}, dimensions={0} | all-to-all | bytes 524288 | tf_op jit(solution)/shard_map/all_to_all | solution.py:399
  74.8 0.0 copy-done.1
  74.8 0.0 copy-done.4
  74.8 0.0 copy-done.7
  74.8 1.4 %shard_map.114 = bf16[144,512]{1,0:T(8,128)(2,1)} custom-call(s32[1]{0:T(128)} %bitcast.refs_10_.refs_1_.me_ref, bf16[8,128,128]{2,1,0:T(8,128)(2,1)S(1)} %all_to_all.15.got_ref, bf16[160,160]{1,0:T(8,128)(2,1)S(1)} %copy-done.7, bf16[160,160]{1,0:T(8,128)(2,1)S(1)} %bitcast.27, bf16[160,512]{1,0:T(8,128)(2,1)S(1)} %bitcast.22, ...), custom_call_target="tpu_custom_call" | custom-call | flops 100000000 | bytes 1000000 | tf_op jit(solution)/shard_map/pallas_call | solution.py:400
Async XLA Ops:
  3.8 36.9 %copy-start.2 = (bf16[3,160,640]{2,1,0:T(8,128)(2,1)S(1)}, bf16[3,160,640]{2,1,0:T(8,128)(2,1)}, u32[]{:S(2)}) copy-start(bf16[3,160,640]{2,1,0:T(8,128)(2,1)} %get-tuple-element.31.own_ref) | copy-start | bytes 1843204
  3.8 47.2 %copy-start = (bf16[1,1,4,512,512]{4,3,2,1,0:T(8,128)(2,1)S(1)}, bf16[1,1,4,512,512]{4,3,2,1,0:T(8,128)(2,1)}, u32[]{:S(2)}) copy-start(bf16[1,1,4,512,512]{4,3,2,1,0:T(8,128)(2,1)} %param.13) | copy-start | bytes 6291460
  3.8 47.2 %copy-start.3 = (bf16[1,1,512,144]{2,3,1,0:T(8,128)(2,1)S(1)}, bf16[1,1,512,144]{2,3,1,0:T(8,128)(2,1)}, u32[]{:S(2)}) copy-start(bf16[1,1,512,144]{2,3,1,0:T(8,128)(2,1)} %param.11) | copy-start | bytes 442372
  3.8 47.2 %copy-start.9 = (s32[1,1,4]{2,1,0:T(1,128)S(1)}, s32[1,1,4]{2,1,0:T(1,128)}, u32[]{:S(2)}) copy-start(s32[1,1,4]{2,1,0:T(1,128)} %param.14) | copy-start | bytes 52
  3.8 15.3 %all-to-all-start = ((bf16[16,128,128]{2,1,0:T(8,128)(2,1)}), bf16[16,128,128]{2,1,0:T(8,128)(2,1)}, u32[]{:S(2)}, u32[]{:S(2)}) async-start(bf16[16,128,128]{2,1,0:T(8,128)(2,1)} %get-tuple-element.19), calls=%async_computation | async-start | bytes 1048576 | tf_op jit(solution)/shard_map/all_to_all | solution.py:357
  10.7 21.2 %collective-permute-start.1 = (bf16[3,144,512]{2,1,0:T(8,128)(2,1)}, bf16[3,144,512]{2,1,0:T(8,128)(2,1)}, u32[]{:S(2)}, u32[]{:S(2)}) collective-permute-start(bf16[3,144,512]{2,1,0:T(8,128)(2,1)} %get-tuple-element.22), channel_id=1, source_target_pairs={{0,1},{1,2},{2,3},{3,4},{4,5},{5,6},{6,7},{7,8},{8,9},{9,10},{10,1... | collective-permute-start | bytes 1327112 | tf_op jit(solution)/shard_map/ppermute | solution.py:359
  13.6 29.0 %collective-permute-start.6 = (bf16[3,160,640]{2,1,0:T(8,128)(2,1)}, bf16[3,160,640]{2,1,0:T(8,128)(2,1)}, u32[]{:S(2)}, u32[]{:S(2)}) collective-permute-start(bf16[3,160,640]{2,1,0:T(8,128)(2,1)} %get-tuple-element.31.own_ref), channel_id=1, source_target_pairs={{0,16},{16,0},{1,17},{17,1},{2,18},{18,2},{3,19},{19,3},{4,20},{20... | collective-permute-start | bytes 1843208 | tf_op jit(solution)/shard_map/ppermute | solution.py:360
  16.6 15.3 %collective-permute-start = (bf16[2,144,512]{2,1,0:T(8,128)(2,1)}, bf16[2,144,512]{2,1,0:T(8,128)(2,1)S(1)}, u32[]{:S(2)}, u32[]{:S(2)}) collective-permute-start(bf16[2,144,512]{2,1,0:T(8,128)(2,1)} %get-tuple-element.21), channel_id=1, source_target_pairs={{1,0},{2,1},{3,2},{4,3},{5,4},{6,5},{7,6},{8,7},{9,8},{10,9},{11,1... | collective-permute-start | bytes 884744 | tf_op jit(solution)/shard_map/ppermute | solution.py:358
  21.3 21.9 %all-to-all-start.1 = ((bf16[4,8,40,128]{3,2,1,0:T(8,128)(2,1)}), bf16[4,8,40,128]{3,2,1,0:T(8,128)(2,1)S(1)}, u32[]{:S(2)}, u32[]{:S(2)}) async-start(bf16[4,8,40,128]{3,2,1,0:T(8,128)(2,1)} %get-tuple-element.25), calls=%async_computation.1 | async-start | bytes 655360 | tf_op jit(solution)/shard_map/all_to_all | solution.py:371
  31.9 0.7 copy-start.5
  34.8 16.2 %collective-permute-start.2 = (bf16[3,144,512]{2,1,0:T(8,128)(2,1)}, bf16[3,144,512]{2,1,0:T(8,128)(2,1)}, u32[]{:S(2)}, u32[]{:S(2)}) collective-permute-start(bf16[3,144,512]{2,1,0:T(8,128)(2,1)} %get-tuple-element.27), channel_id=1, source_target_pairs={{16,0},{32,16},{48,32},{64,48},{80,64},{96,80},{112,96},{128,112},... | collective-permute-start | bytes 1327112 | tf_op jit(solution)/shard_map/ppermute | solution.py:376
  36.7 10.8 %collective-permute-start.3 = (bf16[144,512]{1,0:T(8,128)(2,1)}, bf16[144,512]{1,0:T(8,128)(2,1)S(1)}, u32[]{:S(2)}, u32[]{:S(2)}) collective-permute-start(bf16[144,512]{1,0:T(8,128)(2,1)} %get-tuple-element.28), channel_id=1, source_target_pairs={{0,16},{16,32},{32,48},{48,64},{64,80},{80,96},{96,112},{112,128},... | collective-permute-start | bytes 442376 | tf_op jit(solution)/shard_map/ppermute | solution.py:377
  40.7 14.6 %collective-permute-start.7 = (bf16[3,160,640]{2,1,0:T(8,128)(2,1)S(1)}, bf16[3,160,640]{2,1,0:T(8,128)(2,1)}, u32[]{:S(2)}, u32[]{:S(2)}) collective-permute-start(bf16[3,160,640]{2,1,0:T(8,128)(2,1)S(1)} %copy-done.2), channel_id=1, source_target_pairs={{0,1},{1,0},{2,3},{3,2},{4,5},{5,4},{6,7},{7,6},{8,9},{9,8},{10,11... | collective-permute-start | bytes 1843208 | tf_op jit(solution)/shard_map/ppermute | solution.py:378
  43.2 17.2 %collective-permute-start.8 = (bf16[3,160,640]{2,1,0:T(8,128)(2,1)}, bf16[3,160,640]{2,1,0:T(8,128)(2,1)S(1)}, u32[]{:S(2)}, u32[]{:S(2)}) collective-permute-start(bf16[3,160,640]{2,1,0:T(8,128)(2,1)} %collective-permute-done.6.beside_ref), channel_id=1, source_target_pairs={{0,1},{1,0},{2,3},{3,2},{4,5},{5,4},{6,7},{7,6},{8,9},{9,8},{10,11... | collective-permute-start | bytes 1843208 | tf_op jit(solution)/shard_map/ppermute | solution.py:380
  45.1 12.0 %collective-permute-start.5 = (bf16[4,8,40,128]{3,2,1,0:T(8,128)(2,1)S(1)}, bf16[4,8,40,128]{3,2,1,0:T(8,128)(2,1)S(1)}, u32[]{:S(2)}, u32[]{:S(2)}) collective-permute-start(bf16[4,8,40,128]{3,2,1,0:T(8,128)(2,1)S(1)} %all-to-all-done.1.mid_ref), channel_id=1, source_target_pairs={{64,0},{128,64},{192,128},{256,192},{320,256},{384,320},{448,384},... | collective-permute-start | bytes 983048 | tf_op jit(solution)/shard_map/ppermute | solution.py:382
  47.5 12.9 %collective-permute-start.4 = (bf16[4,8,40,128]{3,2,1,0:T(8,128)(2,1)S(1)}, bf16[4,8,40,128]{3,2,1,0:T(8,128)(2,1)S(1)}, u32[]{:S(2)}, u32[]{:S(2)}) collective-permute-start(bf16[4,8,40,128]{3,2,1,0:T(8,128)(2,1)S(1)} %all-to-all-done.1.mid_ref), channel_id=1, source_target_pairs={{0,64},{64,128},{128,192},{192,256},{256,320},{320,384},{384,448},... | collective-permute-start | bytes 983048 | tf_op jit(solution)/shard_map/ppermute | solution.py:381
  51.0 1.0 %copy-start.6 = (bf16[2,144,512]{2,1,0:T(8,128)(2,1)S(1)}, bf16[2,144,512]{2,1,0:T(8,128)(2,1)}, u32[]{:S(2)}) copy-start(bf16[2,144,512]{2,1,0:T(8,128)(2,1)} %copy-done.5) | copy-start | bytes 884740
  52.0 1.0 %copy-start.10 = (bf16[1,1,512,512]{3,2,1,0:T(8,128)(2,1)S(1)}, bf16[1,1,512,512]{3,2,1,0:T(8,128)(2,1)}, u32[]{:S(2)}) copy-start(bf16[1,1,512,512]{3,2,1,0:T(8,128)(2,1)} %param.12) | copy-start | bytes 1572868
  53.1 7.4 %copy-start.8 = (s32[8,128]{1,0:T(8,128)S(1)}, s32[8,128]{1,0:T(8,128)}, u32[]{:S(2)}) copy-start(s32[8,128]{1,0:T(8,128)} %get-tuple-element.29.lists_ref) | copy-start | bytes 12292
  55.2 19.6 %copy-start.1 = (bf16[1,1,512,160]{2,3,1,0:T(8,128)(2,1)S(1)}, bf16[1,1,512,160]{2,3,1,0:T(8,128)(2,1)}, u32[]{:S(2)}) copy-start(bf16[1,1,512,160]{2,3,1,0:T(8,128)(2,1)} %param.15) | copy-start | bytes 491524
  55.2 19.6 %copy-start.4 = (bf16[1,1,160,160]{3,2,1,0:T(8,128)(2,1)S(1)}, bf16[1,1,160,160]{3,2,1,0:T(8,128)(2,1)}, u32[]{:S(2)}) copy-start(bf16[1,1,160,160]{3,2,1,0:T(8,128)(2,1)} %param.16) | copy-start | bytes 153604
  55.2 19.5 %copy-start.7 = (bf16[160,160]{1,0:T(8,128)(2,1)S(1)}, bf16[160,160]{1,0:T(8,128)(2,1)}, u32[]{:S(2)}) copy-start(bf16[160,160]{1,0:T(8,128)(2,1)} %get-tuple-element.32.level_ref) | copy-start | bytes 153604

commit v4 on v3

--- a/solution.py
+++ b/solution.py
@@ -18,11 +18,14 @@
 
 
 class Stage:
-    def __init__(self, body, outs, scratch, args, lists=(), scalars=(), repeats=None):
+    def __init__(self, body, outs, scratch, args, lists=(), scalars=(), repeats=None, heads=None, also=()):
         self.body, self.outs, self.scratch, self.args = body, outs, scratch, list(args)
         self.lists, self.scalars, self.repeats = list(lists), list(scalars), repeats or {}
+        self.heads, self.also = heads or {}, also
         self.ready = [
-            shape(max(self.repeats[o]) + 1, *out.shape[1:], dtype=out.dtype) if o in self.repeats else out
+            shape(max(self.repeats[o]) + 1, *out.shape[1:], dtype=out.dtype)
+            if o in self.repeats
+            else shape(self.heads.get(o, out.shape[0]), *out.shape[1:], dtype=out.dtype)
             for o, out in enumerate(outs)
         ]
 
@@ -43,6 +46,7 @@
     outs = [o for stage in stages for o in stage.outs]
     ready = [o for stage in stages for o in stage.ready]
     n_copies = sum(len(stage.repeats.get(o, (0,))) for stage in stages for o in range(len(stage.outs)))
+    n_copies += sum(len(stage.also) for stage in stages)
 
     def run(*refs):
         refs = list(refs)
@@ -62,7 +66,7 @@
             copy.start()
         for copy in fetch[len(shared) :]:
             copy.wait()
-        arrived, leaving = set(), []
+        arrived, leaving, everything = set(), [], list(results)
         for stage, use in zip(stages, uses):
             for i in use:
                 if i not in arrived:
@@ -73,9 +77,13 @@
             heads = [plain.pop(0) for _ in stage.scalars] + [read.pop(0) for _ in stage.lists]
             stage.body(*heads, *[held[i] for i in use], *mine, *take(len(stage.scratch)))
             for o in range(len(stage.outs)):
-                pairs = [(mine[o], targets[o])]
+                whole = targets[o].at[pl.ds(0, stage.heads[o])] if o in stage.heads else targets[o]
+                pairs = [(mine[o], whole)]
                 if o in stage.repeats:
                     pairs = [(mine[o].at[part], targets[o].at[d]) for d, part in enumerate(stage.repeats[o])]
+                for held_at, out, row in stage.also:
+                    if held_at == o:
+                        pairs.append((mine[o], everything[out].at[pl.ds(row, mine[o].shape[0])]))
                 for source, target in pairs:
                     leaving.append(pltpu.make_async_copy(source, target, out_sems.at[len(leaving)]))
                     leaving[-1].start()
@@ -137,11 +145,26 @@
     return jnp.where(hit, 1.0, 0.0).astype(BF16)
 
 
+ROWS = 104
+
+
 def packed(a, b, tail, wide):
     wide[0, :, :RANK] = a
     wide[1, :, :RANK] = b
-    rest = wide[0, :, 128:] + pltpu.roll(wide[1, :, 128:], 32, 1)
-    return jnp.concatenate([wide[0, :, :128], wide[1, :, :128], rest, tail], axis=0).astype(BF16)
+    first, second = wide[0, :, 128:], wide[1, :, 128:]
+    rest = (
+        first[:24]
+        + pltpu.roll(jnp.concatenate([first[24:], tail], axis=0), 32, 1)
+        + pltpu.roll(second[:24], 64, 1)
+        + pltpu.roll(jnp.concatenate([second[24:], jnp.zeros((8, 128), F32)], axis=0), 96, 1)
+    )
+    return jnp.concatenate([wide[0, :, :128], wide[1, :, :128], rest], axis=0).astype(BF16)
+
+
+def rest_of(block, which):
+    rest = block[2 * PAD :]
+    left = pltpu.roll(rest, 64, 1) if which else rest
+    return jnp.concatenate([left, pltpu.roll(left, 96, 1)[:16]], axis=0)
 
 
 def up_body(far_one_ref, far_two_ref, x_ref, basis_ref, one_ref, two_ref, out_ref, wide):
@@ -152,6 +175,7 @@
     for r, ref in enumerate((far_one_ref, far_two_ref)):
         for k in range(SLOTS[r]):
             tail = jnp.where((row == r) & (lane == k), ref[0, k].astype(F32), tail)
+    tail = jnp.where(lane < 32, tail, 0.0)
     leaf = mul_t(x_ref[...], basis_ref[...]).astype(BF16)
     up = mul(leaf, one_ref[...]).astype(BF16)
     chunks = mul(spreader(4, 144), up)
@@ -174,15 +198,14 @@
     for xh in range(2):
         second = jnp.zeros((PAD, RANK), F32)
         for zl in range(2):
-            main = jnp.zeros((PAD, 128), F32)
-            rest = jnp.zeros((PAD, 128), F32)
+            total = jnp.zeros((ROWS, 128), F32)
             for q in range(4):
                 block = got_ref[xh * 8 + (q // 2) * 4 + zl * 2 + q % 2].astype(F32)
-                main += block[:PAD]
-                rest += block[2 * PAD : 3 * PAD]
+                total += block
                 rows = slice(PAD * q, PAD * (q + 1))
                 levels[xh * 2 + zl, rows, :128] = block[PAD : 2 * PAD]
-                levels[xh * 2 + zl, rows, 128:] = pltpu.roll(block[2 * PAD : 3 * PAD], 96, 1)
+                levels[xh * 2 + zl, rows, 128:] = rest_of(block, 1)
+            main, rest = total[:PAD], rest_of(total, 0)
             wide[:, :128] = main
             wide[:, 128:] = rest
             first = wide[:, :RANK]
@@ -195,25 +218,9 @@
     level_ref[...] = levels[own, :, :RANK].astype(BF16)
     for q in range(4):
         place = (me // 32) % 2 * 8 + (q // 2) * 4 + me // 2 % 2 * 2 + q % 2
-        tail = got_ref[place, 112:, :].astype(F32)
-        lists_ref[q : q + 1, :] = tail[8:9].astype(I32)
-        lists_ref[4 + q : 5 + q, :] = tail[9:10].astype(I32)
-
-
-def pack_body(one_ref, two_ref, out_ref, wide):
-    wide[...] = jnp.zeros_like(wide)
-    for g in range(3):
-        rest = jnp.zeros((RANK, 128), F32)
-        for s in range(4):
-            lanes = slice(128 * s, 128 * (s + 1))
-            if 4 * g + s == SLOTS[0]:
-                out_ref[g, :, lanes] = jnp.zeros((RANK, 128), BF16)
-                continue
-            block = one_ref[4 * g + s] if g < 2 else two_ref[s]
-            out_ref[g, :, lanes] = block[:, :128]
-            wide[:, :32] = block[:, 128:].astype(F32)
-            rest += wide[...] if s == 0 else pltpu.roll(wide[...], 32 * s, 1)
-        out_ref[g, :, 512:] = rest.astype(BF16)
+        tail = pltpu.roll(got_ref[place].astype(F32)[2 * PAD :], 96, 1)
+        lists_ref[q : q + 1, :] = tail[16:17].astype(I32)
+        lists_ref[4 + q : 5 + q, :] = tail[17:18].astype(I32)
 
 
 def couple_body(me_ref, lists_ref, up_ref, mid_ref, down_ref, own_ref, beside_ref, across_ref, opposite_ref, out_ref, rows, stack, wide):
@@ -224,11 +231,11 @@
     rows[1] = mid_ref[...]
     rows[2] = down_ref[...]
     lane = lax.broadcasted_iota(I32, (PAD, 128), 1)
-    sources = ((own_ref, q_own), (beside_ref, q_own ^ 2), (across_ref, q_own ^ 1), (opposite_ref, q_own ^ 3))
+    sources = ((own_ref, 0, q_own), (beside_ref, 0, q_own ^ 2), (across_ref, 432, q_own ^ 1), (opposite_ref, 0, q_own ^ 3))
     totals = [jnp.zeros((PAD, RANK), F32)] * 2
     for g in range(3):
         level = g // 2
-        for which, (ref, q) in enumerate(sources):
+        for which, (ref, start, q) in enumerate(sources):
             rest = jnp.zeros((PAD, 128), F32)
             for s in range(4):
                 if 4 * g + s == SLOTS[0]:
@@ -246,7 +253,9 @@
                 inside = (lane >= 32 * s) & (lane < jnp.where(valid, 32 * (s + 1), 0))
                 rest = jnp.where(inside, turned, rest)
             stack[which, g, :, 512:] = rest.astype(BF16)
-            totals[level] = totals[level] + mul_t(stack[which, g], ref[g])
+            main = ref[start + RANK * g : start + RANK * (g + 1), :]
+            last = ref[start + 3 * RANK : start + 4 * RANK, 128 * g : 128 * (g + 1)]
+            totals[level] = totals[level] + mul_t(stack[which, g, :, :512], main) + mul_t(stack[which, g, :, 512:], last)
     wide[...] = jnp.zeros_like(wide)
     block = packed(totals[0], totals[1], jnp.zeros((8, 128), F32), wide)
     for d in range(8):
@@ -261,10 +270,10 @@
         mine = got_ref[base + zl_own * 2].astype(F32)
         both = got_ref[base].astype(F32) + got_ref[base + 2].astype(F32)
         wide[:, :128] = both[PAD : 2 * PAD]
-        wide[:, 128:] = pltpu.roll(both[2 * PAD : 3 * PAD], 96, 1)
+        wide[:, 128:] = rest_of(both, 1)
         second = wide[:, :RANK].astype(BF16)
         wide[:, :128] = mine[:PAD]
-        wide[:, 128:] = mine[2 * PAD : 3 * PAD]
+        wide[:, 128:] = rest_of(mine, 0)
         local[PAD * q : PAD * (q + 1), :] = wide[:, :RANK] + mul_t(second, level_ref[...])
     one = mul(spreader(4, 144, True), local[...].astype(BF16)).astype(BF16)
     leaf = mul_t(one, one_ref[...]).astype(BF16)
@@ -278,34 +287,78 @@
     return found
 
 
-def mirror_body(me_ref, list_ref, x_ref, blocks_ref, left_ref, right_ref, below_ref):
+def side_body(me_ref, list_ref, x_ref, blocks_ref, chip_ref, cross_ref, below_ref):
     me = me_ref[0]
+    even = me % 2 == 0
     x = x_ref[...]
-    left_ref[0] = x
-    right_ref[0] = x
-    right_ref[1] = mul(x, blocks_ref[slot_of(list_ref, me, 1)]).astype(BF16)
-    left_ref[1] = mul(x, blocks_ref[slot_of(list_ref, me, 15)]).astype(BF16)
+    chip_ref[0:144] = x
+    cross_ref[0] = x
+    right_one = mul(x, blocks_ref[slot_of(list_ref, me, 1)]).astype(BF16)
+    right_two = mul(x, blocks_ref[slot_of(list_ref, me, 17)]).astype(BF16)
+    left = mul(x, blocks_ref[slot_of(list_ref, me, 15)]).astype(BF16)
     below_ref[...] = mul(x, blocks_ref[slot_of(list_ref, me, 16)]).astype(BF16)
-    right_ref[2] = mul(x, blocks_ref[slot_of(list_ref, me, 17)]).astype(BF16)
-
-
-def turn_body(x_ref, below_ref, from_right_ref, from_left_ref, rise_ref, sink_ref):
-    rise_ref[0] = from_left_ref[0]
+
+    @pl.when(even)
+    def _():
+        chip_ref[144:288] = right_one
+        chip_ref[288:432] = right_two
+        cross_ref[1] = left
+        cross_ref[2] = jnp.zeros_like(left)
+
+    @pl.when(jnp.logical_not(even))
+    def _():
+        cross_ref[1] = right_one
+        cross_ref[2] = right_two
+        chip_ref[144:288] = left
+        chip_ref[288:432] = jnp.zeros_like(left)
+
+
+def pack_body(one_ref, two_ref, own_ref, wide):
+    wide[...] = jnp.zeros_like(wide)
+    own_ref[3 * RANK :, 384:] = jnp.zeros((RANK, 128), BF16)
+    for g in range(3):
+        rest = jnp.zeros((RANK, 128), F32)
+        for s in range(4):
+            place = (slice(RANK * g, RANK * (g + 1)), slice(128 * s, 128 * (s + 1)))
+            if 4 * g + s == SLOTS[0]:
+                own_ref[place] = jnp.zeros((RANK, 128), BF16)
+                continue
+            block = one_ref[4 * g + s] if g < 2 else two_ref[s]
+            own_ref[place] = block[:, :128]
+            wide[:, :32] = block[:, 128:].astype(F32)
+            rest += wide[...] if s == 0 else pltpu.roll(wide[...], 32 * s, 1)
+        own_ref[3 * RANK :, 128 * g : 128 * (g + 1)] = rest.astype(BF16)
+
+
+def turn_body(me_ref, x_ref, below_ref, chip_ref, cross_ref, rise_ref, sink_ref, mirror_ref):
+    even = me_ref[0] % 2 == 0
     rise_ref[1] = x_ref[...]
-    rise_ref[2] = from_right_ref[0]
-    sink_ref[...] = (
-        below_ref[...].astype(F32) + from_left_ref[2].astype(F32) + from_right_ref[1].astype(F32)
-    ).astype(BF16)
-
-
-def near_body(me_ref, list_ref, x_ref, self_ref, blocks_ref, from_right_ref, from_left_ref, risen_ref, sunk_ref, out_ref):
+
+    @pl.when(even)
+    def _():
+        rise_ref[0] = cross_ref[0]
+        rise_ref[2] = chip_ref[0:144]
+        mirror_ref[...] = cross_ref[1]
+        sides = chip_ref[144:288].astype(F32) + cross_ref[2].astype(F32)
+        sink_ref[...] = (below_ref[...].astype(F32) + sides).astype(BF16)
+
+    @pl.when(jnp.logical_not(even))
+    def _():
+        rise_ref[0] = chip_ref[0:144]
+        rise_ref[2] = cross_ref[0]
+        mirror_ref[...] = chip_ref[144:288]
+        sides = cross_ref[1].astype(F32) + chip_ref[288:432].astype(F32)
+        sink_ref[...] = (below_ref[...].astype(F32) + sides).astype(BF16)
+
+
+def near_body(me_ref, list_ref, self_ref, blocks_ref, rise_ref, mirror_ref, risen_ref, sunk_ref, out_ref):
     me = me_ref[0]
-    total = mul_t(x_ref[...], self_ref[...])
-    total += mul_t(from_right_ref[0], blocks_ref[slot_of(list_ref, me, 1)])
+    total = mul_t(rise_ref[1], self_ref[...])
+    total += mul_t(rise_ref[2], blocks_ref[slot_of(list_ref, me, 1)])
     total += mul_t(risen_ref[0], blocks_ref[slot_of(list_ref, me, 15)])
     total += mul_t(risen_ref[1], blocks_ref[slot_of(list_ref, me, 16)])
     total += mul_t(risen_ref[2], blocks_ref[slot_of(list_ref, me, 17)])
-    out_ref[...] = total + from_left_ref[1].astype(F32) + sunk_ref[...].astype(F32)
+    out_ref[...] = total + mirror_ref[...].astype(F32) + sunk_ref[...].astype(F32)
 
 
 def shards(
@@ -332,31 +385,37 @@
     along_gx = ("y", "xh", "xl")
     swap = [(0, 1), (1, 0)]
 
-    message, left, right, below, own = fused(
+    message, own, chip, cross, below = fused(
         Stage(
             up_body,
-            [shape(16, 128, 128)],
+            [shape(16, ROWS, 128)],
             [pltpu.VMEM((2, PAD, 256), F32)],
             [x, vectors, one, transfer_two[0, 0]],
             lists=[far_list_one[0], far_list_two[0]],
             repeats={0: [d // 4 % 2 * 2 + d % 2 for d in range(16)]},
         ),
         Stage(
-            mirror_body,
-            [shape(2, 144, 512), shape(3, 144, 512), shape(144, 512)],
+            pack_body,
+            [shape(4 * RANK, 512)],
+            [pltpu.VMEM((RANK, 128), F32)],
+            [couple_one[0, 0], couple_two[0, 0]],
+            also=[(0, 2, 432)],
+        ),
+        Stage(
+            side_body,
+            [shape(1072, 512), shape(3, 144, 512), shape(144, 512)],
             [],
             [x, blocks],
             lists=[links],
             scalars=[me],
-        ),
-        Stage(
-            pack_body, [shape(3, RANK, 640)], [pltpu.VMEM((RANK, 128), F32)], [couple_one[0, 0], couple_two[0, 0]]
+            heads={0: 432},
         ),
         flops=4 * 10**8,
     )
     got = lax.all_to_all(message, ("xh", "xl", "zl", "c"), 0, 0)
-    from_right = lax.ppermute(left, across_gy, [(i + 1, i) for i in range(15)])
-    from_left = lax.ppermute(right, across_gy, [(i, i + 1) for i in range(15)])
+    from_chip = lax.ppermute(chip, "c", swap)
+    steps = [(i, i + 1) for i in range(1, 15, 2)] + [(i, i - 1) for i in range(2, 16, 2)]
+    from_cross = lax.ppermute(cross, across_gy, steps)
     beside = lax.ppermute(own, "xl", swap)
     window, level, codes = fused(
         Stage(
@@ -367,26 +426,28 @@
             scalars=[me],
             repeats={0: [0] * 4},
         ),
+        flops=6 * 10**9,
     )
     plane = lax.all_to_all(window, "zh", 0, 0)
-    below, late, _ = lax.optimization_barrier((below, own, window))
-    rise, sink = fused(
-        Stage(turn_body, [shape(3, 144, 512), shape(144, 512)], [], [x, below, from_right, from_left])
+    below, _ = lax.optimization_barrier((below, window))
+    rise, sink, mirror = fused(
+        Stage(
+            turn_body, [shape(3, 144, 512), shape(144, 512), shape(144, 512)], [], [x, below, from_chip, from_cross], scalars=[me]
+        )
     )
     risen = lax.ppermute(rise, along_gx, [(i + 1, i) for i in range(31)])
     sunk = lax.ppermute(sink, along_gx, [(i, i + 1) for i in range(31)])
-    across = lax.ppermute(late, "c", swap)
-    beside, _ = lax.optimization_barrier((beside, plane))
+    beside, _ = lax.optimization_barrier((beside, window))
     opposite = lax.ppermute(beside, "c", swap)
     above = lax.ppermute(plane, "y", [(i, i + 1) for i in range(7)])
     under = lax.ppermute(plane, "y", [(i + 1, i) for i in range(7)])
     near = call(
-        near_body, shape(144, 512, dtype=F32), [], [SMEM, SMEM] + [VMEM] * 7, 5 * 10**9, 4 * 10**6
-    )(me, links, x, near_self[0, 0], blocks, from_right, from_left, risen, sunk)
+        near_body, shape(144, 512, dtype=F32), [], [SMEM, SMEM] + [VMEM] * 6, 5 * 10**9, 4 * 10**6
+    )(me, links, near_self[0, 0], blocks, rise, mirror, risen, sunk)
     codes = after(codes, near)
     partial = call(
         couple_body,
-        shape(8, 128, 128),
+        shape(8, ROWS, 128),
         [
             pltpu.VMEM((3, 4, SLABS, PAD, 128), BF16),
             pltpu.VMEM((4, 3, PAD, 640), BF16),
@@ -395,7 +456,7 @@
         [SMEM, SMEM] + [VMEM] * 7,
         6 * 10**8,
         4 * 10**6,
-    )(me, codes, above, plane, under, own, beside, across, opposite)
+    )(me, codes, above, plane, under, own, beside, from_chip, opposite)
     sums = lax.all_to_all(partial, ("xl", "zl", "c"), 0, 0)
     applied = call(
         down_body,

time: 76.9 us -> 75.6 us (0.983)
  the two profiles are of different devices: /device:TPU:36 before, /device:TPU:28 now
where the time goes in v4:
time: 75.6 us; the launch traced here: 74.8 us
  starting transfers between devices  37.7 us (50%)
  Pallas kernels  14.8 us (20%)
  blocking collectives  11.4 us (15%)
  waiting for transfers between devices  5.95 us (8%)
  local copies, waits for them, and re-layouts  4.73 us (6%)
    all_to_all x1, blocking collectives, shards(): sums = lax.all_to_all(partial, ('xl', 'zl', 'c'), 0, 0)  11.4 us
    all_to_all x1, starting transfers between devices, shards(): plane = lax.all_to_all(window, 'zh', 0, 0)  9.9 us
    pallas_call x3, Pallas kernels, fused(): pl.pallas_call(run, out_shape=outs, in_specs=[ANY] * (len(shared) + len(l...  8.74 us
    all_to_all x1, starting transfers between devices, shards(): got = lax.all_to_all(message, ('xh', 'xl', 'zl', 'c'), 0, 0)  6.64 us
    unnamed x26, local copies, waits for them, and re-layouts  4.73 us
    ppermute x1, starting transfers between devices, shards(): above = lax.ppermute(plane, 'y', [(i, i + 1) for i in range(7)])  4.69 us
    ppermute x1, waiting for transfers between devices, shards(): under = lax.ppermute(plane, 'y', [(i + 1, i) for i in range(7)])  4.03 us
    ppermute x1, starting transfers between devices, shards(): sunk = lax.ppermute(sink, along_gx, [(i, i + 1) for i in range(31)])  3.64 us
  transfers between devices with their start and end apart: 10, of which 3 were waited for; matrix products, arithmetic and copies ran while one was open for 0% of the time, Pallas kernels for 9%

profile of v4, /device:TPU:28, one launch (start us, length us, event | category | flops | bytes accessed | tf_op | source)
XLA Modules:
  0.0 74.8 jit_solution(3159576869528566513)
XLA Ops:
  0.0 3.9 %shard_map.109 = (bf16[16,104,128]{2,1,0:T(8,128)(2,1)}, bf16[640,512]{1,0:T(8,128)(2,1)}, bf16[1072,512]{1,0:T(8,128)(2,1)}, bf16[3,144,512]{2,1,0:T(8,128)(2,1)}, bf16[144,512]{1,0:T(8,128)(2,1)}) custom-call(bf16[144,512]{1,0:T(8,128)(2,1)} %bitcast.28, bf16[160,512]{1,0:T(8,128)(2,1)} %bitcast.21, bf16[160,160]{1,0:T(8,128)(2,1)} %bitcast.23, ...), custom_call_target="tpu_custom_call" | custom-call | flops 400000000 | bytes 5804544 | tf_op jit(solution)/shard_map/pallas_call | solution.py:98
  3.9 6.6 %all-to-all-start = ((bf16[16,104,128]{2,1,0:T(8,128)(2,1)}), bf16[16,104,128]{2,1,0:T(8,128)(2,1)S(1)}, u32[]{:S(2)}, u32[]{:S(2)}) async-start(bf16[16,104,128]{2,1,0:T(8,128)(2,1)} %get-tuple-element.19), calls=%async_computation | async-start | bytes 851968 | tf_op jit(solution)/shard_map/all_to_all | solution.py:415
  10.5 2.0 %collective-permute-start = (bf16[1072,512]{1,0:T(8,128)(2,1)}, bf16[1072,512]{1,0:T(8,128)(2,1)S(1)}, u32[]{:S(2)}, u32[]{:S(2)}) collective-permute-start(bf16[1072,512]{1,0:T(8,128)(2,1)} %get-tuple-element.24), channel_id=1, source_target_pairs={{0,1},{1,0},{2,3},{3,2},{4,5},{5,4},{6,7},{7,6},{8,9},{9,8},{10,11... | collective-permute-start | bytes 3293192 | tf_op jit(solution)/shard_map/ppermute | solution.py:416
  12.6 1.4 %collective-permute-start.1 = (bf16[3,144,512]{2,1,0:T(8,128)(2,1)}, bf16[3,144,512]{2,1,0:T(8,128)(2,1)}, u32[]{:S(2)}, u32[]{:S(2)}) collective-permute-start(bf16[3,144,512]{2,1,0:T(8,128)(2,1)} %get-tuple-element.25), channel_id=1, source_target_pairs={{1,2},{3,4},{5,6},{7,8},{9,10},{11,12},{13,14},{2,1},{4,3},{6,5},{... | collective-permute-start | bytes 1327112 | tf_op jit(solution)/shard_map/ppermute | solution.py:418
  14.0 3.1 %collective-permute-start.6 = (bf16[640,512]{1,0:T(8,128)(2,1)}, bf16[640,512]{1,0:T(8,128)(2,1)}, u32[]{:S(2)}, u32[]{:S(2)}) collective-permute-start(bf16[640,512]{1,0:T(8,128)(2,1)} %get-tuple-element.30.own_ref), channel_id=1, source_target_pairs={{0,16},{16,0},{1,17},{17,1},{2,18},{18,2},{3,19},{19,3},{4,20},{20... | collective-permute-start | bytes 1966088 | tf_op jit(solution)/shard_map/ppermute | solution.py:419
  17.1 0.6 all-to-all-done.refs_0_
  17.7 0.0 copy-start.12
  17.7 0.8 %copy-done.12 = bf16[16,104,128]{2,1,0:T(8,128)(2,1)} copy-done((bf16[16,104,128]{2,1,0:T(8,128)(2,1)}, bf16[16,104,128]{2,1,0:T(8,128)(2,1)S(1)}, u32[]{:S(2)}) %copy-start.12) | copy-done | bytes 426008
  18.5 2.3 %shard_map.110 = (bf16[4,8,40,128]{3,2,1,0:T(8,128)(2,1)}, bf16[160,160]{1,0:T(8,128)(2,1)}, s32[8,128]{1,0:T(8,128)}) custom-call(bf16[16,104,128]{2,1,0:T(8,128)(2,1)} %copy-done.12, s32[1]{0:T(128)} %bitcast.refs_10_.refs_1_.refs_4_.me_ref), custom_call_target="tpu_custom_call" | custom-call | flops 6000000000 | bytes 808960 | tf_op jit(solution)/shard_map/pallas_call | solution.py:98
  20.9 0.0 copy-start.2
  20.9 0.0 copy-start.8
  20.9 9.9 %all-to-all-start.1 = ((bf16[4,8,40,128]{3,2,1,0:T(8,128)(2,1)}), bf16[4,8,40,128]{3,2,1,0:T(8,128)(2,1)S(1)}, u32[]{:S(2)}, u32[]{:S(2)}) async-start(bf16[4,8,40,128]{3,2,1,0:T(8,128)(2,1)} %get-tuple-element.22), calls=%async_computation.1 | async-start | bytes 655360 | tf_op jit(solution)/shard_map/all_to_all | solution.py:431
  30.8 0.0 collective-permute-done.1.refs_3_
  30.8 0.0 collective-permute-done.refs_2_.across_ref
  30.8 0.0 copy-start
  30.8 1.0 %copy-done = bf16[1072,512]{1,0:T(8,128)(2,1)} copy-done((bf16[1072,512]{1,0:T(8,128)(2,1)}, bf16[1072,512]{1,0:T(8,128)(2,1)S(1)}, u32[]{:S(2)}) %copy-start) | copy-done | bytes 1097752
  31.8 2.5 %shard_map.111 = (bf16[3,144,512]{2,1,0:T(8,128)(2,1)}, bf16[144,512]{1,0:T(8,128)(2,1)}, bf16[144,512]{1,0:T(8,128)(2,1)}) custom-call(bf16[144,512]{1,0:T(8,128)(2,1)} %bitcast.29, bf16[144,512]{1,0:T(8,128)(2,1)} %get-tuple-element.23.refs_1_, bf16[1072,512]{1,0:T(8,128)(2,1)} %copy-done, bf16[3,144,512]{2,1,0:T(8,128)(2,1)} %collective-permute-done.1.refs_3_, ...), custom_call_target="tpu_custom_call" | custom-call | flops 100000000 | bytes 2572288 | tf_op jit(solution)/shard_map/pallas_call | solution.py:98
  34.3 2.1 %collective-permute-start.2 = (bf16[3,144,512]{2,1,0:T(8,128)(2,1)}, bf16[3,144,512]{2,1,0:T(8,128)(2,1)}, u32[]{:S(2)}, u32[]{:S(2)}) collective-permute-start(bf16[3,144,512]{2,1,0:T(8,128)(2,1)} %get-tuple-element.26.rise_ref), channel_id=1, source_target_pairs={{16,0},{32,16},{48,32},{64,48},{80,64},{96,80},{112,96},{128,112},... | collective-permute-start | bytes 1327112 | tf_op jit(solution)/shard_map/ppermute | solution.py:438
  36.4 0.0 collective-permute-done.6.beside_ref
  36.4 2.2 %collective-permute-start.7 = (bf16[640,512]{1,0:T(8,128)(2,1)}, bf16[640,512]{1,0:T(8,128)(2,1)S(1)}, u32[]{:S(2)}, u32[]{:S(2)}) collective-permute-start(bf16[640,512]{1,0:T(8,128)(2,1)} %collective-permute-done.6.beside_ref), channel_id=1, source_target_pairs={{0,1},{1,0},{2,3},{3,2},{4,5},{5,4},{6,7},{7,6},{8,9},{9,8},{10,11... | collective-permute-start | bytes 1966088 | tf_op jit(solution)/shard_map/ppermute | solution.py:441
  38.7 3.6 %collective-permute-start.3 = (bf16[144,512]{1,0:T(8,128)(2,1)}, bf16[144,512]{1,0:T(8,128)(2,1)}, u32[]{:S(2)}, u32[]{:S(2)}) collective-permute-start(bf16[144,512]{1,0:T(8,128)(2,1)} %get-tuple-element.28), channel_id=1, source_target_pairs={{0,16},{16,32},{32,48},{48,64},{64,80},{80,96},{96,112},{112,128},... | collective-permute-start | bytes 442376 | tf_op jit(solution)/shard_map/ppermute | solution.py:439
  42.3 1.3 %all-to-all-done.1.mid_ref = bf16[4,8,40,128]{3,2,1,0:T(8,128)(2,1)S(1)} async-done(((bf16[4,8,40,128]{3,2,1,0:T(8,128)(2,1)}), bf16[4,8,40,128]{3,2,1,0:T(8,128)(2,1)S(1)}, u32[]{:S(2)}, u32[]{:S(2)}) %all-to-all-start.1) | async-done | bytes 327712 | tf_op jit(solution)/shard_map/all_to_all | solution.py:431
  43.6 4.7 %collective-permute-start.4 = (bf16[4,8,40,128]{3,2,1,0:T(8,128)(2,1)S(1)}, bf16[4,8,40,128]{3,2,1,0:T(8,128)(2,1)S(1)}, u32[]{:S(2)}, u32[]{:S(2)}) collective-permute-start(bf16[4,8,40,128]{3,2,1,0:T(8,128)(2,1)S(1)} %all-to-all-done.1.mid_ref), channel_id=1, source_target_pairs={{0,64},{64,128},{128,192},{192,256},{256,320},{320,384},{384,448},... | collective-permute-start | bytes 983048 | tf_op jit(solution)/shard_map/ppermute | solution.py:442
  48.3 1.9 %collective-permute-start.5 = (bf16[4,8,40,128]{3,2,1,0:T(8,128)(2,1)S(1)}, bf16[4,8,40,128]{3,2,1,0:T(8,128)(2,1)S(1)}, u32[]{:S(2)}, u32[]{:S(2)}) collective-permute-start(bf16[4,8,40,128]{3,2,1,0:T(8,128)(2,1)S(1)} %all-to-all-done.1.mid_ref), channel_id=1, source_target_pairs={{64,0},{128,64},{192,128},{256,192},{320,256},{384,320},{448,384},... | collective-permute-start | bytes 983048 | tf_op jit(solution)/shard_map/ppermute | solution.py:443
  50.2 0.0 collective-permute-done.3.sunk_ref
  50.2 0.0 collective-permute-done.2.risen_ref
  50.2 0.0 copy-done.2
  50.2 0.0 copy-done.8
  50.2 0.0 copy-start.9
  50.2 1.0 %copy-done.9 = bf16[1,1,512,512]{3,2,1,0:T(8,128)(2,1)S(1)} copy-done((bf16[1,1,512,512]{3,2,1,0:T(8,128)(2,1)S(1)}, bf16[1,1,512,512]{3,2,1,0:T(8,128)(2,1)}, u32[]{:S(2)}) %copy-start.9) | copy-done | bytes 524312
  51.3 0.0 copy-start.10
  51.3 1.0 %copy-done.10 = bf16[3,144,512]{2,1,0:T(8,128)(2,1)S(1)} copy-done((bf16[3,144,512]{2,1,0:T(8,128)(2,1)S(1)}, bf16[3,144,512]{2,1,0:T(8,128)(2,1)}, u32[]{:S(2)}) %copy-start.10) | copy-done | bytes 442392
  52.3 0.0 copy-start.11
  52.3 0.9 %copy-done.11 = bf16[144,512]{1,0:T(8,128)(2,1)S(1)} copy-done((bf16[144,512]{1,0:T(8,128)(2,1)S(1)}, bf16[144,512]{1,0:T(8,128)(2,1)}, u32[]{:S(2)}) %copy-start.11) | copy-done | bytes 147480
  53.2 0.0 copy-start.1
  53.2 0.0 copy-start.4
  53.2 0.0 copy-start.7
  53.2 2.2 %shard_map.112.near_ref = f32[144,512]{1,0:T(8,128)S(1)} custom-call(s32[1]{0:T(128)} %bitcast.refs_10_.refs_1_.refs_4_.me_ref, s32[1,4]{1,0:T(1,128)S(1)} %bitcast.26, bf16[512,512]{1,0:T(8,128)(2,1)S(1)} %bitcast.27, bf16[4,512,512]{2,1,0:T(8,128)(2,1)S(1)} %bitcast.20, bf16[3,144,512]{2,1,0:T(8,128)(2,1)S(1)} %copy-done.10, ...), custom_call_target="tpu_custom_call" | custom-call | flops 5000000000 | bytes 4000000 | tf_op jit(solution)/shard_map/pallas_call | solution.py:444
  55.4 0.0 copy-start.3
  55.4 0.0 copy-start.5
  55.4 0.0 copy-start.6
  55.4 0.0 collective-permute-done.7.opposite_ref
  55.4 0.0 collective-permute-done.4.up_ref
  55.4 4.0 %collective-permute-done.5.down_ref = bf16[4,8,40,128]{3,2,1,0:T(8,128)(2,1)S(1)} collective-permute-done((bf16[4,8,40,128]{3,2,1,0:T(8,128)(2,1)S(1)}, bf16[4,8,40,128]{3,2,1,0:T(8,128)(2,1)S(1)}, u32[]{:S(2)}, u32[]{:S(2)}) %collective-permute-start.5) | collective-permute-done | bytes 327712 | tf_op jit(solution)/shard_map/ppermute | solution.py:443
  59.5 0.0 copy-done.1
  59.5 0.0 copy-done.4
  59.5 0.0 copy-done.7
  59.5 2.6 %shard_map.113 = bf16[8,104,128]{2,1,0:T(8,128)(2,1)S(1)} custom-call(s32[1]{0:T(128)} %bitcast.refs_10_.refs_1_.refs_4_.me_ref, s32[8,128]{1,0:T(8,128)S(1)} %copy-done.7, bf16[4,8,40,128]{3,2,1,0:T(8,128)(2,1)S(1)} %collective-permute-done.4.up_ref, bf16[4,8,40,128]{3,2,1,0:T(8,128)(2,1)S(1)} %all-to-all-done.1.mid_ref, ...), custom_call_target="tpu_custom_call" | custom-call | flops 600000000 | bytes 4000000 | tf_op jit(solution)/shard_map/pallas_call | solution.py:448
  62.1 11.4 %all_to_all.15.got_ref = bf16[8,104,128]{2,1,0:T(8,128)(2,1)S(1)} all-to-all(bf16[8,104,128]{2,1,0:T(8,128)(2,1)S(1)} %shard_map.113), channel_id=1, replica_groups=mesh['y'=8,'xh'=2,'xl'=2,'zh'=4,'zl'=2,'c'=2] {'xl','zl','c'}, dimensions={0} | all-to-all | bytes 425984 | tf_op jit(solution)/shard_map/all_to_all | solution.py:460
  73.4 0.0 copy-done.3
  73.4 0.0 copy-done.5
  73.4 0.0 copy-done.6
  73.4 1.4 %shard_map.114 = bf16[144,512]{1,0:T(8,128)(2,1)} custom-call(s32[1]{0:T(128)} %bitcast.refs_10_.refs_1_.refs_4_.me_ref, bf16[8,104,128]{2,1,0:T(8,128)(2,1)S(1)} %all_to_all.15.got_ref, bf16[160,160]{1,0:T(8,128)(2,1)S(1)} %copy-done.6, bf16[160,160]{1,0:T(8,128)(2,1)S(1)} %bitcast.24, bf16[160,512]{1,0:T(8,128)(2,1)S(1)} %bitcast.22, ...), custom_call_target="tpu_custom_call" | custom-call | flops 100000000 | bytes 1000000 | tf_op jit(solution)/shard_map/pallas_call | solution.py:461
Async XLA Ops:
  3.9 13.9 %all-to-all-start = ((bf16[16,104,128]{2,1,0:T(8,128)(2,1)}), bf16[16,104,128]{2,1,0:T(8,128)(2,1)S(1)}, u32[]{:S(2)}, u32[]{:S(2)}) async-start(bf16[16,104,128]{2,1,0:T(8,128)(2,1)} %get-tuple-element.19), calls=%async_computation | async-start | bytes 851968 | tf_op jit(solution)/shard_map/all_to_all | solution.py:415
  10.5 20.3 %collective-permute-start = (bf16[1072,512]{1,0:T(8,128)(2,1)}, bf16[1072,512]{1,0:T(8,128)(2,1)S(1)}, u32[]{:S(2)}, u32[]{:S(2)}) collective-permute-start(bf16[1072,512]{1,0:T(8,128)(2,1)} %get-tuple-element.24), channel_id=1, source_target_pairs={{0,1},{1,0},{2,3},{3,2},{4,5},{5,4},{6,7},{7,6},{8,9},{9,8},{10,11... | collective-permute-start | bytes 3293192 | tf_op jit(solution)/shard_map/ppermute | solution.py:416
  12.6 18.2 %collective-permute-start.1 = (bf16[3,144,512]{2,1,0:T(8,128)(2,1)}, bf16[3,144,512]{2,1,0:T(8,128)(2,1)}, u32[]{:S(2)}, u32[]{:S(2)}) collective-permute-start(bf16[3,144,512]{2,1,0:T(8,128)(2,1)} %get-tuple-element.25), channel_id=1, source_target_pairs={{1,2},{3,4},{5,6},{7,8},{9,10},{11,12},{13,14},{2,1},{4,3},{6,5},{... | collective-permute-start | bytes 1327112 | tf_op jit(solution)/shard_map/ppermute | solution.py:418
  14.0 22.4 %collective-permute-start.6 = (bf16[640,512]{1,0:T(8,128)(2,1)}, bf16[640,512]{1,0:T(8,128)(2,1)}, u32[]{:S(2)}, u32[]{:S(2)}) collective-permute-start(bf16[640,512]{1,0:T(8,128)(2,1)} %get-tuple-element.30.own_ref), channel_id=1, source_target_pairs={{0,16},{16,0},{1,17},{17,1},{2,18},{18,2},{3,19},{19,3},{4,20},{20... | collective-permute-start | bytes 1966088 | tf_op jit(solution)/shard_map/ppermute | solution.py:419
  17.7 0.8 %copy-start.12 = (bf16[16,104,128]{2,1,0:T(8,128)(2,1)}, bf16[16,104,128]{2,1,0:T(8,128)(2,1)S(1)}, u32[]{:S(2)}) copy-start(bf16[16,104,128]{2,1,0:T(8,128)(2,1)S(1)} %all-to-all-done.refs_0_) | copy-start | bytes 1277956
  20.9 29.4 %copy-start.2 = (bf16[1,1,4,512,512]{4,3,2,1,0:T(8,128)(2,1)S(1)}, bf16[1,1,4,512,512]{4,3,2,1,0:T(8,128)(2,1)}, u32[]{:S(2)}) copy-start(bf16[1,1,4,512,512]{4,3,2,1,0:T(8,128)(2,1)} %param.13) | copy-start | bytes 6291460
  20.9 29.4 %copy-start.8 = (s32[1,1,4]{2,1,0:T(1,128)S(1)}, s32[1,1,4]{2,1,0:T(1,128)}, u32[]{:S(2)}) copy-start(s32[1,1,4]{2,1,0:T(1,128)} %param.14) | copy-start | bytes 52
  20.9 22.7 %all-to-all-start.1 = ((bf16[4,8,40,128]{3,2,1,0:T(8,128)(2,1)}), bf16[4,8,40,128]{3,2,1,0:T(8,128)(2,1)S(1)}, u32[]{:S(2)}, u32[]{:S(2)}) async-start(bf16[4,8,40,128]{3,2,1,0:T(8,128)(2,1)} %get-tuple-element.22), calls=%async_computation.1 | async-start | bytes 655360 | tf_op jit(solution)/shard_map/all_to_all | solution.py:431
  30.8 1.0 %copy-start = (bf16[1072,512]{1,0:T(8,128)(2,1)}, bf16[1072,512]{1,0:T(8,128)(2,1)S(1)}, u32[]{:S(2)}) copy-start(bf16[1072,512]{1,0:T(8,128)(2,1)S(1)} %collective-permute-done.refs_2_.across_ref) | copy-start | bytes 3293188
  34.3 15.9 %collective-permute-start.2 = (bf16[3,144,512]{2,1,0:T(8,128)(2,1)}, bf16[3,144,512]{2,1,0:T(8,128)(2,1)}, u32[]{:S(2)}, u32[]{:S(2)}) collective-permute-start(bf16[3,144,512]{2,1,0:T(8,128)(2,1)} %get-tuple-element.26.rise_ref), channel_id=1, source_target_pairs={{16,0},{32,16},{48,32},{64,48},{80,64},{96,80},{112,96},{128,112},... | collective-permute-start | bytes 1327112 | tf_op jit(solution)/shard_map/ppermute | solution.py:438
  36.4 19.0 %collective-permute-start.7 = (bf16[640,512]{1,0:T(8,128)(2,1)}, bf16[640,512]{1,0:T(8,128)(2,1)S(1)}, u32[]{:S(2)}, u32[]{:S(2)}) collective-permute-start(bf16[640,512]{1,0:T(8,128)(2,1)} %collective-permute-done.6.beside_ref), channel_id=1, source_target_pairs={{0,1},{1,0},{2,3},{3,2},{4,5},{5,4},{6,7},{7,6},{8,9},{9,8},{10,11... | collective-permute-start | bytes 1966088 | tf_op jit(solution)/shard_map/ppermute | solution.py:441
  38.7 11.5 %collective-permute-start.3 = (bf16[144,512]{1,0:T(8,128)(2,1)}, bf16[144,512]{1,0:T(8,128)(2,1)}, u32[]{:S(2)}, u32[]{:S(2)}) collective-permute-start(bf16[144,512]{1,0:T(8,128)(2,1)} %get-tuple-element.28), channel_id=1, source_target_pairs={{0,16},{16,32},{32,48},{48,64},{64,80},{80,96},{96,112},{112,128},... | collective-permute-start | bytes 442376 | tf_op jit(solution)/shard_map/ppermute | solution.py:439
  43.6 11.9 %collective-permute-start.4 = (bf16[4,8,40,128]{3,2,1,0:T(8,128)(2,1)S(1)}, bf16[4,8,40,128]{3,2,1,0:T(8,128)(2,1)S(1)}, u32[]{:S(2)}, u32[]{:S(2)}) collective-permute-start(bf16[4,8,40,128]{3,2,1,0:T(8,128)(2,1)S(1)} %all-to-all-done.1.mid_ref), channel_id=1, source_target_pairs={{0,64},{64,128},{128,192},{192,256},{256,320},{320,384},{384,448},... | collective-permute-start | bytes 983048 | tf_op jit(solution)/shard_map/ppermute | solution.py:442
  48.3 11.2 %collective-permute-start.5 = (bf16[4,8,40,128]{3,2,1,0:T(8,128)(2,1)S(1)}, bf16[4,8,40,128]{3,2,1,0:T(8,128)(2,1)S(1)}, u32[]{:S(2)}, u32[]{:S(2)}) collective-permute-start(bf16[4,8,40,128]{3,2,1,0:T(8,128)(2,1)S(1)} %all-to-all-done.1.mid_ref), channel_id=1, source_target_pairs={{64,0},{128,64},{192,128},{256,192},{320,256},{384,320},{448,384},... | collective-permute-start | bytes 983048 | tf_op jit(solution)/shard_map/ppermute | solution.py:443
  50.2 1.0 %copy-start.9 = (bf16[1,1,512,512]{3,2,1,0:T(8,128)(2,1)S(1)}, bf16[1,1,512,512]{3,2,1,0:T(8,128)(2,1)}, u32[]{:S(2)}) copy-start(bf16[1,1,512,512]{3,2,1,0:T(8,128)(2,1)} %param.12) | copy-start | bytes 1572868
  51.3 1.0 %copy-start.10 = (bf16[3,144,512]{2,1,0:T(8,128)(2,1)S(1)}, bf16[3,144,512]{2,1,0:T(8,128)(2,1)}, u32[]{:S(2)}) copy-start(bf16[3,144,512]{2,1,0:T(8,128)(2,1)} %get-tuple-element.26.rise_ref) | copy-start | bytes 1327108
  52.3 0.9 %copy-start.11 = (bf16[144,512]{1,0:T(8,128)(2,1)S(1)}, bf16[144,512]{1,0:T(8,128)(2,1)}, u32[]{:S(2)}) copy-start(bf16[144,512]{1,0:T(8,128)(2,1)} %get-tuple-element.27.mirror_ref) | copy-start | bytes 442372
  53.2 6.3 %copy-start.1 = (bf16[1072,512]{1,0:T(8,128)(2,1)S(1)}, bf16[1072,512]{1,0:T(8,128)(2,1)}, u32[]{:S(2)}) copy-start(bf16[1072,512]{1,0:T(8,128)(2,1)} %copy-done) | copy-start | bytes 3293188
  53.2 6.3 %copy-start.4 = (bf16[640,512]{1,0:T(8,128)(2,1)S(1)}, bf16[640,512]{1,0:T(8,128)(2,1)}, u32[]{:S(2)}) copy-start(bf16[640,512]{1,0:T(8,128)(2,1)} %get-tuple-element.30.own_ref) | copy-start | bytes 1966084
  53.2 6.3 %copy-start.7 = (s32[8,128]{1,0:T(8,128)S(1)}, s32[8,128]{1,0:T(8,128)}, u32[]{:S(2)}) copy-start(s32[8,128]{1,0:T(8,128)} %get-tuple-element.29.lists_ref) | copy-start | bytes 12292
  55.4 18.0 %copy-start.3 = (bf16[1,1,512,160]{2,3,1,0:T(8,128)(2,1)S(1)}, bf16[1,1,512,160]{2,3,1,0:T(8,128)(2,1)}, u32[]{:S(2)}) copy-start(bf16[1,1,512,160]{2,3,1,0:T(8,128)(2,1)} %param.15) | copy-start | bytes 491524
  55.4 18.0 %copy-start.5 = (bf16[1,1,160,160]{3,2,1,0:T(8,128)(2,1)S(1)}, bf16[1,1,160,160]{3,2,1,0:T(8,128)(2,1)}, u32[]{:S(2)}) copy-start(bf16[1,1,160,160]{3,2,1,0:T(8,128)(2,1)} %param.16) | copy-start | bytes 153604
  55.4 18.0 %copy-start.6 = (bf16[160,160]{1,0:T(8,128)(2,1)S(1)}, bf16[160,160]{1,0:T(8,128)(2,1)}, u32[]{:S(2)}) copy-start(bf16[160,160]{1,0:T(8,128)(2,1)} %get-tuple-element.32.level_ref) | copy-start | bytes 153604

commit v5 on v4

--- a/solution.py
+++ b/solution.py
@@ -18,10 +18,10 @@
 
 
 class Stage:
-    def __init__(self, body, outs, scratch, args, lists=(), scalars=(), repeats=None, heads=None, also=()):
+    def __init__(self, body, outs, scratch, args, lists=(), scalars=(), repeats=None, heads=None, also=(), direct=()):
         self.body, self.outs, self.scratch, self.args = body, outs, scratch, list(args)
         self.lists, self.scalars, self.repeats = list(lists), list(scalars), repeats or {}
-        self.heads, self.also = heads or {}, also
+        self.heads, self.also, self.direct = heads or {}, also, list(direct)
         self.ready = [
             shape(max(self.repeats[o]) + 1, *out.shape[1:], dtype=out.dtype)
             if o in self.repeats
@@ -43,6 +43,7 @@
     uses = [[index(a) for a in stage.args] for stage in stages]
     lists = [a for stage in stages for a in stage.lists]
     scalars = [a for stage in stages for a in stage.scalars]
+    directs = [a for stage in stages for a in stage.direct]
     outs = [o for stage in stages for o in stage.outs]
     ready = [o for stage in stages for o in stage.ready]
     n_copies = sum(len(stage.repeats.get(o, (0,))) for stage in stages for o in range(len(stage.outs)))
@@ -56,7 +57,8 @@
             del refs[:n]
             return taken
 
-        ins, tables, plain, results = take(len(shared)), take(len(lists)), take(len(scalars)), take(len(outs))
+        ins, tables, plain = take(len(shared)), take(len(lists)), take(len(scalars))
+        whole_ins, results = take(len(directs)), take(len(outs))
         held, read, buffers, in_sems, out_sems = take(len(shared)), take(len(lists)), take(len(outs)), *take(2)
         fetch = [
             pltpu.make_async_copy(source, target, in_sems.at[i])
@@ -75,7 +77,8 @@
             mine = [buffers.pop(0) for _ in stage.outs]
             targets = [results.pop(0) for _ in stage.outs]
             heads = [plain.pop(0) for _ in stage.scalars] + [read.pop(0) for _ in stage.lists]
-            stage.body(*heads, *[held[i] for i in use], *mine, *take(len(stage.scratch)))
+            given = [held[i] for i in use] + [whole_ins.pop(0) for _ in stage.direct]
+            stage.body(*heads, *given, *mine, *take(len(stage.scratch)))
             for o in range(len(stage.outs)):
                 whole = targets[o].at[pl.ds(0, stage.heads[o])] if o in stage.heads else targets[o]
                 pairs = [(mine[o], whole)]
@@ -98,12 +101,12 @@
     return pl.pallas_call(
         run,
         out_shape=outs,
-        in_specs=[ANY] * (len(shared) + len(lists)) + [SMEM] * len(scalars),
+        in_specs=[ANY] * (len(shared) + len(lists)) + [SMEM] * len(scalars) + [VMEM] * len(directs),
         out_specs=[ANY] * len(outs),
         scratch_shapes=buffers + [b for stage in stages for b in stage.scratch],
         compiler_params=pltpu.CompilerParams(vmem_limit_bytes=limit * 2**20),
         cost_estimate=pl.CostEstimate(flops=flops, bytes_accessed=moved, transcendentals=0),
-    )(*shared, *lists, *scalars)
+    )(*shared, *lists, *scalars, *directs)
 
 
 def call(body, outs, scratch, specs, flops, moved):
@@ -145,7 +148,7 @@
     return jnp.where(hit, 1.0, 0.0).astype(BF16)
 
 
-ROWS = 104
+ROWS = 112
 
 
 def packed(a, b, tail, wide):
@@ -158,11 +161,11 @@
         + pltpu.roll(second[:24], 64, 1)
         + pltpu.roll(jnp.concatenate([second[24:], jnp.zeros((8, 128), F32)], axis=0), 96, 1)
     )
-    return jnp.concatenate([wide[0, :, :128], wide[1, :, :128], rest], axis=0).astype(BF16)
+    return jnp.concatenate([wide[0, :, :128], wide[1, :, :128], rest, jnp.zeros((8, 128), F32)], axis=0).astype(BF16)
 
 
 def rest_of(block, which):
-    rest = block[2 * PAD :]
+    rest = block[2 * PAD : 2 * PAD + 24]
     left = pltpu.roll(rest, 64, 1) if which else rest
     return jnp.concatenate([left, pltpu.roll(left, 96, 1)[:16]], axis=0)
 
@@ -189,9 +192,10 @@
     own = (me // 32) % 2 * 2 + me // 2 % 2
     lane = lax.broadcasted_iota(I32, (PAD, 128), 1)
     rests = [jnp.zeros((PAD, 128), F32)] * 2
+    slabs = [None] * SLABS
 
     def deposit(level, place, main, rest):
-        window_ref[0, 5 * level + place] = main.astype(BF16)
+        slabs[5 * level + place] = main
         rest = jnp.where(lane < 32, rest, 0.0)
         rests[level] = rests[level] + (pltpu.roll(rest, 32 * place, 1) if place else rest)
 
@@ -213,12 +217,12 @@
             second += mul(first.astype(BF16), levels[xh * 2 + zl, :, :RANK].astype(BF16))
         wide[:, :RANK] = second
         deposit(1, xh, wide[:, :128], wide[:, 128:])
-    window_ref[0, 4] = rests[0].astype(BF16)
-    window_ref[0, 7] = rests[1].astype(BF16)
+    slabs[4], slabs[7] = rests
+    window_ref[0] = jnp.concatenate(slabs, axis=0).astype(BF16)
     level_ref[...] = levels[own, :, :RANK].astype(BF16)
     for q in range(4):
         place = (me // 32) % 2 * 8 + (q // 2) * 4 + me // 2 % 2 * 2 + q % 2
-        tail = pltpu.roll(got_ref[place].astype(F32)[2 * PAD :], 96, 1)
+        tail = pltpu.roll(got_ref[place].astype(F32)[2 * PAD : 2 * PAD + 24], 96, 1)
         lists_ref[q : q + 1, :] = tail[16:17].astype(I32)
         lists_ref[4 + q : 5 + q, :] = tail[17:18].astype(I32)
 
@@ -227,9 +231,11 @@
     me = me_ref[0]
     y = me // 64
     q_own = me // 16 % 2 * 2 + me % 2
-    rows[0] = up_ref[...]
-    rows[1] = mid_ref[...]
-    rows[2] = down_ref[...]
+    for p, ref in enumerate((up_ref, mid_ref, down_ref)):
+        for zh in range(4):
+            block = ref[zh].astype(F32)
+            for g in range(SLABS):
+                rows[p, zh, g] = block[PAD * g : PAD * (g + 1)]
     lane = lax.broadcasted_iota(I32, (PAD, 128), 1)
     sources = ((own_ref, 0, q_own), (beside_ref, 0, q_own ^ 2), (across_ref, 432, q_own ^ 1), (opposite_ref, 0, q_own ^ 3))
     totals = [jnp.zeros((PAD, RANK), F32)] * 2
@@ -247,9 +253,9 @@
                 row, col = (safe // 4, safe % 4) if level else (safe // 8, safe % 8)
                 zh, place = (col, row % 2) if level else (col // 2, row % 2 * 2 + col % 2)
                 plane = row // 2 - y + 1
-                main = rows[plane, zh, 5 * level + place].astype(F32)
+                main = rows[plane, zh, 5 * level + place]
                 stack[which, g, :, 128 * s : 128 * (s + 1)] = jnp.where(valid, main, 0.0).astype(BF16)
-                turned = pltpu.roll(rows[plane, zh, 4 + 3 * level].astype(F32), (s + 4 - place) % 4 * 32, 1)
+                turned = pltpu.roll(rows[plane, zh, 4 + 3 * level], (s + 4 - place) % 4 * 32, 1)
                 inside = (lane >= 32 * s) & (lane < jnp.where(valid, 32 * (s + 1), 0))
                 rest = jnp.where(inside, turned, rest)
             stack[which, g, :, 512:] = rest.astype(BF16)
@@ -390,7 +396,8 @@
             up_body,
             [shape(16, ROWS, 128)],
             [pltpu.VMEM((2, PAD, 256), F32)],
-            [x, vectors, one, transfer_two[0, 0]],
+            [x, vectors, one],
+            direct=[transfer_two[0, 0]],
             lists=[far_list_one[0], far_list_two[0]],
             repeats={0: [d // 4 % 2 * 2 + d % 2 for d in range(16)]},
         ),
@@ -420,7 +427,7 @@
     window, level, codes = fused(
         Stage(
             merge_body,
-            [shape(4, SLABS, PAD, 128), shape(RANK, RANK), shape(8, 128, dtype=I32)],
+            [shape(4, SLABS * PAD, 128), shape(RANK, RANK), shape(8, 128, dtype=I32)],
             [pltpu.VMEM((PAD, 256), F32), pltpu.VMEM((4, RANK, 256), F32)],
             [got],
             scalars=[me],
@@ -449,7 +456,7 @@
         couple_body,
         shape(8, ROWS, 128),
         [
-            pltpu.VMEM((3, 4, SLABS, PAD, 128), BF16),
+            pltpu.VMEM((3, 4, SLABS, PAD, 128), F32),
             pltpu.VMEM((4, 3, PAD, 640), BF16),
             pltpu.VMEM((2, PAD, 256), F32),
         ],

time: 75.6 us -> 76.7 us (1.015)
  Pallas kernels: 14.8 us -> 15.7 us
where the time goes in v5:
time: 76.7 us; the launch traced here: 75.8 us
  starting transfers between devices  37.3 us (49%)
  Pallas kernels  15.7 us (20%)
  blocking collectives  11.5 us (15%)
  waiting for transfers between devices  6.31 us (8%)
  local copies, waits for them, and re-layouts  4.79 us (6%)
    all_to_all x1, blocking collectives, shards(): sums = lax.all_to_all(partial, ('xl', 'zl', 'c'), 0, 0)  11.5 us
    all_to_all x1, starting transfers between devices, shards(): plane = lax.all_to_all(window, 'zh', 0, 0)  9.55 us
    pallas_call x3, Pallas kernels, fused(): pl.pallas_call(run, out_shape=outs, in_specs=[ANY] * (len(shared) + len(l...  9.45 us
    all_to_all x1, starting transfers between devices, shards(): got = lax.all_to_all(message, ('xh', 'xl', 'zl', 'c'), 0, 0)  6.64 us
    unnamed x26, local copies, waits for them, and re-layouts  4.79 us
    ppermute x1, starting transfers between devices, shards(): above = lax.ppermute(plane, 'y', [(i, i + 1) for i in range(7)])  4.68 us
    ppermute x1, waiting for transfers between devices, shards(): under = lax.ppermute(plane, 'y', [(i + 1, i) for i in range(7)])  4.08 us
    ppermute x1, starting transfers between devices, shards(): sunk = lax.ppermute(sink, along_gx, [(i, i + 1) for i in range(31)])  3.59 us
  transfers between devices with their start and end apart: 10, of which 3 were waited for; matrix products, arithmetic and copies ran while one was open for 0% of the time, Pallas kernels for 9%

profile of v5, /device:TPU:28, one launch (start us, length us, event | category | flops | bytes accessed | tf_op | source)
XLA Modules:
  0.0 75.8 jit_solution(16493964213018008004)
XLA Ops:
  0.0 4.6 %shard_map.109 = (bf16[16,112,128]{2,1,0:T(8,128)(2,1)}, bf16[640,512]{1,0:T(8,128)(2,1)}, bf16[1072,512]{1,0:T(8,128)(2,1)}, bf16[3,144,512]{2,1,0:T(8,128)(2,1)}, bf16[144,512]{1,0:T(8,128)(2,1)}) custom-call(bf16[144,512]{1,0:T(8,128)(2,1)} %bitcast.28, bf16[160,512]{1,0:T(8,128)(2,1)} %bitcast.21, bf16[160,160]{1,0:T(8,128)(2,1)} %bitcast.23, ...), custom_call_target="tpu_custom_call" | custom-call | flops 400000000 | bytes 5824512 | tf_op jit(solution)/shard_map/pallas_call | solution.py:101
  4.6 6.6 %all-to-all-start = ((bf16[16,112,128]{2,1,0:T(8,128)(2,1)}), bf16[16,112,128]{2,1,0:T(8,128)(2,1)S(1)}, u32[]{:S(2)}, u32[]{:S(2)}) async-start(bf16[16,112,128]{2,1,0:T(8,128)(2,1)} %get-tuple-element.19), calls=%async_computation | async-start | bytes 917504 | tf_op jit(solution)/shard_map/all_to_all | solution.py:422
  11.2 2.0 %collective-permute-start = (bf16[1072,512]{1,0:T(8,128)(2,1)}, bf16[1072,512]{1,0:T(8,128)(2,1)S(1)}, u32[]{:S(2)}, u32[]{:S(2)}) collective-permute-start(bf16[1072,512]{1,0:T(8,128)(2,1)} %get-tuple-element.24), channel_id=1, source_target_pairs={{0,1},{1,0},{2,3},{3,2},{4,5},{5,4},{6,7},{7,6},{8,9},{9,8},{10,11... | collective-permute-start | bytes 3293192 | tf_op jit(solution)/shard_map/ppermute | solution.py:423
  13.3 1.4 %collective-permute-start.1 = (bf16[3,144,512]{2,1,0:T(8,128)(2,1)}, bf16[3,144,512]{2,1,0:T(8,128)(2,1)}, u32[]{:S(2)}, u32[]{:S(2)}) collective-permute-start(bf16[3,144,512]{2,1,0:T(8,128)(2,1)} %get-tuple-element.25), channel_id=1, source_target_pairs={{1,2},{3,4},{5,6},{7,8},{9,10},{11,12},{13,14},{2,1},{4,3},{6,5},{... | collective-permute-start | bytes 1327112 | tf_op jit(solution)/shard_map/ppermute | solution.py:425
  14.7 3.1 %collective-permute-start.6 = (bf16[640,512]{1,0:T(8,128)(2,1)}, bf16[640,512]{1,0:T(8,128)(2,1)}, u32[]{:S(2)}, u32[]{:S(2)}) collective-permute-start(bf16[640,512]{1,0:T(8,128)(2,1)} %get-tuple-element.30.own_ref), channel_id=1, source_target_pairs={{0,16},{16,0},{1,17},{17,1},{2,18},{18,2},{3,19},{19,3},{4,20},{20... | collective-permute-start | bytes 1966088 | tf_op jit(solution)/shard_map/ppermute | solution.py:426
  17.8 1.0 %all-to-all-done.refs_0_ = bf16[16,112,128]{2,1,0:T(8,128)(2,1)S(1)} async-done(((bf16[16,112,128]{2,1,0:T(8,128)(2,1)}), bf16[16,112,128]{2,1,0:T(8,128)(2,1)S(1)}, u32[]{:S(2)}, u32[]{:S(2)}) %all-to-all-start) | async-done | bytes 458784 | tf_op jit(solution)/shard_map/all_to_all | solution.py:422
  18.8 0.0 copy-start.12
  18.8 0.8 %copy-done.12 = bf16[16,112,128]{2,1,0:T(8,128)(2,1)} copy-done((bf16[16,112,128]{2,1,0:T(8,128)(2,1)}, bf16[16,112,128]{2,1,0:T(8,128)(2,1)S(1)}, u32[]{:S(2)}) %copy-start.12) | copy-done | bytes 458776
  19.6 2.3 %shard_map.110 = (bf16[4,320,128]{2,1,0:T(8,128)(2,1)}, bf16[160,160]{1,0:T(8,128)(2,1)}, s32[8,128]{1,0:T(8,128)}) custom-call(bf16[16,112,128]{2,1,0:T(8,128)(2,1)} %copy-done.12, s32[1]{0:T(128)} %bitcast.refs_9_.refs_1_.refs_4_.me_ref), custom_call_target="tpu_custom_call" | custom-call | flops 6000000000 | bytes 841728 | tf_op jit(solution)/shard_map/pallas_call | solution.py:101
  21.9 0.0 copy-start.2
  21.9 0.0 copy-start.8
  22.0 9.6 %all-to-all-start.1 = ((bf16[4,320,128]{2,1,0:T(8,128)(2,1)}), bf16[4,320,128]{2,1,0:T(8,128)(2,1)S(1)}, u32[]{:S(2)}, u32[]{:S(2)}) async-start(bf16[4,320,128]{2,1,0:T(8,128)(2,1)} %get-tuple-element.22), calls=%async_computation.1 | async-start | bytes 655360 | tf_op jit(solution)/shard_map/all_to_all | solution.py:438
  31.5 0.0 collective-permute-done.1.refs_3_
  31.5 0.0 collective-permute-done.refs_2_.across_ref
  31.5 0.0 copy-start
  31.5 1.0 %copy-done = bf16[1072,512]{1,0:T(8,128)(2,1)} copy-done((bf16[1072,512]{1,0:T(8,128)(2,1)}, bf16[1072,512]{1,0:T(8,128)(2,1)S(1)}, u32[]{:S(2)}) %copy-start) | copy-done | bytes 1097752
  32.5 2.5 %shard_map.111 = (bf16[3,144,512]{2,1,0:T(8,128)(2,1)}, bf16[144,512]{1,0:T(8,128)(2,1)}, bf16[144,512]{1,0:T(8,128)(2,1)}) custom-call(bf16[144,512]{1,0:T(8,128)(2,1)} %bitcast.29, bf16[144,512]{1,0:T(8,128)(2,1)} %get-tuple-element.23.refs_1_, bf16[1072,512]{1,0:T(8,128)(2,1)} %copy-done, bf16[3,144,512]{2,1,0:T(8,128)(2,1)} %collective-permute-done.1.refs_3_, ...), custom_call_target="tpu_custom_call" | custom-call | flops 100000000 | bytes 2572288 | tf_op jit(solution)/shard_map/pallas_call | solution.py:101
  35.1 2.5 %collective-permute-start.2 = (bf16[3,144,512]{2,1,0:T(8,128)(2,1)}, bf16[3,144,512]{2,1,0:T(8,128)(2,1)}, u32[]{:S(2)}, u32[]{:S(2)}) collective-permute-start(bf16[3,144,512]{2,1,0:T(8,128)(2,1)} %get-tuple-element.26.rise_ref), channel_id=1, source_target_pairs={{16,0},{32,16},{48,32},{64,48},{80,64},{96,80},{112,96},{128,112},... | collective-permute-start | bytes 1327112 | tf_op jit(solution)/shard_map/ppermute | solution.py:445
  37.6 0.0 collective-permute-done.6.beside_ref
  37.6 1.9 %collective-permute-start.7 = (bf16[640,512]{1,0:T(8,128)(2,1)}, bf16[640,512]{1,0:T(8,128)(2,1)S(1)}, u32[]{:S(2)}, u32[]{:S(2)}) collective-permute-start(bf16[640,512]{1,0:T(8,128)(2,1)} %collective-permute-done.6.beside_ref), channel_id=1, source_target_pairs={{0,1},{1,0},{2,3},{3,2},{4,5},{5,4},{6,7},{7,6},{8,9},{9,8},{10,11... | collective-permute-start | bytes 1966088 | tf_op jit(solution)/shard_map/ppermute | solution.py:448
  39.5 3.6 %collective-permute-start.3 = (bf16[144,512]{1,0:T(8,128)(2,1)}, bf16[144,512]{1,0:T(8,128)(2,1)}, u32[]{:S(2)}, u32[]{:S(2)}) collective-permute-start(bf16[144,512]{1,0:T(8,128)(2,1)} %get-tuple-element.28), channel_id=1, source_target_pairs={{0,16},{16,32},{32,48},{48,64},{64,80},{80,96},{96,112},{112,128},... | collective-permute-start | bytes 442376 | tf_op jit(solution)/shard_map/ppermute | solution.py:446
  43.1 1.2 %all-to-all-done.1.mid_ref = bf16[4,320,128]{2,1,0:T(8,128)(2,1)S(1)} async-done(((bf16[4,320,128]{2,1,0:T(8,128)(2,1)}), bf16[4,320,128]{2,1,0:T(8,128)(2,1)S(1)}, u32[]{:S(2)}, u32[]{:S(2)}) %all-to-all-start.1) | async-done | bytes 327712 | tf_op jit(solution)/shard_map/all_to_all | solution.py:438
  44.3 4.7 %collective-permute-start.4 = (bf16[4,320,128]{2,1,0:T(8,128)(2,1)S(1)}, bf16[4,320,128]{2,1,0:T(8,128)(2,1)S(1)}, u32[]{:S(2)}, u32[]{:S(2)}) collective-permute-start(bf16[4,320,128]{2,1,0:T(8,128)(2,1)S(1)} %all-to-all-done.1.mid_ref), channel_id=1, source_target_pairs={{0,64},{64,128},{128,192},{192,256},{256,320},{320,384},{384,448},... | collective-permute-start | bytes 983048 | tf_op jit(solution)/shard_map/ppermute | solution.py:449
  49.0 1.9 %collective-permute-start.5 = (bf16[4,320,128]{2,1,0:T(8,128)(2,1)S(1)}, bf16[4,320,128]{2,1,0:T(8,128)(2,1)S(1)}, u32[]{:S(2)}, u32[]{:S(2)}) collective-permute-start(bf16[4,320,128]{2,1,0:T(8,128)(2,1)S(1)} %all-to-all-done.1.mid_ref), channel_id=1, source_target_pairs={{64,0},{128,64},{192,128},{256,192},{320,256},{384,320},{448,384},... | collective-permute-start | bytes 983048 | tf_op jit(solution)/shard_map/ppermute | solution.py:450
  50.9 0.0 collective-permute-done.3.sunk_ref
  50.9 0.0 collective-permute-done.2.risen_ref
  50.9 0.0 copy-done.2
  50.9 0.0 copy-done.8
  51.0 0.0 copy-start.9
  51.0 1.0 %copy-done.9 = bf16[1,1,512,512]{3,2,1,0:T(8,128)(2,1)S(1)} copy-done((bf16[1,1,512,512]{3,2,1,0:T(8,128)(2,1)S(1)}, bf16[1,1,512,512]{3,2,1,0:T(8,128)(2,1)}, u32[]{:S(2)}) %copy-start.9) | copy-done | bytes 524312
  52.0 0.0 copy-start.10
  52.0 1.0 %copy-done.10 = bf16[3,144,512]{2,1,0:T(8,128)(2,1)S(1)} copy-done((bf16[3,144,512]{2,1,0:T(8,128)(2,1)S(1)}, bf16[3,144,512]{2,1,0:T(8,128)(2,1)}, u32[]{:S(2)}) %copy-start.10) | copy-done | bytes 442392
  53.0 0.0 copy-start.11
  53.0 0.9 %copy-done.11 = bf16[144,512]{1,0:T(8,128)(2,1)S(1)} copy-done((bf16[144,512]{1,0:T(8,128)(2,1)S(1)}, bf16[144,512]{1,0:T(8,128)(2,1)}, u32[]{:S(2)}) %copy-start.11) | copy-done | bytes 147480
  53.9 0.0 copy-start.1
  53.9 0.0 copy-start.4
  53.9 0.0 copy-start.7
  53.9 2.2 %shard_map.112.near_ref = f32[144,512]{1,0:T(8,128)S(1)} custom-call(s32[1]{0:T(128)} %bitcast.refs_9_.refs_1_.refs_4_.me_ref, s32[1,4]{1,0:T(1,128)S(1)} %bitcast.26, bf16[512,512]{1,0:T(8,128)(2,1)S(1)} %bitcast.27, bf16[4,512,512]{2,1,0:T(8,128)(2,1)S(1)} %bitcast.20, bf16[3,144,512]{2,1,0:T(8,128)(2,1)S(1)} %copy-done.10, ...), custom_call_target="tpu_custom_call" | custom-call | flops 5000000000 | bytes 4000000 | tf_op jit(solution)/shard_map/pallas_call | solution.py:451
  56.1 0.0 copy-start.3
  56.1 0.0 copy-start.5
  56.1 0.0 copy-start.6
  56.1 0.0 collective-permute-done.7.opposite_ref
  56.2 0.0 collective-permute-done.4.up_ref
  56.2 4.1 %collective-permute-done.5.down_ref = bf16[4,320,128]{2,1,0:T(8,128)(2,1)S(1)} collective-permute-done((bf16[4,320,128]{2,1,0:T(8,128)(2,1)S(1)}, bf16[4,320,128]{2,1,0:T(8,128)(2,1)S(1)}, u32[]{:S(2)}, u32[]{:S(2)}) %collective-permute-start.5) | collective-permute-done | bytes 327712 | tf_op jit(solution)/shard_map/ppermute | solution.py:450
  60.2 0.0 copy-done.1
  60.2 0.0 copy-done.4
  60.2 0.0 copy-done.7
  60.3 2.7 %shard_map.113 = bf16[8,112,128]{2,1,0:T(8,128)(2,1)S(1)} custom-call(s32[1]{0:T(128)} %bitcast.refs_9_.refs_1_.refs_4_.me_ref, s32[8,128]{1,0:T(8,128)S(1)} %copy-done.7, bf16[4,320,128]{2,1,0:T(8,128)(2,1)S(1)} %collective-permute-done.4.up_ref, bf16[4,320,128]{2,1,0:T(8,128)(2,1)S(1)} %all-to-all-done.1.mid_ref, ...), custom_call_target="tpu_custom_call" | custom-call | flops 600000000 | bytes 4000000 | tf_op jit(solution)/shard_map/pallas_call | solution.py:455
  62.9 11.5 %all_to_all.15.got_ref = bf16[8,112,128]{2,1,0:T(8,128)(2,1)S(1)} all-to-all(bf16[8,112,128]{2,1,0:T(8,128)(2,1)S(1)} %shard_map.113), channel_id=1, replica_groups=mesh['y'=8,'xh'=2,'xl'=2,'zh'=4,'zl'=2,'c'=2] {'xl','zl','c'}, dimensions={0} | all-to-all | bytes 458752 | tf_op jit(solution)/shard_map/all_to_all | solution.py:467
  74.5 0.0 copy-done.3
  74.5 0.0 copy-done.5
  74.5 0.0 copy-done.6
  74.5 1.4 %shard_map.114 = bf16[144,512]{1,0:T(8,128)(2,1)} custom-call(s32[1]{0:T(128)} %bitcast.refs_9_.refs_1_.refs_4_.me_ref, bf16[8,112,128]{2,1,0:T(8,128)(2,1)S(1)} %all_to_all.15.got_ref, bf16[160,160]{1,0:T(8,128)(2,1)S(1)} %copy-done.6, bf16[160,160]{1,0:T(8,128)(2,1)S(1)} %bitcast.24, bf16[160,512]{1,0:T(8,128)(2,1)S(1)} %bitcast.22, ...), custom_call_target="tpu_custom_call" | custom-call | flops 100000000 | bytes 1000000 | tf_op jit(solution)/shard_map/pallas_call | solution.py:468
Async XLA Ops:
  4.6 14.2 %all-to-all-start = ((bf16[16,112,128]{2,1,0:T(8,128)(2,1)}), bf16[16,112,128]{2,1,0:T(8,128)(2,1)S(1)}, u32[]{:S(2)}, u32[]{:S(2)}) async-start(bf16[16,112,128]{2,1,0:T(8,128)(2,1)} %get-tuple-element.19), calls=%async_computation | async-start | bytes 917504 | tf_op jit(solution)/shard_map/all_to_all | solution.py:422
  11.2 20.3 %collective-permute-start = (bf16[1072,512]{1,0:T(8,128)(2,1)}, bf16[1072,512]{1,0:T(8,128)(2,1)S(1)}, u32[]{:S(2)}, u32[]{:S(2)}) collective-permute-start(bf16[1072,512]{1,0:T(8,128)(2,1)} %get-tuple-element.24), channel_id=1, source_target_pairs={{0,1},{1,0},{2,3},{3,2},{4,5},{5,4},{6,7},{7,6},{8,9},{9,8},{10,11... | collective-permute-start | bytes 3293192 | tf_op jit(solution)/shard_map/ppermute | solution.py:423
  13.3 18.2 %collective-permute-start.1 = (bf16[3,144,512]{2,1,0:T(8,128)(2,1)}, bf16[3,144,512]{2,1,0:T(8,128)(2,1)}, u32[]{:S(2)}, u32[]{:S(2)}) collective-permute-start(bf16[3,144,512]{2,1,0:T(8,128)(2,1)} %get-tuple-element.25), channel_id=1, source_target_pairs={{1,2},{3,4},{5,6},{7,8},{9,10},{11,12},{13,14},{2,1},{4,3},{6,5},{... | collective-permute-start | bytes 1327112 | tf_op jit(solution)/shard_map/ppermute | solution.py:425
  14.7 22.8 %collective-permute-start.6 = (bf16[640,512]{1,0:T(8,128)(2,1)}, bf16[640,512]{1,0:T(8,128)(2,1)}, u32[]{:S(2)}, u32[]{:S(2)}) collective-permute-start(bf16[640,512]{1,0:T(8,128)(2,1)} %get-tuple-element.30.own_ref), channel_id=1, source_target_pairs={{0,16},{16,0},{1,17},{17,1},{2,18},{18,2},{3,19},{19,3},{4,20},{20... | collective-permute-start | bytes 1966088 | tf_op jit(solution)/shard_map/ppermute | solution.py:426
  18.8 0.8 %copy-start.12 = (bf16[16,112,128]{2,1,0:T(8,128)(2,1)}, bf16[16,112,128]{2,1,0:T(8,128)(2,1)S(1)}, u32[]{:S(2)}) copy-start(bf16[16,112,128]{2,1,0:T(8,128)(2,1)S(1)} %all-to-all-done.refs_0_) | copy-start | bytes 1376260
  21.9 29.0 %copy-start.2 = (bf16[1,1,4,512,512]{4,3,2,1,0:T(8,128)(2,1)S(1)}, bf16[1,1,4,512,512]{4,3,2,1,0:T(8,128)(2,1)}, u32[]{:S(2)}) copy-start(bf16[1,1,4,512,512]{4,3,2,1,0:T(8,128)(2,1)} %param.13) | copy-start | bytes 6291460
  21.9 29.0 %copy-start.8 = (s32[1,1,4]{2,1,0:T(1,128)S(1)}, s32[1,1,4]{2,1,0:T(1,128)}, u32[]{:S(2)}) copy-start(s32[1,1,4]{2,1,0:T(1,128)} %param.14) | copy-start | bytes 52
  22.0 22.3 %all-to-all-start.1 = ((bf16[4,320,128]{2,1,0:T(8,128)(2,1)}), bf16[4,320,128]{2,1,0:T(8,128)(2,1)S(1)}, u32[]{:S(2)}, u32[]{:S(2)}) async-start(bf16[4,320,128]{2,1,0:T(8,128)(2,1)} %get-tuple-element.22), calls=%async_computation.1 | async-start | bytes 655360 | tf_op jit(solution)/shard_map/all_to_all | solution.py:438
  31.5 1.0 %copy-start = (bf16[1072,512]{1,0:T(8,128)(2,1)}, bf16[1072,512]{1,0:T(8,128)(2,1)S(1)}, u32[]{:S(2)}) copy-start(bf16[1072,512]{1,0:T(8,128)(2,1)S(1)} %collective-permute-done.refs_2_.across_ref) | copy-start | bytes 3293188
  35.1 15.8 %collective-permute-start.2 = (bf16[3,144,512]{2,1,0:T(8,128)(2,1)}, bf16[3,144,512]{2,1,0:T(8,128)(2,1)}, u32[]{:S(2)}, u32[]{:S(2)}) collective-permute-start(bf16[3,144,512]{2,1,0:T(8,128)(2,1)} %get-tuple-element.26.rise_ref), channel_id=1, source_target_pairs={{16,0},{32,16},{48,32},{64,48},{80,64},{96,80},{112,96},{128,112},... | collective-permute-start | bytes 1327112 | tf_op jit(solution)/shard_map/ppermute | solution.py:445
  37.6 18.6 %collective-permute-start.7 = (bf16[640,512]{1,0:T(8,128)(2,1)}, bf16[640,512]{1,0:T(8,128)(2,1)S(1)}, u32[]{:S(2)}, u32[]{:S(2)}) collective-permute-start(bf16[640,512]{1,0:T(8,128)(2,1)} %collective-permute-done.6.beside_ref), channel_id=1, source_target_pairs={{0,1},{1,0},{2,3},{3,2},{4,5},{5,4},{6,7},{7,6},{8,9},{9,8},{10,11... | collective-permute-start | bytes 1966088 | tf_op jit(solution)/shard_map/ppermute | solution.py:448
  39.5 11.4 %collective-permute-start.3 = (bf16[144,512]{1,0:T(8,128)(2,1)}, bf16[144,512]{1,0:T(8,128)(2,1)}, u32[]{:S(2)}, u32[]{:S(2)}) collective-permute-start(bf16[144,512]{1,0:T(8,128)(2,1)} %get-tuple-element.28), channel_id=1, source_target_pairs={{0,16},{16,32},{32,48},{48,64},{64,80},{80,96},{96,112},{112,128},... | collective-permute-start | bytes 442376 | tf_op jit(solution)/shard_map/ppermute | solution.py:446
  44.3 11.9 %collective-permute-start.4 = (bf16[4,320,128]{2,1,0:T(8,128)(2,1)S(1)}, bf16[4,320,128]{2,1,0:T(8,128)(2,1)S(1)}, u32[]{:S(2)}, u32[]{:S(2)}) collective-permute-start(bf16[4,320,128]{2,1,0:T(8,128)(2,1)S(1)} %all-to-all-done.1.mid_ref), channel_id=1, source_target_pairs={{0,64},{64,128},{128,192},{192,256},{256,320},{320,384},{384,448},... | collective-permute-start | bytes 983048 | tf_op jit(solution)/shard_map/ppermute | solution.py:449
  49.0 11.3 %collective-permute-start.5 = (bf16[4,320,128]{2,1,0:T(8,128)(2,1)S(1)}, bf16[4,320,128]{2,1,0:T(8,128)(2,1)S(1)}, u32[]{:S(2)}, u32[]{:S(2)}) collective-permute-start(bf16[4,320,128]{2,1,0:T(8,128)(2,1)S(1)} %all-to-all-done.1.mid_ref), channel_id=1, source_target_pairs={{64,0},{128,64},{192,128},{256,192},{320,256},{384,320},{448,384},... | collective-permute-start | bytes 983048 | tf_op jit(solution)/shard_map/ppermute | solution.py:450
  51.0 1.0 %copy-start.9 = (bf16[1,1,512,512]{3,2,1,0:T(8,128)(2,1)S(1)}, bf16[1,1,512,512]{3,2,1,0:T(8,128)(2,1)}, u32[]{:S(2)}) copy-start(bf16[1,1,512,512]{3,2,1,0:T(8,128)(2,1)} %param.12) | copy-start | bytes 1572868
  52.0 1.0 %copy-start.10 = (bf16[3,144,512]{2,1,0:T(8,128)(2,1)S(1)}, bf16[3,144,512]{2,1,0:T(8,128)(2,1)}, u32[]{:S(2)}) copy-start(bf16[3,144,512]{2,1,0:T(8,128)(2,1)} %get-tuple-element.26.rise_ref) | copy-start | bytes 1327108
  53.0 0.9 %copy-start.11 = (bf16[144,512]{1,0:T(8,128)(2,1)S(1)}, bf16[144,512]{1,0:T(8,128)(2,1)}, u32[]{:S(2)}) copy-start(bf16[144,512]{1,0:T(8,128)(2,1)} %get-tuple-element.27.mirror_ref) | copy-start | bytes 442372
  53.9 6.3 %copy-start.1 = (bf16[1072,512]{1,0:T(8,128)(2,1)S(1)}, bf16[1072,512]{1,0:T(8,128)(2,1)}, u32[]{:S(2)}) copy-start(bf16[1072,512]{1,0:T(8,128)(2,1)} %copy-done) | copy-start | bytes 3293188
  53.9 6.3 %copy-start.4 = (bf16[640,512]{1,0:T(8,128)(2,1)S(1)}, bf16[640,512]{1,0:T(8,128)(2,1)}, u32[]{:S(2)}) copy-start(bf16[640,512]{1,0:T(8,128)(2,1)} %get-tuple-element.30.own_ref) | copy-start | bytes 1966084
  53.9 6.3 %copy-start.7 = (s32[8,128]{1,0:T(8,128)S(1)}, s32[8,128]{1,0:T(8,128)}, u32[]{:S(2)}) copy-start(s32[8,128]{1,0:T(8,128)} %get-tuple-element.29.lists_ref) | copy-start | bytes 12292
  56.1 18.3 %copy-start.3 = (bf16[1,1,512,160]{2,3,1,0:T(8,128)(2,1)S(1)}, bf16[1,1,512,160]{2,3,1,0:T(8,128)(2,1)}, u32[]{:S(2)}) copy-start(bf16[1,1,512,160]{2,3,1,0:T(8,128)(2,1)} %param.15) | copy-start | bytes 491524
  56.1 18.3 %copy-start.5 = (bf16[1,1,160,160]{3,2,1,0:T(8,128)(2,1)S(1)}, bf16[1,1,160,160]{3,2,1,0:T(8,128)(2,1)}, u32[]{:S(2)}) copy-start(bf16[1,1,160,160]{3,2,1,0:T(8,128)(2,1)} %param.16) | copy-start | bytes 153604
  56.1 18.3 %copy-start.6 = (bf16[160,160]{1,0:T(8,128)(2,1)S(1)}, bf16[160,160]{1,0:T(8,128)(2,1)}, u32[]{:S(2)}) copy-start(bf16[160,160]{1,0:T(8,128)(2,1)} %get-tuple-element.32.level_ref) | copy-start | bytes 153604

commit v6 on v5

--- a/solution.py
+++ b/solution.py
@@ -18,10 +18,11 @@
 
 
 class Stage:
-    def __init__(self, body, outs, scratch, args, lists=(), scalars=(), repeats=None, heads=None, also=(), direct=()):
+    def __init__(self, body, outs, scratch, args, lists=(), scalars=(), repeats=None, heads=None, also=(), direct=(), first_rows=None):
         self.body, self.outs, self.scratch, self.args = body, outs, scratch, list(args)
         self.lists, self.scalars, self.repeats = list(lists), list(scalars), repeats or {}
         self.heads, self.also, self.direct = heads or {}, also, list(direct)
+        self.first_rows = first_rows or {}
         self.ready = [
             shape(max(self.repeats[o]) + 1, *out.shape[1:], dtype=out.dtype)
             if o in self.repeats
@@ -41,6 +42,7 @@
         return len(shared) - 1
 
     uses = [[index(a) for a in stage.args] for stage in stages]
+    fetched = {use[i]: n for stage, use in zip(stages, uses) for i, n in stage.first_rows.items()}
     lists = [a for stage in stages for a in stage.lists]
     scalars = [a for stage in stages for a in stage.scalars]
     directs = [a for stage in stages for a in stage.direct]
@@ -60,9 +62,10 @@
         ins, tables, plain = take(len(shared)), take(len(lists)), take(len(scalars))
         whole_ins, results = take(len(directs)), take(len(outs))
         held, read, buffers, in_sems, out_sems = take(len(shared)), take(len(lists)), take(len(outs)), *take(2)
+        parts = [ref.at[pl.ds(0, fetched[i])] if i in fetched else ref for i, ref in enumerate(ins)]
         fetch = [
             pltpu.make_async_copy(source, target, in_sems.at[i])
-            for i, (source, target) in enumerate(zip(ins + tables, held + read))
+            for i, (source, target) in enumerate(zip(parts + tables, held + read))
         ]
         for copy in fetch:
             copy.start()
@@ -93,7 +96,7 @@
         for copy in leaving:
             copy.wait()
 
-    buffers = [pltpu.VMEM(a.shape, a.dtype) for a in shared]
+    buffers = [pltpu.VMEM((fetched.get(i, a.shape[0]), *a.shape[1:]), a.dtype) for i, a in enumerate(shared)]
     buffers += [pltpu.SMEM(a.shape, a.dtype) for a in lists]
     buffers += [pltpu.VMEM(a.shape, a.dtype) for a in ready]
     buffers += [pltpu.SemaphoreType.DMA((len(shared) + len(lists),)), pltpu.SemaphoreType.DMA((n_copies,))]
@@ -439,7 +442,7 @@
     below, _ = lax.optimization_barrier((below, window))
     rise, sink, mirror = fused(
         Stage(
-            turn_body, [shape(3, 144, 512), shape(144, 512), shape(144, 512)], [], [x, below, from_chip, from_cross], scalars=[me]
+            turn_body, [shape(3, 144, 512), shape(144, 512), shape(144, 512)], [], [x, below, from_chip, from_cross], scalars=[me], first_rows={2: 432}
         )
     )
     risen = lax.ppermute(rise, along_gx, [(i + 1, i) for i in range(31)])

time: 76.7 us -> 76.5 us (level)
  no operation moved by 1% of the time
where the time goes in v6:
time: 76.5 us; the launch traced here: 75.6 us
  starting transfers between devices  37.3 us (49%)
  Pallas kernels  15.5 us (20%)
  blocking collectives  11.5 us (15%)
  waiting for transfers between devices  6.31 us (8%)
  local copies, waits for them, and re-layouts  4.79 us (6%)
    all_to_all x1, blocking collectives, shards(): sums = lax.all_to_all(partial, ('xl', 'zl', 'c'), 0, 0)  11.5 us
    all_to_all x1, starting transfers between devices, shards(): plane = lax.all_to_all(window, 'zh', 0, 0)  9.55 us
    pallas_call x3, Pallas kernels, fused(): pl.pallas_call(run, out_shape=outs, in_specs=[ANY] * (len(shared) + len(l...  9.25 us
    all_to_all x1, starting transfers between devices, shards(): got = lax.all_to_all(message, ('xh', 'xl', 'zl', 'c'), 0, 0)  6.64 us
    unnamed x26, local copies, waits for them, and re-layouts  4.79 us
    ppermute x1, starting transfers between devices, shards(): above = lax.ppermute(plane, 'y', [(i, i + 1) for i in range(7)])  4.68 us
    ppermute x1, waiting for transfers between devices, shards(): under = lax.ppermute(plane, 'y', [(i + 1, i) for i in range(7)])  3.88 us
    ppermute x1, starting transfers between devices, shards(): sunk = lax.ppermute(sink, along_gx, [(i, i + 1) for i in range(31)])  3.59 us
  transfers between devices with their start and end apart: 10, of which 3 were waited for; matrix products, arithmetic and copies ran while one was open for 0% of the time, Pallas kernels for 9%

profile of v6, /device:TPU:28, one launch (start us, length us, event | category | flops | bytes accessed | tf_op | source)
XLA Modules:
  0.0 75.6 jit_solution(8589238327079050102)
XLA Ops:
  0.0 4.6 %shard_map.109 = (bf16[16,112,128]{2,1,0:T(8,128)(2,1)}, bf16[640,512]{1,0:T(8,128)(2,1)}, bf16[1072,512]{1,0:T(8,128)(2,1)}, bf16[3,144,512]{2,1,0:T(8,128)(2,1)}, bf16[144,512]{1,0:T(8,128)(2,1)}) custom-call(bf16[144,512]{1,0:T(8,128)(2,1)} %bitcast.28, bf16[160,512]{1,0:T(8,128)(2,1)} %bitcast.21, bf16[160,160]{1,0:T(8,128)(2,1)} %bitcast.23, ...), custom_call_target="tpu_custom_call" | custom-call | flops 400000000 | bytes 5824512 | tf_op jit(solution)/shard_map/pallas_call | solution.py:104
  4.6 6.6 %all-to-all-start = ((bf16[16,112,128]{2,1,0:T(8,128)(2,1)}), bf16[16,112,128]{2,1,0:T(8,128)(2,1)S(1)}, u32[]{:S(2)}, u32[]{:S(2)}) async-start(bf16[16,112,128]{2,1,0:T(8,128)(2,1)} %get-tuple-element.19), calls=%async_computation | async-start | bytes 917504 | tf_op jit(solution)/shard_map/all_to_all | solution.py:425
  11.2 2.0 %collective-permute-start = (bf16[1072,512]{1,0:T(8,128)(2,1)}, bf16[1072,512]{1,0:T(8,128)(2,1)S(1)}, u32[]{:S(2)}, u32[]{:S(2)}) collective-permute-start(bf16[1072,512]{1,0:T(8,128)(2,1)} %get-tuple-element.24), channel_id=1, source_target_pairs={{0,1},{1,0},{2,3},{3,2},{4,5},{5,4},{6,7},{7,6},{8,9},{9,8},{10,11... | collective-permute-start | bytes 3293192 | tf_op jit(solution)/shard_map/ppermute | solution.py:426
  13.3 1.4 %collective-permute-start.1 = (bf16[3,144,512]{2,1,0:T(8,128)(2,1)}, bf16[3,144,512]{2,1,0:T(8,128)(2,1)}, u32[]{:S(2)}, u32[]{:S(2)}) collective-permute-start(bf16[3,144,512]{2,1,0:T(8,128)(2,1)} %get-tuple-element.25), channel_id=1, source_target_pairs={{1,2},{3,4},{5,6},{7,8},{9,10},{11,12},{13,14},{2,1},{4,3},{6,5},{... | collective-permute-start | bytes 1327112 | tf_op jit(solution)/shard_map/ppermute | solution.py:428
  14.7 3.1 %collective-permute-start.6 = (bf16[640,512]{1,0:T(8,128)(2,1)}, bf16[640,512]{1,0:T(8,128)(2,1)}, u32[]{:S(2)}, u32[]{:S(2)}) collective-permute-start(bf16[640,512]{1,0:T(8,128)(2,1)} %get-tuple-element.30.own_ref), channel_id=1, source_target_pairs={{0,16},{16,0},{1,17},{17,1},{2,18},{18,2},{3,19},{19,3},{4,20},{20... | collective-permute-start | bytes 1966088 | tf_op jit(solution)/shard_map/ppermute | solution.py:429
  17.8 1.0 %all-to-all-done.refs_0_ = bf16[16,112,128]{2,1,0:T(8,128)(2,1)S(1)} async-done(((bf16[16,112,128]{2,1,0:T(8,128)(2,1)}), bf16[16,112,128]{2,1,0:T(8,128)(2,1)S(1)}, u32[]{:S(2)}, u32[]{:S(2)}) %all-to-all-start) | async-done | bytes 458784 | tf_op jit(solution)/shard_map/all_to_all | solution.py:425
  18.8 0.0 copy-start.12
  18.8 0.8 %copy-done.12 = bf16[16,112,128]{2,1,0:T(8,128)(2,1)} copy-done((bf16[16,112,128]{2,1,0:T(8,128)(2,1)}, bf16[16,112,128]{2,1,0:T(8,128)(2,1)S(1)}, u32[]{:S(2)}) %copy-start.12) | copy-done | bytes 458776
  19.6 2.3 %shard_map.110 = (bf16[4,320,128]{2,1,0:T(8,128)(2,1)}, bf16[160,160]{1,0:T(8,128)(2,1)}, s32[8,128]{1,0:T(8,128)}) custom-call(bf16[16,112,128]{2,1,0:T(8,128)(2,1)} %copy-done.12, s32[1]{0:T(128)} %bitcast.refs_9_.refs_1_.refs_4_.me_ref), custom_call_target="tpu_custom_call" | custom-call | flops 6000000000 | bytes 841728 | tf_op jit(solution)/shard_map/pallas_call | solution.py:104
  21.9 0.0 copy-start.2
  21.9 0.0 copy-start.8
  22.0 9.6 %all-to-all-start.1 = ((bf16[4,320,128]{2,1,0:T(8,128)(2,1)}), bf16[4,320,128]{2,1,0:T(8,128)(2,1)S(1)}, u32[]{:S(2)}, u32[]{:S(2)}) async-start(bf16[4,320,128]{2,1,0:T(8,128)(2,1)} %get-tuple-element.22), calls=%async_computation.1 | async-start | bytes 655360 | tf_op jit(solution)/shard_map/all_to_all | solution.py:441
  31.5 0.0 collective-permute-done.1.refs_3_
  31.5 0.0 collective-permute-done.refs_2_.across_ref
  31.5 0.0 copy-start
  31.5 1.0 %copy-done = bf16[1072,512]{1,0:T(8,128)(2,1)} copy-done((bf16[1072,512]{1,0:T(8,128)(2,1)}, bf16[1072,512]{1,0:T(8,128)(2,1)S(1)}, u32[]{:S(2)}) %copy-start) | copy-done | bytes 1097752
  32.5 2.3 %shard_map.111 = (bf16[3,144,512]{2,1,0:T(8,128)(2,1)}, bf16[144,512]{1,0:T(8,128)(2,1)}, bf16[144,512]{1,0:T(8,128)(2,1)}) custom-call(bf16[144,512]{1,0:T(8,128)(2,1)} %bitcast.29, bf16[144,512]{1,0:T(8,128)(2,1)} %get-tuple-element.23.refs_1_, bf16[1072,512]{1,0:T(8,128)(2,1)} %copy-done, bf16[3,144,512]{2,1,0:T(8,128)(2,1)} %collective-permute-done.1.refs_3_, ...), custom_call_target="tpu_custom_call" | custom-call | flops 100000000 | bytes 2572288 | tf_op jit(solution)/shard_map/pallas_call | solution.py:104
  34.9 2.5 %collective-permute-start.2 = (bf16[3,144,512]{2,1,0:T(8,128)(2,1)}, bf16[3,144,512]{2,1,0:T(8,128)(2,1)}, u32[]{:S(2)}, u32[]{:S(2)}) collective-permute-start(bf16[3,144,512]{2,1,0:T(8,128)(2,1)} %get-tuple-element.26.rise_ref), channel_id=1, source_target_pairs={{16,0},{32,16},{48,32},{64,48},{80,64},{96,80},{112,96},{128,112},... | collective-permute-start | bytes 1327112 | tf_op jit(solution)/shard_map/ppermute | solution.py:448
  37.4 0.0 collective-permute-done.6.beside_ref
  37.4 1.9 %collective-permute-start.7 = (bf16[640,512]{1,0:T(8,128)(2,1)}, bf16[640,512]{1,0:T(8,128)(2,1)S(1)}, u32[]{:S(2)}, u32[]{:S(2)}) collective-permute-start(bf16[640,512]{1,0:T(8,128)(2,1)} %collective-permute-done.6.beside_ref), channel_id=1, source_target_pairs={{0,1},{1,0},{2,3},{3,2},{4,5},{5,4},{6,7},{7,6},{8,9},{9,8},{10,11... | collective-permute-start | bytes 1966088 | tf_op jit(solution)/shard_map/ppermute | solution.py:451
  39.3 3.6 %collective-permute-start.3 = (bf16[144,512]{1,0:T(8,128)(2,1)}, bf16[144,512]{1,0:T(8,128)(2,1)}, u32[]{:S(2)}, u32[]{:S(2)}) collective-permute-start(bf16[144,512]{1,0:T(8,128)(2,1)} %get-tuple-element.28), channel_id=1, source_target_pairs={{0,16},{16,32},{32,48},{48,64},{64,80},{80,96},{96,112},{112,128},... | collective-permute-start | bytes 442376 | tf_op jit(solution)/shard_map/ppermute | solution.py:449
  42.9 1.4 %all-to-all-done.1.mid_ref = bf16[4,320,128]{2,1,0:T(8,128)(2,1)S(1)} async-done(((bf16[4,320,128]{2,1,0:T(8,128)(2,1)}), bf16[4,320,128]{2,1,0:T(8,128)(2,1)S(1)}, u32[]{:S(2)}, u32[]{:S(2)}) %all-to-all-start.1) | async-done | bytes 327712 | tf_op jit(solution)/shard_map/all_to_all | solution.py:441
  44.3 4.7 %collective-permute-start.4 = (bf16[4,320,128]{2,1,0:T(8,128)(2,1)S(1)}, bf16[4,320,128]{2,1,0:T(8,128)(2,1)S(1)}, u32[]{:S(2)}, u32[]{:S(2)}) collective-permute-start(bf16[4,320,128]{2,1,0:T(8,128)(2,1)S(1)} %all-to-all-done.1.mid_ref), channel_id=1, source_target_pairs={{0,64},{64,128},{128,192},{192,256},{256,320},{320,384},{384,448},... | collective-permute-start | bytes 983048 | tf_op jit(solution)/shard_map/ppermute | solution.py:452
  49.0 1.9 %collective-permute-start.5 = (bf16[4,320,128]{2,1,0:T(8,128)(2,1)S(1)}, bf16[4,320,128]{2,1,0:T(8,128)(2,1)S(1)}, u32[]{:S(2)}, u32[]{:S(2)}) collective-permute-start(bf16[4,320,128]{2,1,0:T(8,128)(2,1)S(1)} %all-to-all-done.1.mid_ref), channel_id=1, source_target_pairs={{64,0},{128,64},{192,128},{256,192},{320,256},{384,320},{448,384},... | collective-permute-start | bytes 983048 | tf_op jit(solution)/shard_map/ppermute | solution.py:453
  50.9 0.0 collective-permute-done.3.sunk_ref
  50.9 0.0 collective-permute-done.2.risen_ref
  50.9 0.0 copy-done.2
  50.9 0.0 copy-done.8
  51.0 0.0 copy-start.9
  51.0 1.0 %copy-done.9 = bf16[1,1,512,512]{3,2,1,0:T(8,128)(2,1)S(1)} copy-done((bf16[1,1,512,512]{3,2,1,0:T(8,128)(2,1)S(1)}, bf16[1,1,512,512]{3,2,1,0:T(8,128)(2,1)}, u32[]{:S(2)}) %copy-start.9) | copy-done | bytes 524312
  52.0 0.0 copy-start.10
  52.0 1.0 %copy-done.10 = bf16[3,144,512]{2,1,0:T(8,128)(2,1)S(1)} copy-done((bf16[3,144,512]{2,1,0:T(8,128)(2,1)S(1)}, bf16[3,144,512]{2,1,0:T(8,128)(2,1)}, u32[]{:S(2)}) %copy-start.10) | copy-done | bytes 442392
  53.0 0.0 copy-start.11
  53.0 0.9 %copy-done.11 = bf16[144,512]{1,0:T(8,128)(2,1)S(1)} copy-done((bf16[144,512]{1,0:T(8,128)(2,1)S(1)}, bf16[144,512]{1,0:T(8,128)(2,1)}, u32[]{:S(2)}) %copy-start.11) | copy-done | bytes 147480
  53.9 0.0 copy-start.1
  53.9 0.0 copy-start.4
  53.9 0.0 copy-start.7
  53.9 2.2 %shard_map.112.near_ref = f32[144,512]{1,0:T(8,128)S(1)} custom-call(s32[1]{0:T(128)} %bitcast.refs_9_.refs_1_.refs_4_.me_ref, s32[1,4]{1,0:T(1,128)S(1)} %bitcast.26, bf16[512,512]{1,0:T(8,128)(2,1)S(1)} %bitcast.27, bf16[4,512,512]{2,1,0:T(8,128)(2,1)S(1)} %bitcast.20, bf16[3,144,512]{2,1,0:T(8,128)(2,1)S(1)} %copy-done.10, ...), custom_call_target="tpu_custom_call" | custom-call | flops 5000000000 | bytes 4000000 | tf_op jit(solution)/shard_map/pallas_call | solution.py:454
  56.1 0.0 copy-start.3
  56.1 0.0 copy-start.5
  56.1 0.0 copy-start.6
  56.1 0.0 collective-permute-done.7.opposite_ref
  56.2 0.0 collective-permute-done.4.up_ref
  56.2 3.9 %collective-permute-done.5.down_ref = bf16[4,320,128]{2,1,0:T(8,128)(2,1)S(1)} collective-permute-done((bf16[4,320,128]{2,1,0:T(8,128)(2,1)S(1)}, bf16[4,320,128]{2,1,0:T(8,128)(2,1)S(1)}, u32[]{:S(2)}, u32[]{:S(2)}) %collective-permute-start.5) | collective-permute-done | bytes 327712 | tf_op jit(solution)/shard_map/ppermute | solution.py:453
  60.0 0.0 copy-done.1
  60.0 0.0 copy-done.4
  60.0 0.0 copy-done.7
  60.1 2.7 %shard_map.113 = bf16[8,112,128]{2,1,0:T(8,128)(2,1)S(1)} custom-call(s32[1]{0:T(128)} %bitcast.refs_9_.refs_1_.refs_4_.me_ref, s32[8,128]{1,0:T(8,128)S(1)} %copy-done.7, bf16[4,320,128]{2,1,0:T(8,128)(2,1)S(1)} %collective-permute-done.4.up_ref, bf16[4,320,128]{2,1,0:T(8,128)(2,1)S(1)} %all-to-all-done.1.mid_ref, ...), custom_call_target="tpu_custom_call" | custom-call | flops 600000000 | bytes 4000000 | tf_op jit(solution)/shard_map/pallas_call | solution.py:458
  62.7 11.5 %all_to_all.15.got_ref = bf16[8,112,128]{2,1,0:T(8,128)(2,1)S(1)} all-to-all(bf16[8,112,128]{2,1,0:T(8,128)(2,1)S(1)} %shard_map.113), channel_id=1, replica_groups=mesh['y'=8,'xh'=2,'xl'=2,'zh'=4,'zl'=2,'c'=2] {'xl','zl','c'}, dimensions={0} | all-to-all | bytes 458752 | tf_op jit(solution)/shard_map/all_to_all | solution.py:470
  74.3 0.0 copy-done.3
  74.3 0.0 copy-done.5
  74.3 0.0 copy-done.6
  74.3 1.4 %shard_map.114 = bf16[144,512]{1,0:T(8,128)(2,1)} custom-call(s32[1]{0:T(128)} %bitcast.refs_9_.refs_1_.refs_4_.me_ref, bf16[8,112,128]{2,1,0:T(8,128)(2,1)S(1)} %all_to_all.15.got_ref, bf16[160,160]{1,0:T(8,128)(2,1)S(1)} %copy-done.6, bf16[160,160]{1,0:T(8,128)(2,1)S(1)} %bitcast.24, bf16[160,512]{1,0:T(8,128)(2,1)S(1)} %bitcast.22, ...), custom_call_target="tpu_custom_call" | custom-call | flops 100000000 | bytes 1000000 | tf_op jit(solution)/shard_map/pallas_call | solution.py:471
Async XLA Ops:
  4.6 14.2 %all-to-all-start = ((bf16[16,112,128]{2,1,0:T(8,128)(2,1)}), bf16[16,112,128]{2,1,0:T(8,128)(2,1)S(1)}, u32[]{:S(2)}, u32[]{:S(2)}) async-start(bf16[16,112,128]{2,1,0:T(8,128)(2,1)} %get-tuple-element.19), calls=%async_computation | async-start | bytes 917504 | tf_op jit(solution)/shard_map/all_to_all | solution.py:425
  11.2 20.3 %collective-permute-start = (bf16[1072,512]{1,0:T(8,128)(2,1)}, bf16[1072,512]{1,0:T(8,128)(2,1)S(1)}, u32[]{:S(2)}, u32[]{:S(2)}) collective-permute-start(bf16[1072,512]{1,0:T(8,128)(2,1)} %get-tuple-element.24), channel_id=1, source_target_pairs={{0,1},{1,0},{2,3},{3,2},{4,5},{5,4},{6,7},{7,6},{8,9},{9,8},{10,11... | collective-permute-start | bytes 3293192 | tf_op jit(solution)/shard_map/ppermute | solution.py:426
  13.3 18.2 %collective-permute-start.1 = (bf16[3,144,512]{2,1,0:T(8,128)(2,1)}, bf16[3,144,512]{2,1,0:T(8,128)(2,1)}, u32[]{:S(2)}, u32[]{:S(2)}) collective-permute-start(bf16[3,144,512]{2,1,0:T(8,128)(2,1)} %get-tuple-element.25), channel_id=1, source_target_pairs={{1,2},{3,4},{5,6},{7,8},{9,10},{11,12},{13,14},{2,1},{4,3},{6,5},{... | collective-permute-start | bytes 1327112 | tf_op jit(solution)/shard_map/ppermute | solution.py:428
  14.7 22.6 %collective-permute-start.6 = (bf16[640,512]{1,0:T(8,128)(2,1)}, bf16[640,512]{1,0:T(8,128)(2,1)}, u32[]{:S(2)}, u32[]{:S(2)}) collective-permute-start(bf16[640,512]{1,0:T(8,128)(2,1)} %get-tuple-element.30.own_ref), channel_id=1, source_target_pairs={{0,16},{16,0},{1,17},{17,1},{2,18},{18,2},{3,19},{19,3},{4,20},{20... | collective-permute-start | bytes 1966088 | tf_op jit(solution)/shard_map/ppermute | solution.py:429
  18.8 0.8 %copy-start.12 = (bf16[16,112,128]{2,1,0:T(8,128)(2,1)}, bf16[16,112,128]{2,1,0:T(8,128)(2,1)S(1)}, u32[]{:S(2)}) copy-start(bf16[16,112,128]{2,1,0:T(8,128)(2,1)S(1)} %all-to-all-done.refs_0_) | copy-start | bytes 1376260
  21.9 29.0 %copy-start.2 = (bf16[1,1,4,512,512]{4,3,2,1,0:T(8,128)(2,1)S(1)}, bf16[1,1,4,512,512]{4,3,2,1,0:T(8,128)(2,1)}, u32[]{:S(2)}) copy-start(bf16[1,1,4,512,512]{4,3,2,1,0:T(8,128)(2,1)} %param.13) | copy-start | bytes 6291460
  21.9 29.0 %copy-start.8 = (s32[1,1,4]{2,1,0:T(1,128)S(1)}, s32[1,1,4]{2,1,0:T(1,128)}, u32[]{:S(2)}) copy-start(s32[1,1,4]{2,1,0:T(1,128)} %param.14) | copy-start | bytes 52
  22.0 22.3 %all-to-all-start.1 = ((bf16[4,320,128]{2,1,0:T(8,128)(2,1)}), bf16[4,320,128]{2,1,0:T(8,128)(2,1)S(1)}, u32[]{:S(2)}, u32[]{:S(2)}) async-start(bf16[4,320,128]{2,1,0:T(8,128)(2,1)} %get-tuple-element.22), calls=%async_computation.1 | async-start | bytes 655360 | tf_op jit(solution)/shard_map/all_to_all | solution.py:441
  31.5 1.0 %copy-start = (bf16[1072,512]{1,0:T(8,128)(2,1)}, bf16[1072,512]{1,0:T(8,128)(2,1)S(1)}, u32[]{:S(2)}) copy-start(bf16[1072,512]{1,0:T(8,128)(2,1)S(1)} %collective-permute-done.refs_2_.across_ref) | copy-start | bytes 3293188
  34.9 16.0 %collective-permute-start.2 = (bf16[3,144,512]{2,1,0:T(8,128)(2,1)}, bf16[3,144,512]{2,1,0:T(8,128)(2,1)}, u32[]{:S(2)}, u32[]{:S(2)}) collective-permute-start(bf16[3,144,512]{2,1,0:T(8,128)(2,1)} %get-tuple-element.26.rise_ref), channel_id=1, source_target_pairs={{16,0},{32,16},{48,32},{64,48},{80,64},{96,80},{112,96},{128,112},... | collective-permute-start | bytes 1327112 | tf_op jit(solution)/shard_map/ppermute | solution.py:448
  37.4 18.8 %collective-permute-start.7 = (bf16[640,512]{1,0:T(8,128)(2,1)}, bf16[640,512]{1,0:T(8,128)(2,1)S(1)}, u32[]{:S(2)}, u32[]{:S(2)}) collective-permute-start(bf16[640,512]{1,0:T(8,128)(2,1)} %collective-permute-done.6.beside_ref), channel_id=1, source_target_pairs={{0,1},{1,0},{2,3},{3,2},{4,5},{5,4},{6,7},{7,6},{8,9},{9,8},{10,11... | collective-permute-start | bytes 1966088 | tf_op jit(solution)/shard_map/ppermute | solution.py:451
  39.3 11.6 %collective-permute-start.3 = (bf16[144,512]{1,0:T(8,128)(2,1)}, bf16[144,512]{1,0:T(8,128)(2,1)}, u32[]{:S(2)}, u32[]{:S(2)}) collective-permute-start(bf16[144,512]{1,0:T(8,128)(2,1)} %get-tuple-element.28), channel_id=1, source_target_pairs={{0,16},{16,32},{32,48},{48,64},{64,80},{80,96},{96,112},{112,128},... | collective-permute-start | bytes 442376 | tf_op jit(solution)/shard_map/ppermute | solution.py:449
  44.3 11.9 %collective-permute-start.4 = (bf16[4,320,128]{2,1,0:T(8,128)(2,1)S(1)}, bf16[4,320,128]{2,1,0:T(8,128)(2,1)S(1)}, u32[]{:S(2)}, u32[]{:S(2)}) collective-permute-start(bf16[4,320,128]{2,1,0:T(8,128)(2,1)S(1)} %all-to-all-done.1.mid_ref), channel_id=1, source_target_pairs={{0,64},{64,128},{128,192},{192,256},{256,320},{320,384},{384,448},... | collective-permute-start | bytes 983048 | tf_op jit(solution)/shard_map/ppermute | solution.py:452
  49.0 11.1 %collective-permute-start.5 = (bf16[4,320,128]{2,1,0:T(8,128)(2,1)S(1)}, bf16[4,320,128]{2,1,0:T(8,128)(2,1)S(1)}, u32[]{:S(2)}, u32[]{:S(2)}) collective-permute-start(bf16[4,320,128]{2,1,0:T(8,128)(2,1)S(1)} %all-to-all-done.1.mid_ref), channel_id=1, source_target_pairs={{64,0},{128,64},{192,128},{256,192},{320,256},{384,320},{448,384},... | collective-permute-start | bytes 983048 | tf_op jit(solution)/shard_map/ppermute | solution.py:453
  51.0 1.0 %copy-start.9 = (bf16[1,1,512,512]{3,2,1,0:T(8,128)(2,1)S(1)}, bf16[1,1,512,512]{3,2,1,0:T(8,128)(2,1)}, u32[]{:S(2)}) copy-start(bf16[1,1,512,512]{3,2,1,0:T(8,128)(2,1)} %param.12) | copy-start | bytes 1572868
  52.0 1.0 %copy-start.10 = (bf16[3,144,512]{2,1,0:T(8,128)(2,1)S(1)}, bf16[3,144,512]{2,1,0:T(8,128)(2,1)}, u32[]{:S(2)}) copy-start(bf16[3,144,512]{2,1,0:T(8,128)(2,1)} %get-tuple-element.26.rise_ref) | copy-start | bytes 1327108
  53.0 0.9 %copy-start.11 = (bf16[144,512]{1,0:T(8,128)(2,1)S(1)}, bf16[144,512]{1,0:T(8,128)(2,1)}, u32[]{:S(2)}) copy-start(bf16[144,512]{1,0:T(8,128)(2,1)} %get-tuple-element.27.mirror_ref) | copy-start | bytes 442372
  53.9 6.1 %copy-start.1 = (bf16[1072,512]{1,0:T(8,128)(2,1)S(1)}, bf16[1072,512]{1,0:T(8,128)(2,1)}, u32[]{:S(2)}) copy-start(bf16[1072,512]{1,0:T(8,128)(2,1)} %copy-done) | copy-start | bytes 3293188
  53.9 6.1 %copy-start.4 = (bf16[640,512]{1,0:T(8,128)(2,1)S(1)}, bf16[640,512]{1,0:T(8,128)(2,1)}, u32[]{:S(2)}) copy-start(bf16[640,512]{1,0:T(8,128)(2,1)} %get-tuple-element.30.own_ref) | copy-start | bytes 1966084
  53.9 6.1 %copy-start.7 = (s32[8,128]{1,0:T(8,128)S(1)}, s32[8,128]{1,0:T(8,128)}, u32[]{:S(2)}) copy-start(s32[8,128]{1,0:T(8,128)} %get-tuple-element.29.lists_ref) | copy-start | bytes 12292
  56.1 18.1 %copy-start.3 = (bf16[1,1,512,160]{2,3,1,0:T(8,128)(2,1)S(1)}, bf16[1,1,512,160]{2,3,1,0:T(8,128)(2,1)}, u32[]{:S(2)}) copy-start(bf16[1,1,512,160]{2,3,1,0:T(8,128)(2,1)} %param.15) | copy-start | bytes 491524
  56.1 18.1 %copy-start.5 = (bf16[1,1,160,160]{3,2,1,0:T(8,128)(2,1)S(1)}, bf16[1,1,160,160]{3,2,1,0:T(8,128)(2,1)}, u32[]{:S(2)}) copy-start(bf16[1,1,160,160]{3,2,1,0:T(8,128)(2,1)} %param.16) | copy-start | bytes 153604
  56.1 18.1 %copy-start.6 = (bf16[160,160]{1,0:T(8,128)(2,1)S(1)}, bf16[160,160]{1,0:T(8,128)(2,1)}, u32[]{:S(2)}) copy-start(bf16[160,160]{1,0:T(8,128)(2,1)} %get-tuple-element.32.level_ref) | copy-start | bytes 153604
